TPU v7x, 32 devices: a whole 2x2x4 slice. The times are simulated.
32 devices in a mesh: dp: 2 (over x), ctx: 4 (over z), fsdp: 4 (over y, core).
Axes of the slice: x: 2, y: 2, z: 4, core: 2. Of those that a mesh axis runs over, the one named last changes fastest.
Arguments:
- tokens: bfloat16 [2, 4, 3072, 2048], P('dp', 'fsdp', 'ctx'), may hold values from -6 to 6
- cotangent: bfloat16 [2, 4, 3072, 2048], P('dp', 'fsdp', 'ctx'), may hold values from -6 to 6
- pairing: int32 [2, 4, 4], P('dp', 'fsdp'), may hold values from 0 to 3, each once within a row
- attention_weights: float32 [2048, 8192], P(('dp', 'ctx', 'fsdp')), may hold values from -0.125 to 0.125
- attention_moment: float32 [2048, 8192], P(('dp', 'ctx', 'fsdp')), may hold values from -112 to 112
- attention_square: float32 [2048, 8192], P(('dp', 'ctx', 'fsdp')), may hold values from 1302.528 to 5160.96
- feed_weights: float32 [2048, 24576], P(('dp', 'ctx', 'fsdp')), may hold values from -0.125 to 0.125
- feed_moment: float32 [2048, 24576], P(('dp', 'ctx', 'fsdp')), may hold values from -80 to 80
- feed_square: float32 [2048, 24576], P(('dp', 'ctx', 'fsdp')), may hold values from 638.976 to 2580.48
- gains: float32 [4, 2048], replicated, may hold values from 0.5 to 1.5
- gain_moment: float32 [4, 2048], replicated, may hold values from -112 to 112
- gain_square: float32 [4, 2048], replicated, may hold values from 1302.528 to 5160.96
Outputs:
- output_states: bfloat16 [2, 4, 3072, 2048], P('dp', 'fsdp', 'ctx')
- input_gradient: bfloat16 [2, 4, 3072, 2048], P('dp', 'fsdp', 'ctx')
- attention_gradient: float32 [2048, 8192], P(('dp', 'ctx', 'fsdp'))
- attention_moment_new: float32 [2048, 8192], P(('dp', 'ctx', 'fsdp'))
- attention_square_new: float32 [2048, 8192], P(('dp', 'ctx', 'fsdp'))
- attention_weights_new: float32 [2048, 8192], P(('dp', 'ctx', 'fsdp'))
- feed_gradient: float32 [2048, 24576], P(('dp', 'ctx', 'fsdp'))
- feed_moment_new: float32 [2048, 24576], P(('dp', 'ctx', 'fsdp'))
- feed_square_new: float32 [2048, 24576], P(('dp', 'ctx', 'fsdp'))
- feed_weights_new: float32 [2048, 24576], P(('dp', 'ctx', 'fsdp'))
- gain_gradient: float32 [4, 2048], replicated
- gain_moment_new: float32 [4, 2048], replicated
- gain_square_new: float32 [4, 2048], replicated
- gains_new: float32 [4, 2048], replicated
Inputs may be any that keep to these rules, and one draw needn't show every extreme that they name: Each row of pairing is a permutation of 0 to 3.
All inputs are finite; a program needn't handle non-finite values.
Results may differ from a plain program's by a relative error of at most 0.018.
Values may be sent and summed in bfloat16 or wider, within the bound.
A program may use at most 896 MiB of HBM per device.

v0:
```python
import jax
import jax.numpy as jnp
from jax import lax
from jax.sharding import PartitionSpec as P

HEADS = 16
HEAD = 128
STEP = 10


epsilon_norm = 1e-06
rope_base = 500000.0
masked_value = -1e30
beta_first = 0.9
beta_second = 0.95
learn_rate = 0.05
gain_rate = 1.0
weight_decay = 0.1
epsilon_adam = 1e-08


def stored_positions(pair_row, length, block, ctx_count):
    index = jnp.arange(length, dtype=jnp.int32)
    owner = index // (2 * block)
    upper = index // block % 2
    table = jnp.sum(
        jnp.where(
            owner[:, None] == jnp.arange(ctx_count, dtype=jnp.int32)[None, :], pair_row[None, :], 0
        ),
        axis=1,
    )
    placed = jnp.where(upper == 0, table, 2 * ctx_count - 1 - table)
    return placed * block + index % block


def rotate(values, places, sign):
    rows = values.shape[0]
    half = HEAD // 2
    frequency = rope_base ** (-(jnp.arange(half, dtype=jnp.float32) * (2.0 / HEAD)))
    angle = places.astype(jnp.float32)[:, None] * frequency[None, :]
    cosine = jnp.cos(angle)[:, None, :]
    sine = sign * jnp.sin(angle)[:, None, :]
    shaped = values.reshape(rows, HEADS, HEAD)
    first = shaped[..., :half]
    second = shaped[..., half:]
    turned = jnp.concatenate(
        [first * cosine - second * sine, second * cosine + first * sine], axis=-1
    )
    return turned.reshape(rows, HEADS * HEAD)


def norm_forward(values, gain):
    scale = lax.rsqrt(jnp.mean(values * values, axis=-1, keepdims=True) + epsilon_norm)
    return (values * scale * gain, scale)


def norm_backward(values, scale, gain, upstream):
    weighted = upstream * gain
    inward = scale * (
        weighted - values * (scale * scale) * jnp.mean(weighted * values, axis=-1, keepdims=True)
    )
    return (inward, jnp.sum(upstream * values * scale, axis=0))


def transposed(left, right):
    return lax.dot_general(
        left, right, (((0,), (0,)), ((), ())), preferred_element_type=jnp.float32
    )


def against(left, right):
    return lax.dot_general(
        left, right, (((1,), (1,)), ((), ())), preferred_element_type=jnp.float32
    )


def key_blocks(keys_low, values_low, key_places):
    length = keys_low.shape[0]
    size = 512
    count = length // size
    return (
        keys_low.reshape(count, size, HEADS, HEAD),
        values_low.reshape(count, size, HEADS, HEAD),
        key_places.reshape(count, size),
    )


def block_scores(query_heads, key_piece, place_piece, query_places):
    raw = jnp.einsum(
        "qhd,khd->hqk", query_heads, key_piece, preferred_element_type=jnp.float32
    ) * HEAD ** (-0.5)
    allowed = place_piece[None, None, :] <= query_places[None, :, None]
    return (raw, allowed)


def attend_forward(queries_low, keys_low, values_low, query_places, key_places):
    rows = queries_low.shape[0]
    query_heads = queries_low.reshape(rows, HEADS, HEAD)
    pieces = key_blocks(keys_low, values_low, key_places)

    def measure(carry, piece):
        top, total = carry
        raw, allowed = block_scores(query_heads, piece[0], piece[2], query_places)
        masked = jnp.where(allowed, raw, masked_value)
        new_top = jnp.maximum(top, jnp.max(masked, axis=-1))
        total = total * jnp.exp(top - new_top) + jnp.sum(
            jnp.where(allowed, jnp.exp(masked - new_top[..., None]), 0.0), axis=-1
        )
        return ((new_top, total), None)

    start = (
        jnp.full((HEADS, rows), masked_value, jnp.float32),
        jnp.zeros((HEADS, rows), jnp.float32),
    )
    (top, total), unused = lax.scan(measure, start, pieces)
    log_total = top + jnp.log(total)

    def collect(carry, piece):
        raw, allowed = block_scores(query_heads, piece[0], piece[2], query_places)
        weights = jnp.where(allowed, jnp.exp(raw - log_total[..., None]), 0.0).astype(jnp.bfloat16)
        return (
            carry
            + jnp.einsum("hqk,khd->qhd", weights, piece[1], preferred_element_type=jnp.float32),
            None,
        )

    attended, unused = lax.scan(collect, jnp.zeros((rows, HEADS, HEAD), jnp.float32), pieces)
    return (attended.reshape(rows, HEADS * HEAD), log_total)


def attend_backward(
    queries_low, keys_low, values_low, query_places, key_places, log_total, outward_low, attended
):
    rows = queries_low.shape[0]
    length = keys_low.shape[0]
    scale = HEAD ** (-0.5)
    query_heads = queries_low.reshape(rows, HEADS, HEAD)
    outward_heads = outward_low.reshape(rows, HEADS, HEAD)
    delta = jnp.sum(
        outward_heads.astype(jnp.float32) * attended.reshape(rows, HEADS, HEAD), axis=-1
    ).T
    pieces = key_blocks(keys_low, values_low, key_places)

    def sweep(carry, piece):
        raw, allowed = block_scores(query_heads, piece[0], piece[2], query_places)
        exact = jnp.where(allowed, jnp.exp(raw - log_total[..., None]), 0.0)
        mass = jnp.einsum(
            "qhd,khd->hqk", outward_heads, piece[1], preferred_element_type=jnp.float32
        )
        slope = (exact * (mass - delta[..., None])).astype(jnp.bfloat16)
        carry = (
            carry
            + jnp.einsum("hqk,khd->qhd", slope, piece[0], preferred_element_type=jnp.float32)
            * scale
        )
        key_term = (
            jnp.einsum("hqk,qhd->khd", slope, query_heads, preferred_element_type=jnp.float32)
            * scale
        )
        value_term = jnp.einsum(
            "hqk,qhd->khd",
            exact.astype(jnp.bfloat16),
            outward_heads,
            preferred_element_type=jnp.float32,
        )
        return (carry, (key_term, value_term))

    grad_query, terms = lax.scan(sweep, jnp.zeros((rows, HEADS, HEAD), jnp.float32), pieces)
    return (
        grad_query.reshape(rows, HEADS * HEAD),
        terms[0].reshape(length, HEADS * HEAD),
        terms[1].reshape(length, HEADS * HEAD),
    )


def adamw(weight, moment, square, gradient, rate, decay):
    moment_new = beta_first * moment + (1.0 - beta_first) * gradient
    square_new = beta_second * square + (1.0 - beta_second) * gradient * gradient
    fix_first = 1.0 - beta_first**STEP
    fix_second = 1.0 - beta_second**STEP
    update = moment_new / fix_first / (jnp.sqrt(square_new / fix_second) + epsilon_adam)
    return (moment_new, square_new, weight - rate * (update + decay * weight))


def body(
    tokens,
    cotangent,
    pairing,
    attention_weights,
    attention_moment,
    attention_square,
    feed_weights,
    feed_moment,
    feed_square,
    gains,
    gain_moment,
    gain_square,
):
    inputs = tokens[0, 0]
    rows, width = inputs.shape
    ctx_count = lax.axis_size("ctx")
    block = rows // 2
    length = rows * ctx_count
    hidden = feed_weights.shape[1] // 3
    order = stored_positions(pairing[0, 0], length, block, ctx_count)
    local_places = lax.dynamic_slice_in_dim(order, lax.axis_index("ctx") * rows, rows)
    attention_low = lax.all_gather(
        attention_weights.astype(jnp.bfloat16), ("dp", "ctx", "fsdp"), axis=0, tiled=True
    )
    projected = jnp.dot(inputs, attention_low[:, : 3 * width], preferred_element_type=jnp.float32)
    query_pre = projected[:, :width]
    key_pre = projected[:, width : 2 * width]
    values_low = projected[:, 2 * width :].astype(jnp.bfloat16)
    query_normed, query_scale = norm_forward(query_pre, gains[0])
    key_normed, key_scale = norm_forward(key_pre, gains[1])
    queries_low = rotate(query_normed, local_places, 1.0).astype(jnp.bfloat16)
    keys_low = rotate(key_normed, local_places, 1.0).astype(jnp.bfloat16)
    key_all, value_all = (
        lax.all_gather(keys_low, "ctx", axis=0, tiled=True),
        lax.all_gather(values_low, "ctx", axis=0, tiled=True),
    )
    attended, log_total = attend_forward(queries_low, key_all, value_all, local_places, order)
    attended_low = attended.astype(jnp.bfloat16)
    proj = jnp.dot(attended_low, attention_low[:, 3 * width :], preferred_element_type=jnp.float32)
    branch, proj_scale = norm_forward(proj, gains[2])
    state = inputs.astype(jnp.float32) + branch
    state_low = state.astype(jnp.bfloat16)
    feed_low = lax.all_gather(
        feed_weights.astype(jnp.bfloat16), ("dp", "ctx", "fsdp"), axis=0, tiled=True
    )
    gate_up = jnp.dot(state_low, feed_low[:, : 2 * hidden], preferred_element_type=jnp.float32)
    gate = gate_up[:, :hidden]
    up_part = gate_up[:, hidden:]
    sigma = jax.nn.sigmoid(gate)
    inner_low = (gate * sigma * up_part).astype(jnp.bfloat16)
    down = against(inner_low, feed_low[:, 2 * hidden :])
    mixed, down_scale = norm_forward(down, gains[3])
    output_states = (state + mixed).astype(jnp.bfloat16)
    upstream = cotangent[0, 0].astype(jnp.float32)
    grad_down, gain_down = norm_backward(down, down_scale, gains[3], upstream)
    grad_down_low = grad_down.astype(jnp.bfloat16)
    grad_inner = jnp.dot(
        grad_down_low, feed_low[:, 2 * hidden :], preferred_element_type=jnp.float32
    )
    grad_gate = grad_inner * up_part * sigma * (1.0 + gate * (1.0 - sigma))
    grad_up = grad_inner * gate * sigma
    grad_gate_up = jnp.concatenate([grad_gate, grad_up], axis=1).astype(jnp.bfloat16)
    grad_state = upstream + against(grad_gate_up, feed_low[:, : 2 * hidden])
    grad_proj, gain_branch = norm_backward(proj, proj_scale, gains[2], grad_state)
    grad_proj_low = grad_proj.astype(jnp.bfloat16)
    feed_gradient = lax.psum_scatter(
        jnp.concatenate(
            [transposed(state_low, grad_gate_up), transposed(grad_down_low, inner_low)], axis=1
        ),
        ("dp", "ctx", "fsdp"),
        scatter_dimension=0,
        tiled=True,
    )
    grad_attended = against(grad_proj_low, attention_low[:, 3 * width :]).astype(jnp.bfloat16)
    grad_query, key_terms, value_terms = attend_backward(
        queries_low, key_all, value_all, local_places, order, log_total, grad_attended, attended
    )
    grad_key, grad_value = (
        lax.psum_scatter(
            key_terms.astype(jnp.bfloat16), "ctx", scatter_dimension=0, tiled=True
        ).astype(jnp.float32),
        lax.psum_scatter(
            value_terms.astype(jnp.bfloat16), "ctx", scatter_dimension=0, tiled=True
        ).astype(jnp.float32),
    )
    grad_query_pre, gain_query = norm_backward(
        query_pre, query_scale, gains[0], rotate(grad_query, local_places, -1.0)
    )
    grad_key_pre, gain_key = norm_backward(
        key_pre, key_scale, gains[1], rotate(grad_key, local_places, -1.0)
    )
    grad_projected = jnp.concatenate([grad_query_pre, grad_key_pre, grad_value], axis=1).astype(
        jnp.bfloat16
    )
    input_gradient = (grad_state + against(grad_projected, attention_low[:, : 3 * width])).astype(
        jnp.bfloat16
    )
    attention_gradient = lax.psum_scatter(
        jnp.concatenate(
            [transposed(inputs, grad_projected), transposed(attended_low, grad_proj_low)], axis=1
        ),
        ("dp", "ctx", "fsdp"),
        scatter_dimension=0,
        tiled=True,
    )
    gain_gradient = lax.psum(
        jnp.stack([gain_query, gain_key, gain_branch, gain_down]), ("dp", "ctx", "fsdp")
    )
    attention_moment_new, attention_square_new, attention_weights_new = adamw(
        attention_weights,
        attention_moment,
        attention_square,
        attention_gradient,
        learn_rate,
        weight_decay,
    )
    feed_moment_new, feed_square_new, feed_weights_new = adamw(
        feed_weights, feed_moment, feed_square, feed_gradient, learn_rate, weight_decay
    )
    gain_moment_new, gain_square_new, gains_new = adamw(
        gains, gain_moment, gain_square, gain_gradient, gain_rate, 0.0
    )
    return (
        output_states[None, None],
        input_gradient[None, None],
        attention_gradient,
        attention_moment_new,
        attention_square_new,
        attention_weights_new,
        feed_gradient,
        feed_moment_new,
        feed_square_new,
        feed_weights_new,
        gain_gradient,
        gain_moment_new,
        gain_square_new,
        gains_new,
    )


def solution(mesh):
    placed = (
        P("dp", "fsdp", "ctx", None),
        P("dp", "fsdp", "ctx", None),
        P("dp", "fsdp", None),
        P(("dp", "ctx", "fsdp"), None),
        P(("dp", "ctx", "fsdp"), None),
        P(("dp", "ctx", "fsdp"), None),
        P(("dp", "ctx", "fsdp"), None),
        P(("dp", "ctx", "fsdp"), None),
        P(("dp", "ctx", "fsdp"), None),
        P(),
        P(),
        P(),
    )
    return jax.shard_map(
        body,
        mesh=mesh,
        in_specs=placed,
        out_specs=(
            P("dp", "fsdp", "ctx", None),
            P("dp", "fsdp", "ctx", None),
            P(("dp", "ctx", "fsdp"), None),
            P(("dp", "ctx", "fsdp"), None),
            P(("dp", "ctx", "fsdp"), None),
            P(("dp", "ctx", "fsdp"), None),
            P(("dp", "ctx", "fsdp"), None),
            P(("dp", "ctx", "fsdp"), None),
            P(("dp", "ctx", "fsdp"), None),
            P(("dp", "ctx", "fsdp"), None),
            P(),
            P(),
            P(),
            P(),
        ),
        check_vma=False,
    )
```

profile of v0, /device:TPU:0, one launch (start us, length us, event | category | flops | bytes accessed | tf_op | source)
XLA Modules:
  0.0 4751.9 jit_solution(16845422246860404858)
XLA Ops:
  10.0 199.0 %all-gather.5.cloned.1.call-done = bf16[2048,8192]{1,0:T(8,128)(2,1)} async-done(((bf16[64,8192]{1,0:T(8,128)(2,1)}), bf16[2048,8192]{1,0:T(8,128)(2,1)}) %all-gather.5.cloned.1.call-update) | async-done | bytes 33554448 | tf_op jit(solution)/shard_map/all_gather | solution.py:207
  209.0 23.9 fusion.52
  295.7 162.3 %all-gather.7.cloned.1.call-done = bf16[3072,2048]{1,0:T(8,128)(2,1)} async-done(((bf16[768,2048]{1,0:T(8,128)(2,1)}), bf16[3072,2048]{1,0:T(8,128)(2,1)}) %all-gather.7.cloned.1.call-update) | async-done | bytes 12582928 | tf_op jit(solution)/shard_map/all_gather | solution.py:220
  469.9 206.7 %all-gather.9.cloned.1.call-done = bf16[3072,2048]{1,0:T(8,128)(2,1)} async-done(((bf16[768,2048]{1,0:T(8,128)(2,1)}), bf16[3072,2048]{1,0:T(8,128)(2,1)}) %all-gather.9.cloned.1.call-update) | async-done | bytes 12582928 | tf_op jit(solution)/shard_map/all_gather | solution.py:219
  690.8 163.0 %while.39 = (s32[]{:T(128)}, f32[16,768]{1,0:T(8,128)}, f32[16,768]{1,0:T(8,128)}, s32[6,512]{1,0:T(8,128)}, s32[768]{0:T(1024)S(1)}, /*index=5*/bf16[6,512,16,1...) while((s32[]{:T(128)}, f32[16,768]{1,0:T(8,128)}, ...), condition=%wide.region_6.7_spmd.clone, body=%wide.region_3.6_spmd.clone.sunk | while | flops 1661399040 | bytes 57992392 | solution.py:115
  691.8 13.1 fusion.155
  718.8 12.8 fusion.155
  745.7 12.7 fusion.155
  759.2 13.3 select_reduce_fusion.3
  774.3 12.9 fusion.155
  801.2 12.7 fusion.155
  828.0 12.9 fusion.155
  855.2 123.9 %while.40 = (s32[]{:T(128)}, f32[768,16,128]{0,2,1:T(8,128)}, bf16[6,512,16,128]{3,2,1,0:T(8,128)(2,1)}, s32[6,512]{1,0:T(8,128)}, s32[768]{0:T(1024)S(1)}, /*in...) while((s32[]{:T(128)}, f32[768,16,128]{0,2,1:T(8,128)}, ...), condition=%wide.region_8.9_spmd.clone, body=%wide.region_7.8_spmd.clone.sunk | while | flops 3249930240 | bytes 29156480 | solution.py:127
  925.1 13.3 bitcast_add_fusion.4
  998.3 196.8 %all-gather.11.cloned.1.call-done = bf16[2048,24576]{1,0:T(8,128)(2,1)} async-done(((bf16[64,24576]{1,0:T(8,128)(2,1)}), bf16[2048,24576]{1,0:T(8,128)(2,1)}) %all-gather.11.cloned.1.call-update) | async-done | bytes 100663312 | tf_op jit(solution)/shard_map/all_gather | solution.py:228
  1195.2 59.3 %fusion.44 = f32[768,16384]{1,0:T(8,128)} fusion(bf16[768,2048]{1,0:T(8,128)(2,1)S(1)} %fusion.67, bf16[2048,24576]{1,0:T(8,128)(2,1)} %all-gather.11.cloned.1.call-done), kind=kOutput, calls=%fused_computation.56 | convolution fusion | flops 51539607552 | bytes 120586240 | tf_op jit(solution)/shard_map/dot_general | solution.py:231
  1254.4 21.2 multiply_convert_fusion.2
  1275.7 35.7 multiply_reduce_fusion.7
  1315.9 47.2 multiply_convert_fusion.1
  1363.2 68.7 %multiply_reduce_fusion = (f32[2048]{0:T(1024)}, f32[768]{0:T(1024)S(1)}, f32[768,2048]{1,0:T(8,128)}) fusion(f32[768,2048]{1,0:T(8,128)} %copy-done.5, f32[768]{0:T(1024)S(1)} %copy-done.44, f32[2048]{0:T(1024)S(1)} %bitcast.230, bf16[2048,24576]{1,0:T(8,128)(2,1)} %all-gather.11.cloned.1.call-done, bf16[768,8192]{1,0:T(8,128)(2,1)} %get-tuple-element.539, ...), kind=kOutput, calls=%fused_computation.95 | convolution fusion | flops 51602522112 | bytes 108025856 | tf_op jit(solution)/shard_map/dot_general | solution.py:72
  1461.4 378.7 %while.41 = (s32[]{:T(128)}, f32[768,16,128]{0,2,1:T(8,128)}, bf16[6,512,16,128]{3,1,2,0:T(8,128)(2,1)}, bf16[6,512,16,128]{3,1,2,0:T(8,128)(2,1)}, bf16[6,512,1...) while((s32[]{:T(128)}, f32[768,16,128]{0,2,1:T(8,128)}, ...), condition=%wide.region_15.16_spmd.clone, body=%wide.region_14.15_spmd.clone.sunk | while | flops 8122138624 | bytes 221537504 | solution.py:168
  1461.8 13.5 fusion.170
  1478.3 17.4 fusion.171
  1510.7 12.7 bitcast_dynamic-update-slice_fusion.5
  1523.4 13.5 fusion.170
  1539.9 17.4 fusion.171
  1586.7 13.5 fusion.170
  1603.1 17.4 fusion.171
  1650.0 13.5 fusion.170
  1666.5 17.4 fusion.171
  1713.3 13.5 fusion.170
  1729.8 17.4 fusion.171
  1764.0 12.7 bitcast_dynamic-update-slice_fusion.5
  1776.7 13.5 fusion.170
  1793.1 17.4 fusion.171
  1891.5 177.2 %reduce-scatter.7.cloned.1.call-done = bf16[768,2048]{1,0:T(8,128)(2,1)} async-done(((bf16[3072,2048]{1,0:T(8,128)(2,1)}), bf16[768,2048]{1,0:T(8,128)(2,1)}) %reduce-scatter.7.cloned.1.call-update) | async-done | bytes 3145744 | tf_op jit(solution)/shard_map/reduce_scatter | solution.py:264
  2123.8 160.1 %reduce-scatter.9.cloned.1.call-done = bf16[768,2048]{1,0:T(8,128)(2,1)} async-done(((bf16[3072,2048]{1,0:T(8,128)(2,1)}), bf16[768,2048]{1,0:T(8,128)(2,1)}) %reduce-scatter.9.cloned.1.call-update) | async-done | bytes 3145744 | tf_op jit(solution)/shard_map/reduce_scatter | solution.py:267
  2283.8 31.5 convolution_bitcast_fusion
  2315.3 44.5 pad_maximum_fusion.1
  2359.8 61.2 %copy.178 = f32[2048,8192]{1,0:T(8,128)} copy(f32[2048,8192]{0,1:T(8,128)} %pad_maximum_fusion.1) | data formatting | bytes 134217728
  2422.9 39.5 fusion.105
  2462.4 63.9 %fusion.54 = f32[2048,16384]{1,0:T(8,128)} fusion(bf16[768,2048]{1,0:T(8,128)(2,1)} %copy-done.16, bf16[768,8192]{1,0:T(8,128)(2,1)} %get-tuple-element.539, bf16[768,8192]{1,0:T(8,128)(2,1)} %get-tuple-element.538), kind=kOutput, calls=%fused_computation.72 | convolution fusion | flops 51589939200 | bytes 162529280 | tf_op jit(solution)/shard_map/dot_general | solution.py:66
  2526.4 133.3 %pad_maximum_fusion = f32[2048,24576]{1,0:T(8,128)} fusion(f32[2048,8192]{1,0:T(8,128)} %fusion.105, f32[2048,16384]{1,0:T(8,128)} %fusion.54), kind=kLoop, calls=%fused_computation.52 | loop fusion | flops 50331648 | bytes 402653184 | tf_op jit(solution)/shard_map/concatenate | solution.py:252
  2660.4 45.1 psum.7
  2706.2 28.9 fusion.74
  2735.2 390.9 %reduce-scatter.13.cloned.1.call-done = f32[64,8192]{1,0:T(8,128)} async-done(((f32[2048,8192]{1,0:T(8,128)}), f32[64,8192]{1,0:T(8,128)}) %reduce-scatter.13.cloned.1.call-update) | async-done | bytes 2097168
  3132.6 1595.3 %reduce-scatter.11.cloned.1.call-done = f32[64,24576]{1,0:T(8,128)} async-done(((f32[2048,24576]{1,0:T(8,128)}), f32[64,24576]{1,0:T(8,128)}) %reduce-scatter.11.cloned.1.call-update) | async-done | bytes 6291472 | tf_op jit(solution)/shard_map/reduce_scatter | solution.py:251
  4728.0 16.9 multiply_subtract_fusion
  (357 shorter events, 612.0 us)
Async XLA Ops:
  7.2 201.8 %all-gather.5.cloned.1.call-start = ((), (), s32[]{:S(2)}) async-start(), calls=%async_computation.4 | async-start | bytes 34603008 | tf_op jit(solution)/shard_map/all_gather | solution.py:207
  9.9 448.1 %all-gather.7.cloned.1.call-start = ((), (), s32[]{:S(2)}) async-start(), calls=%async_computation.5 | async-start | bytes 15728640 | tf_op jit(solution)/shard_map/all_gather | solution.py:220
  241.5 435.1 %all-gather.9.cloned.1.call-start = ((), (), s32[]{:S(2)}) async-start(), calls=%async_computation.6 | async-start | bytes 15728640 | tf_op jit(solution)/shard_map/all_gather | solution.py:219
  243.3 31.2 copy-start.20
  284.4 910.7 %all-gather.11.cloned.1.call-start = ((), (), s32[]{:S(2)}) async-start(), calls=%async_computation.7 | async-start | bytes 103809024 | tf_op jit(solution)/shard_map/all_gather | solution.py:228
  289.4 1779.3 %reduce-scatter.7.cloned.1.call-start = ((), (), s32[]{:S(2)}) async-start(), calls=%async_computation.8 | async-start | bytes 15728640 | tf_op jit(solution)/shard_map/reduce_scatter | solution.py:264
  732.5 11.5 copy-start.22
  759.2 13.4 copy-start.12
  759.2 13.4 copy-start.22
  814.8 11.5 copy-start.12
  814.8 11.5 copy-start.22
  979.1 15.4 copy-start.1
  979.1 15.4 copy-start.24
  983.5 13.8 copy-start.7
  983.5 13.8 copy-start.34
  998.3 256.1 %copy-start.16 = (bf16[768,2048]{1,0:T(8,128)(2,1)}, bf16[768,2048]{1,0:T(8,128)(2,1)S(1)}, u32[]{:S(2)}) copy-start(bf16[768,2048]{1,0:T(8,128)(2,1)S(1)} %fusion.67) | copy-start | bytes 9437188
  1275.6 35.7 copy-start.14
  1275.7 35.7 copy-start.36
  1311.3 51.8 %copy-start.56 = (f32[768]{0:T(1024)}, f32[768]{0:T(1024)S(1)}, u32[]{:S(2)}) copy-start(f32[768]{0:T(1024)S(1)} %get-tuple-element.571) | copy-start | bytes 9220
  1311.3 120.6 %copy-start.45 = (f32[768]{0:T(1024)}, f32[768]{0:T(1024)S(1)}, u32[]{:S(2)}) copy-start(f32[768]{0:T(1024)S(1)} %get-tuple-element.572) | copy-start | bytes 9220
  1315.9 47.2 copy-start.58
  1315.9 47.2 copy-start.35
  1315.9 47.2 copy-start.44
  1363.1 68.8 %copy-start.6 = (f32[768,2048]{1,0:T(8,128)S(1)}, f32[768,2048]{1,0:T(8,128)}, u32[]{:S(2)}) copy-start(f32[768,2048]{1,0:T(8,128)} %copy-done.5) | copy-start | bytes 18874372
  1363.2 68.8 %copy-start.8 = (bf16[1,1,768,2048]{3,2,1,0:T(8,128)(2,1)S(1)}, bf16[1,1,768,2048]{3,2,1,0:T(8,128)(2,1)}, u32[]{:S(2)}) copy-start(bf16[1,1,768,2048]{3,2,1,0:T(8,128)(2,1)} %param.18) | copy-start | bytes 9437188
  1363.2 68.8 %copy-start.52 = (f32[768]{0:T(1024)S(1)}, f32[768]{0:T(1024)}, u32[]{:S(2)}) copy-start(f32[768]{0:T(1024)} %get-tuple-element.569) | copy-start | bytes 9220
  1461.8 16.5 copy-start.13
  1523.4 16.5 copy-start.13
  1557.3 12.1 copy-start
  1586.7 16.5 copy-start.13
  1620.6 12.1 copy-start
  1650.0 16.5 copy-start.13
  1683.9 12.1 copy-start
  1713.3 16.5 copy-start.13
  1747.2 12.1 copy-start
  1776.7 16.5 copy-start.13
  1810.6 12.1 copy-start
  1858.5 425.3 %reduce-scatter.9.cloned.1.call-start = ((), (), s32[]{:S(2)}) async-start(), calls=%async_computation.9 | async-start | bytes 15728640 | tf_op jit(solution)/shard_map/reduce_scatter | solution.py:267
  1877.6 1248.5 %reduce-scatter.13.cloned.1.call-start = ((), (), s32[]{:S(2)}) async-start(), calls=%async_computation.11 | async-start | bytes 69206016
  1891.5 182.6 %copy-start.21 = (f32[768,64]{0,1:T(8,128)S(1)}, f32[768,64]{0,1:T(8,128)}, u32[]{:S(2)}) copy-start(f32[768,64]{0,1:T(8,128)} %copy-done.20) | copy-start | bytes 589828
  1891.5 182.6 %copy-start.26 = (f32[768,64]{0,1:T(8,128)S(1)}, f32[768,64]{0,1:T(8,128)}, u32[]{:S(2)}) copy-start(f32[768,64]{0,1:T(8,128)} %get-tuple-element.562) | copy-start | bytes 589828
  2097.2 17.6 slice-start
  2421.1 2306.9 %reduce-scatter.11.cloned.1.call-start = ((), (), s32[]{:S(2)}) async-start(), calls=%async_computation.10 | async-start | bytes 207618048 | tf_op jit(solution)/shard_map/reduce_scatter | solution.py:251
  2659.7 45.8 copy-start.32
  2659.7 45.8 copy-start.49
  2659.7 45.8 copy-start.50
  2705.5 29.6 copy-start.33
  2706.2 419.9 %copy-start.9 = (f32[64,8192]{1,0:T(8,128)S(1)}, f32[64,8192]{1,0:T(8,128)}, u32[]{:S(2)}) copy-start(f32[64,8192]{1,0:T(8,128)} %param.21) | copy-start | bytes 6291460
  (48 other events, 280.3 us)
Sparse Core Ops, SparseCore 0:
  11.5 197.4 all-gather.4
  241.6 216.3 all-gather.6
  460.1 216.3 all-gather.8
  679.9 515.2 all-gather.10
  1858.6 210.0 reduce-scatter.6
  2070.9 212.8 reduce-scatter.8
  2421.2 704.8 reduce-scatter.12
  3133.1 1594.8 reduce-scatter.10
where the time goes:
time: 4760 us; the launch traced here: 4750 us
  waiting for transfers between devices  3090 us (65%)
  matrix products  940 us (20%)
  other arithmetic  400 us (8%)
  local copies, waits for them, and re-layouts  261 us (5%)
    reduce_scatter x1, waiting for transfers between devices, body(): lax.psum_scatter(jnp.concatenate([transposed(state_low, grad_gate_up), tr...  1600 us
    unnamed x9, waiting for transfers between devices  391 us
    all_gather x1, waiting for transfers between devices, body(): lax.all_gather(keys_low, 'ctx', axis=0, tiled=True)  207 us
    all_gather x1, waiting for transfers between devices, body(): lax.all_gather(attention_weights.astype(jnp.bfloat16), ('dp', 'ctx', 'fsd...  199 us
    all_gather x1, waiting for transfers between devices, body(): lax.all_gather(feed_weights.astype(jnp.bfloat16), ('dp', 'ctx', 'fsdp'),...  197 us
    reduce_scatter x1, waiting for transfers between devices, body(): lax.psum_scatter(key_terms.astype(jnp.bfloat16), 'ctx', scatter_dimension...  177 us
    all_gather x1, waiting for transfers between devices, body(): lax.all_gather(values_low, 'ctx', axis=0, tiled=True)  162 us
    reduce_scatter x1, waiting for transfers between devices, body(): lax.psum_scatter(value_terms.astype(jnp.bfloat16), 'ctx', scatter_dimensi...  160 us
  transfers between devices with their start and end apart: 8, of which 8 were waited for; matrix products, arithmetic and copies ran while one was open for 16% of the time, Pallas kernels for 0%

commit v1 on v0

v1 whole, which is shorter than its diff:
```python
import functools
import math

import jax
import jax.numpy as jnp
from jax import lax
from jax.experimental import pallas as pl
from jax.experimental.pallas import tpu as pltpu
from jax.sharding import PartitionSpec as P

HEADS = 16
HEAD = 128
STEP = 10

epsilon_norm = 1e-06
rope_base = 500000.0
masked_value = -1e30
beta_first = 0.9
beta_second = 0.95
learn_rate = 0.05
gain_rate = 1.0
weight_decay = 0.1
epsilon_adam = 1e-08

score_scale = HEAD ** (-0.5)
exponent_scale = score_scale * math.log2(math.e)

EVERY = ("dp", "ctx", "fsdp")


def turn_tables(places):
    half = HEAD // 2
    frequency = rope_base ** (-(jnp.arange(half, dtype=jnp.float32) * (2.0 / HEAD)))
    angle = places.astype(jnp.float32)[:, None] * frequency[None, :]
    cosine = jnp.cos(angle)
    sine = jnp.sin(angle)
    return (
        jnp.concatenate([cosine, cosine], axis=-1),
        jnp.concatenate([-sine, sine], axis=-1),
    )


def norm_backward(values, scale, gain, upstream):
    weighted = upstream * gain
    inward = scale * (
        weighted - values * (scale * scale) * jnp.mean(weighted * values, axis=-1, keepdims=True)
    )
    return inward, jnp.sum(upstream * values * scale, axis=0)


def product(left, right):
    return jnp.dot(left, right, preferred_element_type=jnp.float32)


def transposed(left, right):
    return lax.dot_general(
        left, right, (((0,), (0,)), ((), ())), preferred_element_type=jnp.float32
    )


def against(left, right):
    return lax.dot_general(
        left, right, (((1,), (1,)), ((), ())), preferred_element_type=jnp.float32
    )


low_type = jnp.bfloat16


def tile_of(length):
    for tile in (512, 384, 256, 128):
        if length % tile == 0:
            return tile
    return length


brief = pl.CostEstimate(flops=1024, bytes_accessed=1024, transcendentals=0)


def params(steps, mib):
    return pltpu.CompilerParams(
        dimension_semantics=("arbitrary",) * steps, vmem_limit_bytes=mib * 2**20
    )


def prepare_kernel(order_ref, q_ref, k_ref, v_ref, scale_ref, gain_ref, cos_ref, sin_ref, qo, ko, vo):
    cosine, sine = cos_ref[...], sin_ref[...]
    for which, (source, target) in enumerate(((q_ref, qo), (k_ref, ko))):
        scale = scale_ref[:, which : which + 1]
        for start in range(0, source.shape[1], HEAD):
            at = slice(start, start + HEAD)
            part = source[:, at] * scale * gain_ref[which : which + 1, at]
            turned = part * cosine + pltpu.roll(part, HEAD // 2, 1) * sine
            target[:, at] = turned.astype(low_type)
    vo[...] = v_ref[...].astype(low_type)


def prepare(projected, scales, gains, cosine, sine, order, stream):
    length, width = projected.shape[0] // 2, projected.shape[1] // 3
    count = order.shape[0]
    block = length // count
    out = pl.BlockSpec((block, width), lambda b, o: (o[b], 0))
    turn = pl.BlockSpec((block, HEAD), lambda b, o: (o[b], 0))
    return pl.pallas_call(
        prepare_kernel,
        out_shape=(jax.ShapeDtypeStruct((length, width), low_type),) * 3,
        grid_spec=pltpu.PrefetchScalarGridSpec(
            num_scalar_prefetch=1,
            grid=(count,),
            in_specs=[
                pl.BlockSpec((block, width), lambda b, o: (2 * b + stream, 0)),
                pl.BlockSpec((block, width), lambda b, o: (2 * b + stream, 1)),
                pl.BlockSpec((block, width), lambda b, o: (2 * b + stream, 2)),
                pl.BlockSpec((block, 2), lambda b, o: (2 * b + stream, 0)),
                pl.BlockSpec((2, width), lambda b, o: (0, 0)),
                turn,
                turn,
            ],
            out_specs=(out, out, out),
        ),
        compiler_params=params(1, 32),
        cost_estimate=brief,
        name="prepare",
    )(order, projected, projected, projected, scales, gains, cosine, sine)


def restore_kernel(
    order_ref,
    dq_ref,
    dk_ref,
    dv_ref,
    q_ref,
    k_ref,
    scale_ref,
    gain_ref,
    cos_ref,
    sin_ref,
    out_ref,
    value_ref,
    dot_ref,
    sum_ref,
):
    cosine, sine = cos_ref[...] * score_scale, sin_ref[...] * score_scale
    width = q_ref.shape[1]

    @pl.when(pl.program_id(0) == 0)
    def _():
        sum_ref[...] = jnp.zeros_like(sum_ref)

    for which, (source, pre) in enumerate(((dq_ref, q_ref), (dk_ref, k_ref))):
        scale = scale_ref[:, which : which + 1]
        dots = 0.0
        for start in range(0, width, HEAD):
            at = slice(start, start + HEAD)
            part = source[:, at]
            turned = part * cosine - pltpu.roll(part, HEAD // 2, 1) * sine
            weighted = turned * gain_ref[which : which + 1, at]
            unit = pre[:, at] * scale
            out_ref[:, which * width + start : which * width + start + HEAD] = weighted
            dots = dots + jnp.sum(weighted * unit, axis=1, keepdims=True)
            sum_ref[which : which + 1, at] += jnp.sum(turned * unit, axis=0, keepdims=True)
        dot_ref[:, which : which + 1] = dots
    value_ref[...] = dv_ref[...].astype(low_type)


def restore(grads, projected, scales, gains, cosine, sine, order, stream):
    length, width = grads[0].shape
    count = order.shape[0]
    block = length // count
    first = stream * count
    later = pl.BlockSpec((block, width), lambda b, o: (first + o[b], 0))
    turn = pl.BlockSpec((block, HEAD), lambda b, o: (o[b], 0))
    both = pl.BlockSpec((block, 2), lambda b, o: (b, 0))
    scale = pl.BlockSpec((block, 2), lambda b, o: (2 * b + stream, 0))
    small = pl.BlockSpec((2, width), lambda b, o: (0, 0))
    return pl.pallas_call(
        restore_kernel,
        out_shape=(
            jax.ShapeDtypeStruct((length, 2 * width), jnp.float32),
            jax.ShapeDtypeStruct((length, width), low_type),
            jax.ShapeDtypeStruct((length, 2), jnp.float32),
            jax.ShapeDtypeStruct((2, width), jnp.float32),
        ),
        grid_spec=pltpu.PrefetchScalarGridSpec(
            num_scalar_prefetch=1,
            grid=(count,),
            in_specs=[
                pl.BlockSpec((block, width), lambda b, o: (o[b], 0)),
                later,
                later,
                pl.BlockSpec((block, width), lambda b, o: (2 * b + stream, 0)),
                pl.BlockSpec((block, width), lambda b, o: (2 * b + stream, 1)),
                scale,
                small,
                turn,
                turn,
            ],
            out_specs=(
                pl.BlockSpec((block, 2 * width), lambda b, o: (b, 0)),
                pl.BlockSpec((block, width), lambda b, o: (b, 0)),
                both,
                small,
            ),
        ),
        compiler_params=params(1, 40),
        cost_estimate=brief,
        name="restore",
    )(order, *grads, projected, projected, scales, gains, cosine, sine)


def causal(tile):
    key = lax.broadcasted_iota(jnp.int32, (tile, tile), 0)
    query = lax.broadcasted_iota(jnp.int32, (tile, tile), 1)
    return key <= query


def forward_kernel(tile, parts, spots_ref, q_ref, *refs):
    k_refs, v_refs = refs[:parts], refs[parts : 2 * parts]
    o_ref, log_ref, ks, vt, held_rows = refs[2 * parts :]
    rows = k_refs[0].shape[0]
    step = pl.program_id(1)

    @pl.when(step == 0)
    def _():
        for part in range(parts):
            ks[part * rows : (part + 1) * rows, :] = k_refs[part][...]
            for start in range(0, rows, tile):
                at = slice(part * rows + start, part * rows + start + tile)
                value = v_refs[part][start : start + tile, :]
                vt[:, at] = value.astype(jnp.float32).T.astype(low_type)

    query = q_ref[...]

    def visit(j, carry, masked):
        top, mass, held = carry
        at = pl.ds(pl.multiple_of(j * tile, tile), tile)
        scores = against(ks[at, :], query)
        if masked:
            scores = jnp.where(causal(tile), scores, masked_value)
        new_top = jnp.maximum(top, jnp.max(scores, axis=0, keepdims=True))
        weights = jnp.exp2((scores - new_top) * exponent_scale)
        fade = jnp.exp2((top - new_top) * exponent_scale)
        mass = mass * fade + jnp.sum(weights, axis=0, keepdims=True)
        held = held * fade + product(vt[:, at], weights.astype(low_type))
        return new_top, mass, held

    start = (
        jnp.full((1, tile), masked_value, jnp.float32),
        jnp.zeros((1, tile), jnp.float32),
        jnp.zeros((HEAD, tile), jnp.float32),
    )
    last = step + (parts - 1) * (rows // tile)
    carry = visit(last, start, True)
    top, mass, held = lax.fori_loop(0, last, lambda j, c: visit(j, c, False), carry)
    here = pl.ds(pl.multiple_of(step * tile, tile), tile)
    held_rows[here, :] = (held / mass).T.astype(low_type)
    log_ref[0] = top * exponent_scale + jnp.log2(mass)

    @pl.when(step == rows // tile - 1)
    def _():
        count = spots_ref.shape[0]
        block = rows // count
        for k in range(count):
            there = pl.ds(pl.multiple_of(spots_ref[k] * block, block), block)
            o_ref[k * block : (k + 1) * block, :] = held_rows[there, :]


def attend_forward(queries, keys, values, spots):
    length, width = queries.shape
    heads, parts = width // HEAD, len(keys)
    tile = tile_of(length)
    whole = pl.BlockSpec((length, HEAD), lambda h, i, o: (0, h))
    piece = pl.BlockSpec((tile, HEAD), lambda h, i, o: (i, h))
    return pl.pallas_call(
        functools.partial(forward_kernel, tile, parts),
        out_shape=(
            jax.ShapeDtypeStruct((length, width), low_type),
            jax.ShapeDtypeStruct((heads, 1, length), jnp.float32),
        ),
        grid_spec=pltpu.PrefetchScalarGridSpec(
            num_scalar_prefetch=1,
            grid=(heads, length // tile),
            in_specs=[piece] + [whole] * (2 * parts),
            out_specs=(whole, pl.BlockSpec((1, 1, tile), lambda h, i, o: (h, 0, i))),
            scratch_shapes=[
                pltpu.VMEM((parts * length, HEAD), low_type),
                pltpu.VMEM((HEAD, parts * length), low_type),
                pltpu.VMEM((length, HEAD), low_type),
            ],
        ),
        compiler_params=params(2, 40),
        cost_estimate=brief,
        name="attend_forward",
    )(spots, queries, *keys, *values)


def backward_kernel(tile, parts, extra, spots_ref, q_ref, g_ref, o_ref, log_ref, *refs):
    k_refs, v_refs = refs[:parts], refs[parts : 2 * parts]
    added = refs[2 * parts : 2 * parts + extra]
    dq_ref, dk_ref, dv_ref, ks, vs, kt, gs, os, delta, dqt = refs[2 * parts + extra :]
    rows = q_ref.shape[0]
    steps = rows // tile
    step = pl.program_id(1)

    @pl.when(step == 0)
    def _():
        for part in range(parts):
            ks[part * rows : (part + 1) * rows, :] = k_refs[part][...]
            vs[part * rows : (part + 1) * rows, :] = v_refs[part][...]
            for start in range(0, rows, tile):
                at = slice(part * rows + start, part * rows + start + tile)
                key = k_refs[part][start : start + tile, :]
                kt[:, at] = key.astype(jnp.float32).T.astype(low_type)
        count = spots_ref.shape[0]
        block = rows // count
        for k in range(count):
            there = pl.ds(pl.multiple_of(spots_ref[k] * block, block), block)
            gs[there, :] = g_ref[k * block : (k + 1) * block, :]
            os[there, :] = o_ref[k * block : (k + 1) * block, :]
        for start in range(0, rows, tile):
            at = slice(start, start + tile)
            both = gs[at, :].astype(jnp.float32) * os[at, :].astype(jnp.float32)
            delta[:, at] = jnp.sum(both.T, axis=0, keepdims=True)
        dqt[...] = jnp.zeros_like(dqt)

    here = pl.ds(pl.multiple_of(step * tile, tile), tile)
    key, value, key_turned = ks[here, :], vs[here, :], kt[:, here]

    def visit(i, carry, masked):
        key_sum, value_sum = carry
        at = pl.ds(pl.multiple_of(i * tile, tile), tile)
        query, outward = q_ref[at, :], gs[at, :]
        scores = against(key, query)
        exact = jnp.exp2(scores * exponent_scale - log_ref[0, :, at])
        if masked:
            exact = jnp.where(causal(tile), exact, 0.0)
        slope = (exact * (against(value, outward) - delta[:, at])).astype(low_type)
        value_sum = value_sum + product(exact.astype(low_type), outward)
        key_sum = key_sum + product(slope, query)
        dqt[:, at] += product(key_turned, slope)
        return key_sum, value_sum

    if extra:
        carry = (added[0][...], added[1][...])
    else:
        carry = (jnp.zeros((tile, HEAD), jnp.float32),) * 2
    own = step - (parts - 1) * steps

    def store(carry):
        dk_ref[...], dv_ref[...] = carry

    @pl.when(own < 0)
    def _():
        store(lax.fori_loop(0, steps, lambda i, c: visit(i, c, False), carry))

    @pl.when(own >= 0)
    def _():
        first = visit(own, carry, True)
        store(lax.fori_loop(own + 1, steps, lambda i, c: visit(i, c, False), first))

    @pl.when(own == steps - 1)
    def _():
        for start in range(0, rows, tile):
            at = slice(start, start + tile)
            dq_ref[at, :] = dqt[:, at].T


def attend_backward(queries, outward, attended, logs, keys, values, added, spots):
    length, width = queries.shape
    heads, parts = width // HEAD, len(keys)
    tile = tile_of(length)
    whole = pl.BlockSpec((length, HEAD), lambda h, j, o: (0, h))
    piece = pl.BlockSpec((tile, HEAD), lambda h, j, o: (j, h))
    total = parts * length
    return pl.pallas_call(
        functools.partial(backward_kernel, tile, parts, len(added)),
        out_shape=(
            jax.ShapeDtypeStruct((length, width), jnp.float32),
            jax.ShapeDtypeStruct((total, width), jnp.float32),
            jax.ShapeDtypeStruct((total, width), jnp.float32),
        ),
        grid_spec=pltpu.PrefetchScalarGridSpec(
            num_scalar_prefetch=1,
            grid=(heads, total // tile),
            in_specs=[whole] * 3
            + [pl.BlockSpec((1, 1, length), lambda h, j, o: (h, 0, 0))]
            + [whole] * (2 * parts)
            + [piece] * len(added),
            out_specs=(whole, piece, piece),
            scratch_shapes=[
                pltpu.VMEM((total, HEAD), low_type),
                pltpu.VMEM((total, HEAD), low_type),
                pltpu.VMEM((HEAD, total), low_type),
                pltpu.VMEM((length, HEAD), low_type),
                pltpu.VMEM((length, HEAD), low_type),
                pltpu.VMEM((1, length), jnp.float32),
                pltpu.VMEM((HEAD, length), jnp.float32),
            ],
        ),
        compiler_params=params(2, 48),
        cost_estimate=brief,
        name="attend_backward",
    )(spots, queries, outward, attended, logs, *keys, *values, *added)


def out_kernel(others_ref, x_ref, w_ref, out_ref):
    @pl.when(pl.program_id(1) == 0)
    def _():
        out_ref[...] = jnp.zeros_like(out_ref)

    out_ref[...] += product(x_ref[0], w_ref[...])


def out_project(pieces, weight, others):
    count, rows, depth = pieces.shape
    width = weight.shape[1]
    across = min(1024, width)
    return pl.pallas_call(
        out_kernel,
        out_shape=jax.ShapeDtypeStruct((rows, width), jnp.float32),
        grid_spec=pltpu.PrefetchScalarGridSpec(
            num_scalar_prefetch=1,
            grid=(width // across, count),
            in_specs=[
                pl.BlockSpec((1, rows, depth), lambda n, k, o: (k, 0, 0)),
                pl.BlockSpec((depth, across), lambda n, k, o: (o[k], n)),
            ],
            out_specs=pl.BlockSpec((rows, across), lambda n, k, o: (0, n)),
        ),
        compiler_params=params(2, 32),
        cost_estimate=brief,
        name="out_project",
    )(others, pieces, weight)


def out_back_kernel(others_ref, x_ref, w_ref, out_ref):
    out_ref[0] = against(x_ref[...], w_ref[...]).astype(low_type)


def out_back(grad, weight, others):
    rows, width = grad.shape
    count = others.shape[0]
    depth = weight.shape[0] // count
    return pl.pallas_call(
        out_back_kernel,
        out_shape=jax.ShapeDtypeStruct((count, rows, depth), low_type),
        grid_spec=pltpu.PrefetchScalarGridSpec(
            num_scalar_prefetch=1,
            grid=(count,),
            in_specs=[
                pl.BlockSpec((rows, width), lambda k, o: (0, 0)),
                pl.BlockSpec((depth, width), lambda k, o: (o[k], 0)),
            ],
            out_specs=pl.BlockSpec((1, rows, depth), lambda k, o: (k, 0, 0)),
        ),
        compiler_params=params(1, 32),
        cost_estimate=brief,
        name="out_back",
    )(others, grad, weight)


def out_weight_kernel(streams, others_ref, *refs):
    lefts, rights, out_ref = refs[:streams], refs[streams:-1], refs[-1]
    total = 0.0
    for left, right in zip(lefts, rights):
        total = total + product(left[0].T, right[...])
    out_ref[...] = total.astype(low_type)


def out_weight(lefts, rights, others):
    count, rows, depth = lefts[0].shape
    width = rights[0].shape[1]
    across = min(1024, width)
    return pl.pallas_call(
        functools.partial(out_weight_kernel, len(lefts)),
        out_shape=jax.ShapeDtypeStruct((count * depth, width), low_type),
        grid_spec=pltpu.PrefetchScalarGridSpec(
            num_scalar_prefetch=1,
            grid=(width // across, count),
            in_specs=[pl.BlockSpec((1, rows, depth), lambda n, k, o: (k, 0, 0))] * len(lefts)
            + [pl.BlockSpec((rows, across), lambda n, k, o: (0, n))] * len(rights),
            out_specs=pl.BlockSpec((depth, across), lambda n, k, o: (o[k], n)),
        ),
        compiler_params=params(2, 32),
        cost_estimate=brief,
        name="out_weight",
    )(others, *lefts, *rights)


def chosen(refs, index, use):
    for i, ref in enumerate(refs):
        pl.when(index == i)(functools.partial(use, ref))


def gate_up_kernel(count, parts, *refs):
    pieces, refs = refs[:count], refs[count:]
    gates, ups = refs[:parts], refs[parts : 2 * parts]
    gate_ref, up_ref, inner_ref = refs[2 * parts :]
    half = pieces[0].shape[1] // parts

    def use(x_ref):
        gate = up = 0.0
        for p in range(parts):
            piece = x_ref[:, p * half : (p + 1) * half]
            gate = gate + product(piece, gates[p][...])
            up = up + product(piece, ups[p][...])
        gate_ref[...] = gate.astype(low_type)
        up_ref[...] = up.astype(low_type)
        inner_ref[...] = (gate * jax.nn.sigmoid(gate) * up).astype(low_type)

    chosen(pieces, pl.program_id(1), use)


def gate_up(pieces, gates, ups):
    count, (rows, width) = len(pieces), pieces[0].shape
    parts, columns = len(gates), gates[0].shape[1]
    across = min(512, columns)
    weight = pl.BlockSpec((width // parts, across), lambda n, m: (0, n))
    out = pl.BlockSpec((rows, across), lambda n, m: (m, n))
    return pl.pallas_call(
        functools.partial(gate_up_kernel, count, parts),
        grid=(columns // across, count),
        out_shape=(jax.ShapeDtypeStruct((count * rows, columns), low_type),) * 3,
        in_specs=[pl.BlockSpec((rows, width), lambda n, m: (0, 0))] * count
        + [weight] * (2 * parts),
        out_specs=(out,) * 3,
        compiler_params=params(2, 52),
        cost_estimate=brief,
        name="gate_up",
    )(*pieces, *gates, *ups)


def spread_kernel(terms, parts, *refs):
    lefts, weights, out = refs[:terms], refs[terms:-1], refs[-1]
    for p in range(parts):
        total = 0.0
        for t in range(terms):
            total = total + against(lefts[t][...], weights[t * parts + p][...])
        out[p] = total.astype(low_type)


def spread(lefts, weights, half):
    rows, columns = lefts[0].shape[0] // 2, lefts[0].shape[1]
    terms, parts, features = len(lefts), len(weights[0]), weights[0][0].shape[0]
    across = min(256, features)
    return pl.pallas_call(
        functools.partial(spread_kernel, terms, parts),
        grid=(features // across,),
        out_shape=jax.ShapeDtypeStruct((parts, rows, features), low_type),
        in_specs=[pl.BlockSpec((rows, columns), lambda n: (half, 0))] * terms
        + [pl.BlockSpec((across, columns), lambda n: (n, 0))] * (terms * parts),
        out_specs=pl.BlockSpec((parts, rows, across), lambda n: (0, 0, n)),
        compiler_params=params(1, 52),
        cost_estimate=brief,
        name="spread",
    )(*lefts, *[w for group in weights for w in group])


def inner_kernel(count, parts, *refs):
    pieces, (gate_ref, up_ref), refs = refs[:count], refs[count : count + 2], refs[count + 2 :]
    weights, (dgate_ref, dup_ref) = refs[:parts], refs[parts:]
    half = pieces[0].shape[1] // parts

    def use(x_ref):
        grad = 0.0
        for p in range(parts):
            grad = grad + product(x_ref[:, p * half : (p + 1) * half], weights[p][...])
        gate, up = gate_ref[...].astype(jnp.float32), up_ref[...].astype(jnp.float32)
        sigma = jax.nn.sigmoid(gate)
        dgate_ref[...] = (grad * up * sigma * (1.0 + gate * (1.0 - sigma))).astype(low_type)
        dup_ref[...] = (grad * gate * sigma).astype(low_type)

    chosen(pieces, pl.program_id(1), use)


def inner_backward(pieces, gate, up, downs):
    count, (rows, width) = len(pieces), pieces[0].shape
    parts, columns = len(downs), downs[0].shape[1]
    across = min(1024, columns)
    out = pl.BlockSpec((rows, across), lambda n, m: (m, n))
    return pl.pallas_call(
        functools.partial(inner_kernel, count, parts),
        grid=(columns // across, count),
        out_shape=(jax.ShapeDtypeStruct((count * rows, columns), low_type),) * 2,
        in_specs=[pl.BlockSpec((rows, width), lambda n, m: (0, 0))] * count
        + [out, out]
        + [pl.BlockSpec((width // parts, across), lambda n, m: (0, n))] * parts,
        out_specs=(out,) * 2,
        compiler_params=params(2, 52),
        cost_estimate=brief,
        name="inner_backward",
    )(*pieces, gate, up, *downs)


def weight_kernel(count, each, *refs):
    lefts, rights, (out, turned) = refs[:count], refs[count : count + count // each], refs[-2:]
    rows = lefts[0].shape[0]

    @pl.when(pl.program_id(1) == 0)
    def _():
        for c in range(count):
            turned[:, c * rows : (c + 1) * rows] = lefts[c][...].T

    total = 0.0
    for s, right in enumerate(rights):
        at = slice(s * each * rows, (s + 1) * each * rows)
        total = total + product(turned[:, at], right[...])
    out[...] = total.astype(low_type)


def weight_gradient(lefts, rights, start, size):
    each, rows = len(lefts[0]), lefts[0][0].shape[0]
    columns, count = rights[0].shape[1], len(lefts) * each
    tile = min(512, size)
    across = next(a for a in (1024, 768, 512, 384, 128) if columns % a == 0)
    first = start // tile
    return pl.pallas_call(
        functools.partial(weight_kernel, count, each),
        grid=(size // tile, columns // across),
        out_shape=jax.ShapeDtypeStruct((size, columns), low_type),
        in_specs=[pl.BlockSpec((rows, tile), lambda m, n: (0, first + m))] * count
        + [pl.BlockSpec((each * rows, across), lambda m, n: (0, n))] * len(rights),
        out_specs=pl.BlockSpec((tile, across), lambda m, n: (m, n)),
        scratch_shapes=[pltpu.VMEM((tile, count * rows), low_type)],
        compiler_params=params(2, 52),
        cost_estimate=brief,
        name="weight_gradient",
    )(*[left for group in lefts for left in group], *rights)


def update_kernel(steps, columns_ref, *refs):
    grads, (w, m, v, g_out, m_out, v_out, w_out) = refs[: len(steps)], refs[len(steps) :]
    step = pl.program_id(0)
    first = 0
    for count, grad_ref in zip(steps, grads):

        @pl.when((step >= first) & (step < first + count))
        def _(grad_ref=grad_ref):
            gradient = grad_ref[...].astype(jnp.float32)
            moment, square, weight = adamw(
                w[...], m[...], v[...], gradient, learn_rate, weight_decay
            )
            g_out[...] = gradient
            m_out[...] = moment
            v_out[...] = square
            w_out[...] = weight

        first += count


def update(grads, columns, across, weight, moment, square):
    rows, width = weight.shape
    steps = [g.shape[0] // rows * (g.shape[1] // across) for g in grads]
    specs, first = [], 0
    for g, count in zip(grads, steps):
        per = g.shape[1] // across

        def place(i, c, first=first, count=count, per=per):
            at = jnp.clip(i - first, 0, count - 1)
            return at // per, at % per

        specs.append(pl.BlockSpec((rows, across), place))
        first += count
    here = pl.BlockSpec((rows, across), lambda i, c: (0, c[i]))
    return pl.pallas_call(
        functools.partial(update_kernel, steps),
        out_shape=(jax.ShapeDtypeStruct((rows, width), jnp.float32),) * 4,
        grid_spec=pltpu.PrefetchScalarGridSpec(
            num_scalar_prefetch=1,
            grid=(sum(steps),),
            in_specs=specs + [here] * 3,
            out_specs=(here,) * 4,
        ),
        compiler_params=params(1, 40),
        cost_estimate=brief,
        name="update",
    )(columns, *grads, weight, moment, square)


def swap(value, axis, bits):
    size = lax.axis_size(axis)
    return lax.ppermute(value, axis, [(i, i ^ bits) for i in range(size)])


def pick(pieces, index):
    return lax.dynamic_index_in_dim(pieces, index, axis=0, keepdims=False)


def trade(pieces, axis):
    size, me = lax.axis_size(axis), lax.axis_index(axis)
    mine = pick(pieces, me)
    out = jnp.zeros((size,) + mine.shape, mine.dtype)
    out = lax.dynamic_update_index_in_dim(out, mine, me, 0)
    for bits in range(1, size):
        got = swap(pick(pieces, me ^ bits), axis, bits)
        out = lax.dynamic_update_index_in_dim(out, got, me ^ bits, 0)
    return out


def trade_near(pieces, axis):
    return [pieces[0]] + [swap(pieces[k], axis, k) for k in range(1, lax.axis_size(axis))]


def after(value, *others):
    return lax.optimization_barrier((value,) + others)[0]


def total_of(value, axes):
    for axis in axes:
        bits = 1
        while bits < lax.axis_size(axis):
            value = value + swap(value, axis, bits)
            bits *= 2
    return value


def gather_pairs(value, axis):
    size, me = lax.axis_size(axis), lax.axis_index(axis)
    bits, value = size // 2, value[None]
    while bits:
        other = swap(value, axis, bits)
        low = (me & bits) == 0
        value = jnp.stack([jnp.where(low, value, other), jnp.where(low, other, value)], axis=1)
        value = value.reshape((-1,) + value.shape[2:])
        bits //= 2
    return value


def sum_pairs(pieces, axis):
    size, me = lax.axis_size(axis), lax.axis_index(axis)
    bits = 1
    while bits < size:
        pieces = pieces.reshape((-1, 2) + pieces.shape[1:])
        mine = (me & bits) // bits
        keep = lax.dynamic_index_in_dim(pieces, mine, axis=1, keepdims=False)
        send = lax.dynamic_index_in_dim(pieces, 1 - mine, axis=1, keepdims=False)
        got = swap(send, axis, bits)
        pieces = (keep.astype(jnp.float32) + got.astype(jnp.float32)).astype(pieces.dtype)
        bits *= 2
    return pieces[0]


def near_order(size):
    return list(range(1, size, 2)) + list(range(0, size, 2))


def gather_group(value, axis):
    size = lax.axis_size(axis)
    got, bits = {0: value}, size // 2
    while bits:
        for known in sorted(got):
            got[known ^ bits] = swap(got[known], axis, bits)
        bits //= 2
    return [got[k] for k in near_order(size)]


def sum_group(got, kept, axis):
    size = lax.axis_size(axis)
    parts, bits, low = got.shape[0], 2, got.dtype
    shape = (parts, size // 2, -1) + got.shape[2:]
    pieces, got = kept.reshape(shape), got.reshape(shape)
    while bits < size:
        pieces = pieces.reshape((parts, -1, 2) + pieces.shape[2:])
        got = got.reshape(pieces.shape)
        send = pieces[:, :, 1].astype(jnp.float32) + got[:, :, 1].astype(jnp.float32)
        pieces = pieces[:, :, 0].astype(jnp.float32) + got[:, :, 0].astype(jnp.float32)
        got = swap(send.astype(low), axis, bits)
        bits *= 2
    return pieces[:, 0].astype(jnp.float32) + got[:, 0].astype(jnp.float32)


def own_first(parts, axis):
    size, me = lax.axis_size(axis), lax.axis_index(axis)
    bits = 1
    while bits < size:
        parts = [jnp.where((me & bits) == 0, parts[i], parts[i ^ bits]) for i in range(size)]
        bits *= 2
    return jnp.concatenate(parts, axis=1)


def adamw(weight, moment, square, gradient, rate, decay):
    moment_new = beta_first * moment + (1.0 - beta_first) * gradient
    square_new = beta_second * square + (1.0 - beta_second) * gradient * gradient
    fix_first = 1.0 - beta_first**STEP
    fix_second = 1.0 - beta_second**STEP
    update = moment_new / fix_first / (jnp.sqrt(square_new / fix_second) + epsilon_adam)
    return (moment_new, square_new, weight - rate * (update + decay * weight))


def body(
    tokens,
    cotangent,
    pairing,
    attention_weights,
    attention_moment,
    attention_square,
    feed_weights,
    feed_moment,
    feed_square,
    gains,
    gain_moment,
    gain_square,
):
    inputs = tokens[0, 0]
    rows, width = inputs.shape
    dps, ctxs, groups = lax.axis_size("dp"), lax.axis_size("ctx"), lax.axis_size("fsdp")
    ctx = lax.axis_index("ctx")
    block = rows // 2
    length = block * ctxs
    owned = attention_weights.shape[0]
    hidden = feed_weights.shape[1] // 3
    part = hidden // groups
    head_width = width // ctxs
    upstream = cotangent[0, 0].astype(jnp.float32)

    rows_of = (slice(0, block), slice(block, rows))
    orders = (pairing[0, 0], ctxs - 1 - pairing[0, 0])
    turns = [turn_tables(start + jnp.arange(length, dtype=jnp.int32)) for start in (0, length)]

    def feed_columns(own, after):
        own, after = lax.optimization_barrier((own, after))
        own = lax.all_gather(own, "ctx", axis=0, tiled=True)
        return [own] + [swap(own, "dp", bits) for bits in range(1, dps)]

    inputs_all = lax.all_gather(inputs, "ctx", axis=0, tiled=True)
    qkv_low = attention_weights[:, : 3 * width].astype(low_type)
    qkv_low = qkv_low.reshape(owned, 3, ctxs, head_width).transpose(2, 0, 1, 3)
    qkv_low = qkv_low.reshape(ctxs, owned, 3 * head_width)
    feed_low = after(feed_weights, qkv_low).astype(low_type)
    qkv_mine = qkv_low = trade(qkv_low, "ctx")
    feed_low = feed_low.reshape(owned, 3, groups, part).transpose(2, 1, 0, 3)
    feed_low = trade(feed_low, "fsdp").transpose(1, 0, 2, 3).reshape(3, groups * owned, part)
    qkv_low = gather_pairs(gather_pairs(qkv_low, "dp"), "fsdp")
    qkv_low = qkv_low.transpose(1, 2, 0, 3, 4).reshape(width, 3 * head_width)
    out_low = after(attention_weights[:, 3 * width :].astype(low_type), qkv_mine)
    out_low = gather_pairs(gather_pairs(out_low, "ctx"), "dp")
    inputs_all, qkv_low, feed_low, out_low, turns = lax.optimization_barrier(
        (inputs_all, qkv_low, feed_low, out_low, turns)
    )

    gates = feed_columns(feed_low[0], inputs_all)

    others = jnp.arange(ctxs, dtype=jnp.int32) ^ ctx
    spots = [jnp.sum(jnp.where(others[:, None] == jnp.arange(ctxs), o, 0), axis=1) for o in orders]
    qk_gains = jnp.stack(
        [lax.dynamic_slice_in_dim(gains[i], ctx * head_width, head_width) for i in range(2)]
    )
    queries, keys, values = [], [], []
    attended, logs, attended_near = [], [], []
    projs, proj_scales, states, chunks = [], [], [], []
    projected = product(inputs_all, qkv_low)
    pre = [projected[:, i * head_width : (i + 1) * head_width] for i in range(2)]
    squares = after(jnp.stack([jnp.sum(p * p, axis=-1) for p in pre]), gates[0])
    squares = total_of(squares, ("ctx",))
    scales = lax.rsqrt(squares / width + epsilon_norm).T
    for s in range(2):
        q, k, v = prepare(projected, scales, qk_gains, *turns[s], orders[s], s)
        queries.append(q)
        keys.append(k)
        values.append(v)

    def attend(s, last):
        out, log = attend_forward(after(queries[s], last), keys[: s + 1], values[: s + 1], spots[s])
        attended.append(out)
        logs.append(log)
        attended_near.append(jnp.stack(trade_near(out.reshape(ctxs, block, head_width), "ctx")))

    def leave(s, last):
        proj = out_project(after(attended_near[s], last), out_low, others)
        projs.append(proj)
        proj_scales.append(
            lax.rsqrt(jnp.mean(proj * proj, axis=-1, keepdims=True) + epsilon_norm)
        )
        states.append(
            inputs[rows_of[s]].astype(jnp.float32) + proj * proj_scales[s] * gains[2]
        )
        state_low = states[s].astype(low_type)
        state_low = own_first(jnp.split(state_low, dps, axis=1), "dp")
        chunks.append(gather_group(state_low, "fsdp"))

    out_low = gather_pairs(after(out_low, scales), "fsdp")
    out_low = out_low.transpose(1, 2, 0, 3, 4).reshape(width, width)
    attend(0, gates[0])
    ups = feed_columns(feed_low[1], gates[0])
    last = after(attended[0], ups[0])
    downs = feed_columns(feed_low[2], last)
    attend(1, last)
    leave(0, attended[1])
    attended_near[1] = after(attended_near[1], gates[-1])
    leave(1, states[0])

    gate, up, inner = [None] * 2, [None] * 2, [None] * 2
    chunks[0][-1] = after(chunks[0][-1], downs[0])
    gate[0], up[0], inner[0] = gate_up(chunks[0], gates, ups)
    chunks[1][-1] = after(chunks[1][-1], gate[0])
    gate[1], up[1], inner[1] = gate_up(chunks[1], gates, ups)
    outs, grad_downs, gain_downs = [None] * 2, [None] * 2, [None] * 2
    last, halves = inner[0], {}
    for s in (1, 0):
        last = spread([after(inner[s], last)], [downs], 0)
        halves[s, 0] = swap(last, "fsdp", 1)
        halves[s, 1] = spread([after(inner[s], last)], [downs], 1)
        last = after(halves[s, 1], halves[s, 0])
    for s in (1, 0):
        down = own_first(list(sum_group(halves[s, 0], halves[s, 1], "fsdp")), "dp")
        down_scale = lax.rsqrt(jnp.mean(down * down, axis=-1, keepdims=True) + epsilon_norm)
        outs[s] = (states[s] + down * down_scale * gains[3]).astype(low_type)
        grad_down, gain_downs[s] = norm_backward(
            down, down_scale, gains[3], upstream[rows_of[s]]
        )
        grad_down = own_first(jnp.split(grad_down.astype(low_type), dps, axis=1), "dp")
        grad_downs[s] = gather_group(grad_down, "fsdp")
    output_states = jnp.concatenate(outs, axis=0)

    grad_gates, grad_ups, grad_states = [None] * 2, [None] * 2, [None] * 2
    grad_projs, grad_heads, gain_branches = [None] * 2, [None] * 2, [None] * 2
    size = width // dps

    def inward(s, last):
        grad_gates[s], grad_ups[s] = inner_backward(
            grad_downs[s], after(gate[s], last), up[s], downs
        )
        last = after(grad_ups[s], *grad_downs[0])
        last = spread([after(grad_gates[s], last), grad_ups[s]], [gates, ups], 0)
        got = swap(last, "fsdp", 1)
        last = spread([after(grad_gates[s], last), grad_ups[s]], [gates, ups], 1)
        return [got, last], after(last, got)

    def gradient_parts(lefts, rights, which, last):
        lefts = [[after(left[0], last)] + left[1:] for left in lefts]
        found = [weight_gradient(lefts, rights, bits * size, size) for bits in which]
        return found, found[-1]

    def outward(s, sums):
        back = sum_group(*sums, "fsdp")
        grad_states[s] = upstream[rows_of[s]] + own_first(list(back), "dp")
        grad_proj, gain_branches[s] = norm_backward(
            projs[s], proj_scales[s], gains[2], grad_states[s]
        )
        grad_projs[s] = grad_proj.astype(low_type)
        grad_attended = out_back(grad_projs[s], out_low, others)
        grad_heads[s] = jnp.concatenate(trade_near(grad_attended, "ctx"), axis=0)
        return grad_attended

    away, near = range(1, dps), range(1)
    sums, last = inward(1, downs[-1])
    down_away, last = gradient_parts(grad_downs, inner, away, last)
    down_away = [swap(piece, "dp", bits) for bits, piece in zip(away, down_away)]
    lower_sums, last = inward(0, last)
    gate_away, last = gradient_parts(chunks, grad_gates, away, last)
    gate_away = [swap(piece, "dp", bits) for bits, piece in zip(away, gate_away)]
    down_near, last = gradient_parts(grad_downs, inner, near, last)

    def kept_feed(own, others):
        kept = own[0].astype(jnp.float32)
        for other in others:
            kept = kept + other.astype(jnp.float32)
        return kept.astype(low_type)

    def reduce_feed(kept):
        return lax.psum_scatter(kept, "ctx", scatter_dimension=0, tiled=True)

    down_kept = kept_feed(down_near, down_away)
    down_gradient = reduce_feed(down_kept)
    sums[1] = after(sums[1], last, down_kept)
    last = outward(1, sums)
    up_away, last = gradient_parts(chunks, grad_ups, away, last)
    up_away = [swap(piece, "dp", bits) for bits, piece in zip(away, up_away)]
    lower_sums[1] = after(lower_sums[1], last)
    last = outward(0, lower_sums)
    gate_near, last = gradient_parts(chunks, grad_gates, near, last)
    gate_kept = kept_feed(gate_near, gate_away)
    gate_gradient = reduce_feed(gate_kept)
    last = after(last, gate_kept, grad_heads[1])
    up_near, last = gradient_parts(chunks, grad_ups, near, last)
    attended_near[0] = after(attended_near[0], last)
    out_gradient = out_weight(attended_near, grad_projs, others)
    queries[1] = after(queries[1], out_gradient)
    up_kept = kept_feed(up_near, up_away)
    up_gradient = reduce_feed(up_kept)

    out_gradient = out_gradient.reshape(dps, ctxs, groups, owned, width).transpose(2, 0, 1, 3, 4)
    out_gradient = sum_pairs(out_gradient, "fsdp")

    def stream_rows(values, s):
        return values.reshape((ctxs, 2, block) + values.shape[1:])[:, s].reshape(
            (length,) + values.shape[1:]
        )

    added, grad_inputs, grad_projected = (), [None] * 2, [None] * 2
    gain_qk = 0.0
    for s in (1, 0):
        if s == 0:
            out_gradient = sum_pairs(out_gradient, "dp")
            added, grad_part, out_gradient = lax.optimization_barrier(
                (added, grad_part, out_gradient)
            )
            grad_inputs[1] = lax.psum_scatter(grad_part, "ctx", scatter_dimension=0, tiled=True)
        grads = attend_backward(
            queries[s],
            grad_heads[s],
            attended[s],
            logs[s],
            keys[: s + 1],
            values[: s + 1],
            added,
            spots[s],
        )
        if s == 1:
            grads, out_gradient, up_kept, grad_heads[0] = lax.optimization_barrier(
                (grads, out_gradient, up_kept, grad_heads[0])
            )
        added = grads[1:]
        weighted, value_low, dots, gain_sums = restore(
            grads, projected, scales, qk_gains, *turns[s], orders[s], s
        )
        gain_qk = gain_qk + gain_sums
        means = total_of(dots.T, ("ctx",)).T / width
        grad_pre = []
        for i in range(2):
            at = slice(i * head_width, (i + 1) * head_width)
            scale = stream_rows(scales, s)[:, i : i + 1]
            unit = stream_rows(projected, s)[:, at] * scale
            grad_pre.append(
                (scale * (weighted[:, at] - unit * means[:, i : i + 1])).astype(low_type)
            )
        grad_projected[s] = jnp.concatenate(grad_pre + [value_low], axis=1)
        grad_part = against(grad_projected[s], qkv_low).astype(low_type)
    grad_inputs[0] = lax.psum_scatter(grad_part, "ctx", scatter_dimension=0, tiled=True)
    out_gradient = sum_pairs(out_gradient, "ctx")
    input_gradient = jnp.concatenate(
        [grad_states[s] + grad_inputs[s].astype(jnp.float32) for s in range(2)], axis=0
    ).astype(low_type)

    qkv_gradient = weight_gradient(
        [[stream_rows(inputs_all, 0)], [stream_rows(after(inputs_all, grad_part), 1)]],
        grad_projected,
        0,
        width,
    )
    qkv_gradient = qkv_gradient.reshape(dps, ctxs, groups, owned, 3 * head_width)
    qkv_gradient = sum_pairs(sum_pairs(qkv_gradient.transpose(2, 0, 1, 3, 4), "fsdp"), "dp")
    qkv_gradient = jnp.concatenate(
        trade_near([pick(qkv_gradient, ctx ^ k) for k in range(ctxs)], "ctx"), axis=0
    )

    fsdp = lax.axis_index("fsdp")
    feed_pieces = []
    for piece in (gate_gradient, up_gradient, down_gradient):
        piece = piece.reshape(groups, owned, part)
        feed_pieces += trade_near([pick(piece, fsdp ^ k) for k in range(groups)], "fsdp")
    near_columns = jnp.arange(groups, dtype=jnp.int32) ^ fsdp
    feed_columns_of = jnp.concatenate([kind * groups + near_columns for kind in range(3)])
    feed_gradient, feed_moment_new, feed_square_new, feed_weights_new = update(
        [jnp.concatenate(feed_pieces, axis=0)],
        feed_columns_of,
        part,
        feed_weights,
        feed_moment,
        feed_square,
    )
    attention_columns = jnp.concatenate(
        [
            (jnp.arange(3, dtype=jnp.int32)[None, :] * ctxs + others[:, None]).reshape(-1),
            3 * ctxs + jnp.arange(ctxs, dtype=jnp.int32),
        ]
    )
    attention_gradient, attention_moment_new, attention_square_new, attention_weights_new = update(
        [qkv_gradient, out_gradient],
        attention_columns,
        head_width,
        attention_weights,
        attention_moment,
        attention_square,
    )

    wide = lax.dynamic_update_slice(
        jnp.zeros((2, width), jnp.float32), gain_qk, (0, ctx * head_width)
    )
    gain_gradient = total_of(
        jnp.concatenate([wide, jnp.stack([sum(gain_branches), sum(gain_downs)])], axis=0), EVERY
    )
    gain_moment_new, gain_square_new, gains_new = adamw(
        gains, gain_moment, gain_square, gain_gradient, gain_rate, 0.0
    )
    return (
        output_states[None, None],
        input_gradient[None, None],
        attention_gradient,
        attention_moment_new,
        attention_square_new,
        attention_weights_new,
        feed_gradient,
        feed_moment_new,
        feed_square_new,
        feed_weights_new,
        gain_gradient,
        gain_moment_new,
        gain_square_new,
        gains_new,
    )


def solution(mesh):
    token = P("dp", "fsdp", "ctx", None)
    row = P(EVERY, None)
    return jax.shard_map(
        body,
        mesh=mesh,
        in_specs=(token, token, P("dp", "fsdp", None)) + (row,) * 6 + (P(),) * 3,
        out_specs=(token, token) + (row,) * 8 + (P(),) * 4,
        check_vma=False,
    )
```

time: 4760 us -> 2010 us (0.42)
  waiting for transfers between devices: 3090 us -> 824 us
  matrix products: 940 us -> 52.7 us
  Pallas kernels: 0 us -> 655 us
  other arithmetic: 400 us -> 174 us
  starting transfers between devices: 0.5 us -> 81.7 us
  local copies, waits for them, and re-layouts: 261 us -> 196 us
    reduce_scatter x3 -> x5, waiting for transfers between devices: 1930 us -> 0.07 us  [the longest x3 0.06 us: reduce_feed(): return lax.psum_scatter(kept, 'ctx', scatter_dimension=0, tiled=True)]
    dot_general x50 -> x1, matrix products: 797 us -> 24 us  [product(): return jnp.dot(left, right, preferred_element_type=jnp.float32)]
    ppermute x0 -> x83, waiting for transfers between devices: none -> 683 us  [swap(): return lax.ppermute(value, axis, [(i, i ^ bits) for i in range(size)])]
    pallas_call x0 -> x34, Pallas kernels: none -> 655 us  [the longest x7 159 us: weight_gradient(): pl.pallas_call(functools.partial(weight_kernel, count, each), grid=(size...]
    all_gather x4, waiting for transfers between devices: 765 us -> 139 us  [the longest x3 81.2 us: feed_columns(): own = lax.all_gather(own, 'ctx', axis=0, tiled=True)]
    unnamed x9, waiting for transfers between devices: 391 us -> 0.81 us
    concatenate x6 -> x19, other arithmetic: 189 us -> 24.3 us  [the longest x3 8.05 us: body(): jnp.concatenate([grad_states[s] + grad_inputs[s].astype(jnp.float32) for...]
    dot_general x4 -> x2, matrix products: 144 us -> 28.7 us  [against(): lax.dot_general(left, right, (((1,), (1,)), ((), ())), preferred_element_...]
  transfers between devices with their start and end apart: 8 -> 92, of which waited for: 8 -> 36; matrix products, arithmetic and copies ran while one was open for 16% -> 17% of each run, Pallas kernels for 0% -> 30%
where the time goes in v1:
time: 2010 us; the launch traced here: 2000 us
  waiting for transfers between devices  824 us (41%)
  Pallas kernels  655 us (33%)
  local copies, waits for them, and re-layouts  196 us (10%)
  other arithmetic  174 us (9%)
  starting transfers between devices  81.7 us (4%)
  matrix products  52.7 us (3%)
    ppermute x83, waiting for transfers between devices, swap(): return lax.ppermute(value, axis, [(i, i ^ bits) for i in range(size)])  683 us
    pallas_call x7, Pallas kernels, weight_gradient(): pl.pallas_call(functools.partial(weight_kernel, count, each), grid=(size...  159 us
    pallas_call x8, Pallas kernels, spread(): pl.pallas_call(functools.partial(spread_kernel, terms, parts), grid=(feat...  121 us
    pallas_call x2, Pallas kernels, attend_backward(): pl.pallas_call(functools.partial(backward_kernel, tile, parts, len(added)...  91.1 us
    all_gather x3, waiting for transfers between devices, feed_columns(): own = lax.all_gather(own, 'ctx', axis=0, tiled=True)  81.2 us
    ppermute x83, starting transfers between devices, swap(): return lax.ppermute(value, axis, [(i, i ^ bits) for i in range(size)])  81.2 us
    pallas_call x2, Pallas kernels, gate_up(): pl.pallas_call(functools.partial(gate_up_kernel, count, parts), grid=(col...  73.7 us
    unnamed x294, local copies, waits for them, and re-layouts  71.9 us
  transfers between devices with their start and end apart: 92, of which 36 were waited for; matrix products, arithmetic and copies ran while one was open for 17% of the time, Pallas kernels for 30%

profile of v1, /device:TPU:0, one launch (start us, length us, event | category | flops | bytes accessed | tf_op | source)
XLA Modules:
  0.0 1999.3 jit_solution(529162229669449559)
XLA Ops:
  54.4 11.2 collective-permute-done.3
  85.4 22.3 %collective-permute-done.9 = bf16[1,64,2048]{2,1,0:T(8,128)(2,1)} collective-permute-done((bf16[1,64,2048]{2,1,0:T(8,128)(2,1)S(1)}, bf16[1,64,2048]{2,1,0:T(8,128)(2,1)}, u32[]{:S(2)}, u32[]{:S(2)}) %collective-permute-start.9) | collective-permute-done | bytes 262176 | tf_op jit(solution)/shard_map/ppermute | solution.py:682
  115.7 52.6 %collective-permute-done.10 = bf16[2,64,2048]{2,1,0:T(8,128)(2,1)} collective-permute-done((bf16[2,64,2048]{2,1,0:T(8,128)(2,1)}, bf16[2,64,2048]{2,1,0:T(8,128)(2,1)}, u32[]{:S(2)}, u32[]{:S(2)}) %collective-permute-start.10) | collective-permute-done | bytes 524320 | tf_op jit(solution)/shard_map/ppermute | solution.py:682
  192.7 58.1 %all-gather.12.cloned.1.call-done = bf16[1,1,3072,2048]{3,2,1,0:T(8,128)(2,1)} async-done(((bf16[1,1,768,2048]{3,2,1,0:T(8,128)(2,1)}), bf16[1,1,3072,2048]{3,2,1,0:T(8,128)(2,1)}) %all-gather.12.cloned.1.call-update) | async-done | bytes 12582928 | tf_op jit(solution)/shard_map/all_gather | solution.py:825
  254.6 81.2 %all-gather.6.cloned.1.call-done.refs_4_.refs_2_ = bf16[1024,2048]{1,0:T(8,128)(2,1)} async-done(((bf16[256,2048]{1,0:T(8,128)(2,1)}), bf16[1024,2048]{1,0:T(8,128)(2,1)}) %all-gather.6.cloned.1.call-update) | async-done | bytes 4194320 | tf_op jit(solution)/shard_map/all_gather | solution.py:822
  335.8 24.0 %fusion.46.q_ref.k_ref.v_ref = f32[3072,1536]{1,0:T(8,128)S(1)} fusion(bf16[3072,2048]{1,0:T(8,128)(2,1)} %bitcast.450, bf16[2048,1536]{1,0:T(8,128)(2,1)} %bitcast.464), kind=kOutput, calls=%fused_computation.288 | convolution fusion | flops 19327352832 | bytes 37748736 | tf_op jit(solution)/shard_map/dot_general | solution.py:52
  386.7 42.9 %collective-permute-done.17 = bf16[1,2,4,64,2048]{4,3,2,1,0:T(8,128)(2,1)} collective-permute-done((bf16[1,2,4,64,2048]{4,3,2,1,0:T(8,128)(2,1)}, bf16[1,2,4,64,2048]{4,3,2,1,0:T(8,128)(2,1)}, u32[]{:S(2)}, u32[]{:S(2)}) %collective-permute-start.17) | collective-permute-done | bytes 2097184 | tf_op jit(solution)/shard_map/ppermute | solution.py:682
  441.8 19.7 attend_forward.2
  487.1 49.8 %collective-permute-done.15 = bf16[384,512]{1,0:T(8,128)(2,1)S(1)} collective-permute-done((bf16[384,512]{1,0:T(8,128)(2,1)S(1)}, bf16[384,512]{1,0:T(8,128)(2,1)S(1)}, u32[]{:S(2)}, u32[]{:S(2)}) %collective-permute-start.15) | collective-permute-done | bytes 393248 | tf_op jit(solution)/shard_map/ppermute | solution.py:682
  537.1 46.0 %attend_forward.3 = (bf16[1536,512]{1,0:T(8,128)(2,1)S(1)}, f32[4,1,1536]{2,1,0:T(1,128)S(1)}) custom-call(s32[4]{0:T(128)S(1)} %get-tuple-element.237.spots_ref, bf16[1536,512]{1,0:T(8,128)(2,1)S(1)} %get-tuple-element.181.q_ref, bf16[1536,512]{1,0:T(8,128)(2,1)S(1)} %get-tuple-element.126.refs_0_, bf16[1536,512]{1,0:T(8,128)(2,1)S(1)} %get-tuple-element.135.refs_1_, ...), custom_call_target="tpu_custom_call" | custom-call | flops 1024 | bytes 1024 | tf_op jit(solution)/shard_map/attend_forward/pallas_call | solution.py:274
  654.7 18.3 collective-permute-done.20.refs_3_
  674.2 32.2 %collective-permute-done.31.refs_3_.refs_7_ = bf16[384,2048]{1,0:T(8,128)(2,1)} collective-permute-done((bf16[384,2048]{1,0:T(8,128)(2,1)}, bf16[384,2048]{1,0:T(8,128)(2,1)}, u32[]{:S(2)}, u32[]{:S(2)}) %collective-permute-start.31) | collective-permute-done | bytes 1572896 | tf_op jit(solution)/shard_map/ppermute | solution.py:682
  707.6 36.9 %gate_up.2 = (bf16[1536,2048]{1,0:T(8,128)(2,1)}, bf16[1536,2048]{1,0:T(8,128)(2,1)}, bf16[1536,2048]{1,0:T(8,128)(2,1)}) custom-call(bf16[384,2048]{1,0:T(8,128)(2,1)S(1)} %collective-permute-done.19.refs_0_, bf16[384,2048]{1,0:T(8,128)(2,1)} %copy-done.66, bf16[384,2048]{1,0:T(8,128)(2,1)} %copy-done.64, bf16[384,2048]{1,0:T(8,128)(2,1)} %copy-done.65, ...), custom_call_target="tpu_custom_call" | custom-call | flops 1024 | bytes 1024 | tf_op jit(solution)/shard_map/gate_up/pallas_call | solution.py:520
  744.5 24.8 %collective-permute-done.24.refs_2_.refs_7_ = bf16[1024,2048]{1,0:T(8,128)(2,1)S(1)} collective-permute-done((bf16[1024,2048]{1,0:T(8,128)(2,1)}, bf16[1024,2048]{1,0:T(8,128)(2,1)S(1)}, u32[]{:S(2)}, u32[]{:S(2)}) %collective-permute-start.24) | collective-permute-done | bytes 4194336 | tf_op jit(solution)/shard_map/ppermute | solution.py:682
  783.4 36.8 %gate_up.3 = (bf16[1536,2048]{1,0:T(8,128)(2,1)}, bf16[1536,2048]{1,0:T(8,128)(2,1)}, bf16[1536,2048]{1,0:T(8,128)(2,1)}) custom-call(bf16[384,2048]{1,0:T(8,128)(2,1)S(1)} %collective-permute-done.30.refs_0_.refs_4_, bf16[384,2048]{1,0:T(8,128)(2,1)} %copy-done.67, bf16[384,2048]{1,0:T(8,128)(2,1)} %pad_maximum_fusion.11.refs_2_.refs_6_, ...), custom_call_target="tpu_custom_call" | custom-call | flops 1024 | bytes 1024 | tf_op jit(solution)/shard_map/gate_up/pallas_call | solution.py:520
  831.6 11.3 spread.9
  862.7 20.8 %collective-permute-done.26 = bf16[2,1,384,1024]{3,2,0,1:T(8,128)(2,1)} collective-permute-done((bf16[2,1,384,1024]{3,2,0,1:T(8,128)(2,1)S(1)}, bf16[2,1,384,1024]{3,2,0,1:T(8,128)(2,1)}, u32[]{:S(2)}, u32[]{:S(2)}) %collective-permute-start.26) | collective-permute-done | bytes 1572896 | tf_op jit(solution)/shard_map/ppermute | solution.py:682
  886.7 29.5 %collective-permute-done.34 = bf16[2,1,384,1024]{3,2,0,1:T(8,128)(2,1)S(1)} collective-permute-done((bf16[2,1,384,1024]{3,2,0,1:T(8,128)(2,1)S(1)}, bf16[2,1,384,1024]{3,2,0,1:T(8,128)(2,1)S(1)}, u32[]{:S(2)}, u32[]{:S(2)}) %collective-permute-start.34) | collective-permute-done | bytes 1572896 | tf_op jit(solution)/shard_map/ppermute | solution.py:682
  930.3 34.1 %collective-permute-done.39.refs_3_.refs_7_ = bf16[384,2048]{1,0:T(8,128)(2,1)S(1)} collective-permute-done((bf16[384,2048]{1,0:T(8,128)(2,1)S(1)}, bf16[384,2048]{1,0:T(8,128)(2,1)S(1)}, u32[]{:S(2)}, u32[]{:S(2)}) %collective-permute-start.39) | collective-permute-done | bytes 1572896 | tf_op jit(solution)/shard_map/ppermute | solution.py:682
  969.0 24.8 %inner_backward.2 = (bf16[1536,2048]{1,0:T(8,128)(2,1)}, bf16[1536,2048]{1,0:T(8,128)(2,1)}) custom-call(bf16[384,2048]{1,0:T(8,128)(2,1)S(1)} %collective-permute-done.38.refs_0_.refs_4_, bf16[384,2048]{1,0:T(8,128)(2,1)} %copy-done.82, bf16[384,2048]{1,0:T(8,128)(2,1)} %copy-done.71, bf16[384,2048]{1,0:T(8,128)(2,1)} %copy-done.81, ...), custom_call_target="tpu_custom_call" | custom-call | flops 1024 | bytes 1024 | tf_op jit(solution)/shard_map/inner_backward/pallas_call | solution.py:581
  993.8 19.2 spread.12
  1014.8 35.2 %collective-permute-done.36.refs_3_ = bf16[384,2048]{1,0:T(8,128)(2,1)S(1)} collective-permute-done((bf16[384,2048]{1,0:T(8,128)(2,1)S(1)}, bf16[384,2048]{1,0:T(8,128)(2,1)S(1)}, u32[]{:S(2)}, u32[]{:S(2)}) %collective-permute-start.36) | collective-permute-done | bytes 1572896 | tf_op jit(solution)/shard_map/ppermute | solution.py:682
  1050.0 19.7 spread.13
  1070.9 20.8 %weight_gradient.7 = bf16[1024,2048]{1,0:T(8,128)(2,1)} custom-call(bf16[384,2048]{1,0:T(8,128)(2,1)S(1)} %collective-permute-done.35.refs_0_, bf16[384,2048]{1,0:T(8,128)(2,1)} %copy-done.84, bf16[384,2048]{1,0:T(8,128)(2,1)} %copy-done.72, bf16[384,2048]{1,0:T(8,128)(2,1)} %copy-done.83, bf16[384,2048]{1,0:T(8,128)(2,1)} %copy-done.13, ...), custom_call_target="tpu_custom_call" | custom-call | flops 1024 | bytes 1024 | tf_op jit(solution)/shard_map/weight_gradient/pallas_call | solution.py:617
  1092.6 25.1 %inner_backward.3 = (bf16[1536,2048]{1,0:T(8,128)(2,1)}, bf16[1536,2048]{1,0:T(8,128)(2,1)}) custom-call(bf16[384,2048]{1,0:T(8,128)(2,1)S(1)} %collective-permute-done.35.refs_0_, bf16[384,2048]{1,0:T(8,128)(2,1)} %copy-done.84, bf16[384,2048]{1,0:T(8,128)(2,1)} %copy-done.72, bf16[384,2048]{1,0:T(8,128)(2,1)} %copy-done.83, ...), custom_call_target="tpu_custom_call" | custom-call | flops 1024 | bytes 1024 | tf_op jit(solution)/shard_map/inner_backward/pallas_call | solution.py:581
  1117.7 19.2 spread.14
  1136.8 19.3 spread.15
  1156.1 21.8 %weight_gradient.8 = bf16[1024,2048]{1,0:T(8,128)(2,1)} custom-call(bf16[384,2048]{1,0:T(8,128)(2,1)S(1)} %collective-permute-done.19.refs_0_, bf16[384,2048]{1,0:T(8,128)(2,1)} %copy-done.66, bf16[384,2048]{1,0:T(8,128)(2,1)} %copy-done.64, bf16[384,2048]{1,0:T(8,128)(2,1)} %copy-done.65, bf16[384,2048]{1,0:T(8,128)(2,1)} %copy-done.8, ...), custom_call_target="tpu_custom_call" | custom-call | flops 1024 | bytes 1024 | tf_op jit(solution)/shard_map/weight_gradient/pallas_call | solution.py:617
  1178.0 21.0 %weight_gradient.9 = bf16[1024,2048]{1,0:T(8,128)(2,1)} custom-call(bf16[384,2048]{1,0:T(8,128)(2,1)S(1)} %collective-permute-done.35.refs_0_, bf16[384,2048]{1,0:T(8,128)(2,1)} %copy-done.84, bf16[384,2048]{1,0:T(8,128)(2,1)} %copy-done.72, bf16[384,2048]{1,0:T(8,128)(2,1)} %copy-done.83, bf16[384,2048]{1,0:T(8,128)(2,1)} %copy-done.13, ...), custom_call_target="tpu_custom_call" | custom-call | flops 1024 | bytes 1024 | tf_op jit(solution)/shard_map/weight_gradient/pallas_call | solution.py:617
  1210.8 34.2 %collective-permute-done.44 = bf16[2,1,384,1024]{3,2,0,1:T(8,128)(2,1)} collective-permute-done((bf16[2,1,384,1024]{3,2,0,1:T(8,128)(2,1)S(1)}, bf16[2,1,384,1024]{3,2,0,1:T(8,128)(2,1)}, u32[]{:S(2)}, u32[]{:S(2)}) %collective-permute-start.44) | collective-permute-done | bytes 1572896 | tf_op jit(solution)/shard_map/ppermute | solution.py:682
  1260.4 20.7 %weight_gradient.10 = bf16[1024,2048]{1,0:T(8,128)(2,1)} custom-call(bf16[384,2048]{1,0:T(8,128)(2,1)S(1)} %collective-permute-done.19.refs_0_, bf16[384,2048]{1,0:T(8,128)(2,1)} %copy-done.66, bf16[384,2048]{1,0:T(8,128)(2,1)} %copy-done.64, bf16[384,2048]{1,0:T(8,128)(2,1)} %copy-done.65, bf16[384,2048]{1,0:T(8,128)(2,1)} %copy-done.8, ...), custom_call_target="tpu_custom_call" | custom-call | flops 1024 | bytes 1024 | tf_op jit(solution)/shard_map/weight_gradient/pallas_call | solution.py:617
  1285.4 34.5 %collective-permute-done.45 = bf16[2,1,384,1024]{3,2,0,1:T(8,128)(2,1)S(1)} collective-permute-done((bf16[2,1,384,1024]{3,2,0,1:T(8,128)(2,1)S(1)}, bf16[2,1,384,1024]{3,2,0,1:T(8,128)(2,1)S(1)}, u32[]{:S(2)}, u32[]{:S(2)}) %collective-permute-start.45) | collective-permute-done | bytes 1572896 | tf_op jit(solution)/shard_map/ppermute | solution.py:682
  1336.3 21.4 %weight_gradient.11 = bf16[1024,2048]{1,0:T(8,128)(2,1)} custom-call(bf16[384,2048]{1,0:T(8,128)(2,1)S(1)} %collective-permute-done.19.refs_0_, bf16[384,2048]{1,0:T(8,128)(2,1)} %copy-done.66, bf16[384,2048]{1,0:T(8,128)(2,1)} %copy-done.64, bf16[384,2048]{1,0:T(8,128)(2,1)} %copy-done.65, bf16[384,2048]{1,0:T(8,128)(2,1)} %copy-done.8, ...), custom_call_target="tpu_custom_call" | custom-call | flops 1024 | bytes 1024 | tf_op jit(solution)/shard_map/weight_gradient/pallas_call | solution.py:617
  1373.5 16.7 collective-permute-done.49
  1390.2 55.0 %collective-permute-done.48 = bf16[384,512]{1,0:T(8,128)(2,1)} collective-permute-done((bf16[384,512]{1,0:T(8,128)(2,1)}, bf16[384,512]{1,0:T(8,128)(2,1)}, u32[]{:S(2)}, u32[]{:S(2)}) %collective-permute-start.48) | collective-permute-done | bytes 393248 | tf_op jit(solution)/shard_map/ppermute | solution.py:682
  1447.9 21.2 %weight_gradient.12 = bf16[1024,2048]{1,0:T(8,128)(2,1)} custom-call(bf16[384,2048]{1,0:T(8,128)(2,1)S(1)} %collective-permute-done.19.refs_0_, bf16[384,2048]{1,0:T(8,128)(2,1)} %copy-done.66, bf16[384,2048]{1,0:T(8,128)(2,1)} %copy-done.64, bf16[384,2048]{1,0:T(8,128)(2,1)} %copy-done.65, bf16[384,2048]{1,0:T(8,128)(2,1)} %copy-done.8, ...), custom_call_target="tpu_custom_call" | custom-call | flops 1024 | bytes 1024 | tf_op jit(solution)/shard_map/weight_gradient/pallas_call | solution.py:617
  1469.1 11.6 out_weight.1
  1518.1 13.0 fusion.43
  1533.6 61.7 %attend_backward.2 = (f32[1536,512]{1,0:T(8,128)}, f32[3072,512]{1,0:T(8,128)}, f32[3072,512]{1,0:T(8,128)}) custom-call(s32[4]{0:T(128)S(1)} %get-tuple-element.237.spots_ref, bf16[1536,512]{1,0:T(8,128)(2,1)S(1)} %copy-done.39, bf16[1536,512]{1,0:T(8,128)(2,1)S(1)} %copy-done.36, bf16[1536,512]{1,0:T(8,128)(2,1)S(1)} %copy-done.35, ...), custom_call_target="tpu_custom_call" | custom-call | flops 1024 | bytes 1024 | tf_op jit(solution)/shard_map/attend_backward/pallas_call | solution.py:375
  1633.4 14.5 convolution_convert_fusion.1
  1655.1 29.3 %attend_backward.3 = (f32[1536,512]{1,0:T(8,128)}, f32[1536,512]{1,0:T(8,128)}, f32[1536,512]{1,0:T(8,128)}) custom-call(s32[4]{0:T(128)S(1)} %copy-done.56, bf16[1536,512]{1,0:T(8,128)(2,1)S(1)} %copy-done.31, bf16[1536,512]{1,0:T(8,128)(2,1)S(1)} %copy-done.37, bf16[1536,512]{1,0:T(8,128)(2,1)S(1)} %copy-done.33, ...), custom_call_target="tpu_custom_call" | custom-call | flops 1024 | bytes 1024 | tf_op jit(solution)/shard_map/attend_backward/pallas_call | solution.py:375
  1723.2 14.2 convolution_convert_fusion
  1757.6 32.1 %weight_gradient.13 = bf16[2048,1536]{1,0:T(8,128)(2,1)} custom-call(bf16[1536,2048]{1,0:T(8,128)(2,1)} %bitcast.446, bf16[1536,2048]{1,0:T(8,128)(2,1)} %bitcast.447, bf16[1536,1536]{1,0:T(8,128)(2,1)} %pad_maximum_fusion.3.refs_2_, bf16[1536,1536]{1,0:T(8,128)(2,1)} %pad_maximum_fusion.2.refs_3_), custom_call_target="tpu_custom_call" | custom-call | flops 1024 | bytes 1024 | tf_op jit(solution)/shard_map/weight_gradient/pallas_call | solution.py:617
  1806.2 18.5 collective-permute-done.80
  1829.5 12.0 collective-permute-done.67
  1842.5 30.6 %collective-permute-done.68 = bf16[1,64,2048]{2,1,0:T(8,128)(2,1)S(1)} collective-permute-done((bf16[1,64,2048]{2,1,0:T(8,128)(2,1)S(1)}, bf16[1,64,2048]{2,1,0:T(8,128)(2,1)S(1)}, u32[]{:S(2)}, u32[]{:S(2)}) %collective-permute-start.68) | collective-permute-done | bytes 262176 | tf_op jit(solution)/shard_map/ppermute | solution.py:682
  1893.5 35.6 %collective-permute-done.73 = bf16[64,2048]{1,0:T(8,128)(2,1)S(1)} collective-permute-done((bf16[64,2048]{1,0:T(8,128)(2,1)S(1)}, bf16[64,2048]{1,0:T(8,128)(2,1)S(1)}, u32[]{:S(2)}, u32[]{:S(2)}) %collective-permute-start.73) | collective-permute-done | bytes 262176 | tf_op jit(solution)/shard_map/ppermute | solution.py:682
  1956.8 18.6 update.3
  (660 shorter events, 608.7 us)
Async XLA Ops:
  7.2 243.7 %all-gather.12.cloned.1.call-start = ((), (), s32[]{:S(2)}) async-start(), calls=%async_computation.13 | async-start | bytes 15728640 | tf_op jit(solution)/shard_map/all_gather | solution.py:825
  7.9 327.8 %all-gather.6.cloned.1.call-start = ((), (), s32[]{:S(2)}) async-start(), calls=%async_computation.5 | async-start | bytes 5242880 | tf_op jit(solution)/shard_map/all_gather | solution.py:822
  38.3 132.9 %collective-permute-start.6 = (bf16[3,64,2048]{2,1,0:T(8,128)(2,1)}, bf16[3,64,2048]{2,1,0:T(8,128)(2,1)}, u32[]{:S(2)}, u32[]{:S(2)}) collective-permute-start(bf16[3,64,2048]{2,1,0:T(8,128)(2,1)} %bitcast.415), channel_id=1, source_target_pairs={{0,1},{1,0},{2,3},{3,2},{4,5},{5,4},{6,7},{7,6},{8,9},{9,8},{10,11... | collective-permute-start | bytes 2359304 | tf_op jit(solution)/shard_map/ppermute | solution.py:682
  39.6 133.7 %collective-permute-start.7 = (bf16[3,64,2048]{2,1,0:T(8,128)(2,1)}, bf16[3,64,2048]{2,1,0:T(8,128)(2,1)}, u32[]{:S(2)}, u32[]{:S(2)}) collective-permute-start(bf16[3,64,2048]{2,1,0:T(8,128)(2,1)} %bitcast.414), channel_id=1, source_target_pairs={{0,2},{1,3},{2,0},{3,1},{4,6},{5,7},{6,4},{7,5},{8,10},{9,11},{10,... | collective-permute-start | bytes 2359304 | tf_op jit(solution)/shard_map/ppermute | solution.py:682
  42.8 132.6 %collective-permute-start.8 = (bf16[3,64,2048]{2,1,0:T(8,128)(2,1)}, bf16[3,64,2048]{2,1,0:T(8,128)(2,1)}, u32[]{:S(2)}, u32[]{:S(2)}) collective-permute-start(bf16[3,64,2048]{2,1,0:T(8,128)(2,1)} %bitcast.413), channel_id=1, source_target_pairs={{0,3},{1,2},{2,1},{3,0},{4,7},{5,6},{6,5},{7,4},{8,11},{9,10},{10,... | collective-permute-start | bytes 2359304 | tf_op jit(solution)/shard_map/ppermute | solution.py:682
  66.8 43.6 %collective-permute-start.4 = (bf16[1,2,4,64,1536]{4,3,2,1,0:T(8,128)(2,1)S(1)}, bf16[1,2,4,64,1536]{4,3,2,1,0:T(8,128)(2,1)}, u32[]{:S(2)}, u32[]{:S(2)}) collective-permute-start(bf16[1,2,4,64,1536]{4,3,2,1,0:T(8,128)(2,1)S(1)} %pad_maximum_fusion.7), channel_id=1, source_target_pairs={{0,2},{1,3},{2,0},{3,1},{4,6},{5,7},{6,4},{7,5},{8,10},{9,11},{10,... | collective-permute-start | bytes 4718600 | tf_op jit(solution)/shard_map/ppermute | solution.py:682
  109.7 58.7 %collective-permute-start.10 = (bf16[2,64,2048]{2,1,0:T(8,128)(2,1)}, bf16[2,64,2048]{2,1,0:T(8,128)(2,1)}, u32[]{:S(2)}, u32[]{:S(2)}) collective-permute-start(bf16[2,64,2048]{2,1,0:T(8,128)(2,1)} %maximum_bitcast_fusion.4), channel_id=1, source_target_pairs={{0,4},{4,0},{8,12},{12,8},{1,5},{5,1},{9,13},{13,9},{2,6},{6,2},{1... | collective-permute-start | bytes 1572872 | tf_op jit(solution)/shard_map/ppermute | solution.py:682
  114.5 71.7 %collective-permute-start.5 = (bf16[2,2,4,64,1536]{4,3,2,1,0:T(8,128)(2,1)}, bf16[2,2,4,64,1536]{4,3,2,1,0:T(8,128)(2,1)}, u32[]{:S(2)}, u32[]{:S(2)}) collective-permute-start(bf16[2,2,4,64,1536]{4,3,2,1,0:T(8,128)(2,1)} %maximum_bitcast_fusion.1), channel_id=1, source_target_pairs={{0,1},{1,0},{2,3},{3,2},{4,5},{5,4},{6,7},{7,6},{8,9},{9,8},{10,11... | collective-permute-start | bytes 9437192 | tf_op jit(solution)/shard_map/ppermute | solution.py:682
  254.5 210.5 %all-gather.8.cloned.1.call-start = ((), (), s32[]{:S(2)}) async-start(), calls=%async_computation.6 | async-start | bytes 5242880 | tf_op jit(solution)/shard_map/all_gather | solution.py:822
  335.7 298.3 %all-gather.10.cloned.1.call-start = ((), (), s32[]{:S(2)}) async-start(), calls=%async_computation.7 | async-start | bytes 5242880 | tf_op jit(solution)/shard_map/all_gather | solution.py:822
  385.1 44.5 %collective-permute-start.17 = (bf16[1,2,4,64,2048]{4,3,2,1,0:T(8,128)(2,1)}, bf16[1,2,4,64,2048]{4,3,2,1,0:T(8,128)(2,1)}, u32[]{:S(2)}, u32[]{:S(2)}) collective-permute-start(bf16[1,2,4,64,2048]{4,3,2,1,0:T(8,128)(2,1)} %bitcast.461), channel_id=1, source_target_pairs={{0,2},{1,3},{2,0},{3,1},{4,6},{5,7},{6,4},{7,5},{8,10},{9,11},{10,... | collective-permute-start | bytes 6291464 | tf_op jit(solution)/shard_map/ppermute | solution.py:682
  435.4 153.2 %collective-permute-start.18 = (bf16[2,2,4,64,2048]{4,3,2,1,0:T(8,128)(2,1)}, bf16[2,2,4,64,2048]{4,3,2,1,0:T(8,128)(2,1)}, u32[]{:S(2)}, u32[]{:S(2)}) collective-permute-start(bf16[2,2,4,64,2048]{4,3,2,1,0:T(8,128)(2,1)} %maximum_bitcast_fusion), channel_id=1, source_target_pairs={{0,1},{1,0},{2,3},{3,2},{4,5},{5,4},{6,7},{7,6},{8,9},{9,8},{10,11... | collective-permute-start | bytes 12582920 | tf_op jit(solution)/shard_map/ppermute | solution.py:682
  465.0 1359.9 %reduce-scatter.14.cloned.1.call-start = ((), (), s32[]{:S(2)}) async-start(), calls=%async_computation.12 | async-start | bytes 5242880 | tf_op jit(solution)/shard_map/reduce_scatter | solution.py:961
  465.1 173.7 %collective-permute-start.22 = (bf16[1024,2048]{1,0:T(8,128)(2,1)}, bf16[1024,2048]{1,0:T(8,128)(2,1)}, u32[]{:S(2)}, u32[]{:S(2)}) collective-permute-start(bf16[1024,2048]{1,0:T(8,128)(2,1)} %all-gather.6.cloned.1.call-done.refs_4_.refs_2_), channel_id=1, source_target_pairs={{0,16},{16,0},{1,17},{17,1},{2,18},{18,2},{3,19},{19,3},{4,20},{20... | collective-permute-start | bytes 12582920 | tf_op jit(solution)/shard_map/ppermute | solution.py:682
  471.7 65.2 %collective-permute-start.15 = (bf16[384,512]{1,0:T(8,128)(2,1)S(1)}, bf16[384,512]{1,0:T(8,128)(2,1)S(1)}, u32[]{:S(2)}, u32[]{:S(2)}) collective-permute-start(bf16[384,512]{1,0:T(8,128)(2,1)S(1)} %get-tuple-element.301), channel_id=1, source_target_pairs={{0,8},{4,12},{8,0},{12,4},{1,9},{5,13},{9,1},{13,5},{2,10},{6,14},... | collective-permute-start | bytes 1179656 | tf_op jit(solution)/shard_map/ppermute | solution.py:682
  471.7 65.2 %collective-permute-start.14 = (bf16[384,512]{1,0:T(8,128)(2,1)S(1)}, bf16[384,512]{1,0:T(8,128)(2,1)S(1)}, u32[]{:S(2)}, u32[]{:S(2)}) collective-permute-start(bf16[384,512]{1,0:T(8,128)(2,1)S(1)} %get-tuple-element.302), channel_id=1, source_target_pairs={{0,4},{4,0},{8,12},{12,8},{1,5},{5,1},{9,13},{13,9},{2,6},{6,2},{1... | collective-permute-start | bytes 1179656 | tf_op jit(solution)/shard_map/ppermute | solution.py:682
  584.2 49.8 %collective-permute-start.29 = (bf16[384,512]{1,0:T(8,128)(2,1)S(1)}, bf16[384,512]{1,0:T(8,128)(2,1)S(1)}, u32[]{:S(2)}, u32[]{:S(2)}) collective-permute-start(bf16[384,512]{1,0:T(8,128)(2,1)S(1)} %get-tuple-element.304), channel_id=1, source_target_pairs={{0,12},{4,8},{8,4},{12,0},{1,13},{5,9},{9,5},{13,1},{2,14},{6,10},... | collective-permute-start | bytes 1179656 | tf_op jit(solution)/shard_map/ppermute | solution.py:682
  586.3 49.4 %collective-permute-start.28 = (bf16[384,512]{1,0:T(8,128)(2,1)}, bf16[384,512]{1,0:T(8,128)(2,1)}, u32[]{:S(2)}, u32[]{:S(2)}) collective-permute-start(bf16[384,512]{1,0:T(8,128)(2,1)} %get-tuple-element.305), channel_id=1, source_target_pairs={{0,8},{4,12},{8,0},{12,4},{1,9},{5,13},{9,1},{13,5},{2,10},{6,14},... | collective-permute-start | bytes 1179656 | tf_op jit(solution)/shard_map/ppermute | solution.py:682
  586.3 49.5 %collective-permute-start.27 = (bf16[384,512]{1,0:T(8,128)(2,1)}, bf16[384,512]{1,0:T(8,128)(2,1)}, u32[]{:S(2)}, u32[]{:S(2)}) collective-permute-start(bf16[384,512]{1,0:T(8,128)(2,1)} %get-tuple-element.306), channel_id=1, source_target_pairs={{0,4},{4,0},{8,12},{12,8},{1,5},{5,1},{9,13},{13,9},{2,6},{6,2},{1... | collective-permute-start | bytes 1179656 | tf_op jit(solution)/shard_map/ppermute | solution.py:682
  588.6 119.0 %collective-permute-start.23 = (bf16[1024,2048]{1,0:T(8,128)(2,1)}, bf16[1024,2048]{1,0:T(8,128)(2,1)}, u32[]{:S(2)}, u32[]{:S(2)}) collective-permute-start(bf16[1024,2048]{1,0:T(8,128)(2,1)} %all-gather.8.cloned.1.call-done.refs_6_.refs_4_), channel_id=1, source_target_pairs={{0,16},{16,0},{1,17},{17,1},{2,18},{18,2},{3,19},{19,3},{4,20},{20... | collective-permute-start | bytes 12582920 | tf_op jit(solution)/shard_map/ppermute | solution.py:682
  634.1 135.3 %collective-permute-start.24 = (bf16[1024,2048]{1,0:T(8,128)(2,1)}, bf16[1024,2048]{1,0:T(8,128)(2,1)S(1)}, u32[]{:S(2)}, u32[]{:S(2)}) collective-permute-start(bf16[1024,2048]{1,0:T(8,128)(2,1)} %all-gather.10.cloned.1.call-done.refs_1_.refs_6_), channel_id=1, source_target_pairs={{0,16},{16,0},{1,17},{17,1},{2,18},{18,2},{3,19},{19,3},{4,20},{20... | collective-permute-start | bytes 12582920 | tf_op jit(solution)/shard_map/ppermute | solution.py:682
  654.0 52.4 %collective-permute-start.31 = (bf16[384,2048]{1,0:T(8,128)(2,1)}, bf16[384,2048]{1,0:T(8,128)(2,1)}, u32[]{:S(2)}, u32[]{:S(2)}) collective-permute-start(bf16[384,2048]{1,0:T(8,128)(2,1)} %pad_maximum_fusion.11.refs_2_.refs_6_), channel_id=1, source_target_pairs={{0,2},{1,3},{2,0},{3,1},{4,6},{5,7},{6,4},{7,5},{8,10},{9,11},{10,... | collective-permute-start | bytes 4718600 | tf_op jit(solution)/shard_map/ppermute | solution.py:682
  674.2 107.9 %collective-permute-start.30 = (bf16[384,2048]{1,0:T(8,128)(2,1)}, bf16[384,2048]{1,0:T(8,128)(2,1)S(1)}, u32[]{:S(2)}, u32[]{:S(2)}) collective-permute-start(bf16[384,2048]{1,0:T(8,128)(2,1)} %pad_maximum_fusion.11.refs_2_.refs_6_), channel_id=1, source_target_pairs={{0,1},{1,0},{2,3},{3,2},{4,5},{5,4},{6,7},{7,6},{8,9},{9,8},{10,11... | collective-permute-start | bytes 4718600 | tf_op jit(solution)/shard_map/ppermute | solution.py:682
  706.4 75.7 %collective-permute-start.32 = (bf16[384,2048]{1,0:T(8,128)(2,1)}, bf16[384,2048]{1,0:T(8,128)(2,1)S(1)}, u32[]{:S(2)}, u32[]{:S(2)}) collective-permute-start(bf16[384,2048]{1,0:T(8,128)(2,1)} %collective-permute-done.31.refs_3_.refs_7_), channel_id=1, source_target_pairs={{0,1},{1,0},{2,3},{3,2},{4,5},{5,4},{6,7},{7,6},{8,9},{9,8},{10,11... | collective-permute-start | bytes 4718600 | tf_op jit(solution)/shard_map/ppermute | solution.py:682
  782.1 60.8 %collective-permute-start.25 = (bf16[2,768,1024]{2,1,0:T(8,128)(2,1)}, bf16[2,768,1024]{2,1,0:T(8,128)(2,1)S(1)}, u32[]{:S(2)}, u32[]{:S(2)}) collective-permute-start(bf16[2,768,1024]{2,1,0:T(8,128)(2,1)} %spread.8), channel_id=1, source_target_pairs={{0,1},{1,0},{2,3},{3,2},{4,5},{5,4},{6,7},{7,6},{8,9},{9,8},{10,11... | collective-permute-start | bytes 9437192 | tf_op jit(solution)/shard_map/ppermute | solution.py:682
  861.2 55.0 %collective-permute-start.34 = (bf16[2,1,384,1024]{3,2,0,1:T(8,128)(2,1)S(1)}, bf16[2,1,384,1024]{3,2,0,1:T(8,128)(2,1)S(1)}, u32[]{:S(2)}, u32[]{:S(2)}) collective-permute-start(bf16[2,1,384,1024]{3,2,0,1:T(8,128)(2,1)S(1)} %fusion.23), channel_id=1, source_target_pairs={{0,2},{1,3},{2,0},{3,1},{4,6},{5,7},{6,4},{7,5},{8,10},{9,11},{10,... | collective-permute-start | bytes 4718600 | tf_op jit(solution)/shard_map/ppermute | solution.py:682
  1013.0 56.7 %collective-permute-start.41 = (bf16[2,768,1024]{2,1,0:T(8,128)(2,1)}, bf16[2,768,1024]{2,1,0:T(8,128)(2,1)}, u32[]{:S(2)}, u32[]{:S(2)}) collective-permute-start(bf16[2,768,1024]{2,1,0:T(8,128)(2,1)} %spread.12), channel_id=1, source_target_pairs={{0,1},{1,0},{2,3},{3,2},{4,5},{5,4},{6,7},{7,6},{8,9},{9,8},{10,11... | collective-permute-start | bytes 9437192 | tf_op jit(solution)/shard_map/ppermute | solution.py:682
  1014.7 54.9 %collective-permute-start.35 = (bf16[384,2048]{1,0:T(8,128)(2,1)S(1)}, bf16[384,2048]{1,0:T(8,128)(2,1)S(1)}, u32[]{:S(2)}, u32[]{:S(2)}) collective-permute-start(bf16[384,2048]{1,0:T(8,128)(2,1)S(1)} %pad_maximum_fusion.12.refs_2_), channel_id=1, source_target_pairs={{0,1},{1,0},{2,3},{3,2},{4,5},{5,4},{6,7},{7,6},{8,9},{9,8},{10,11... | collective-permute-start | bytes 4718600 | tf_op jit(solution)/shard_map/ppermute | solution.py:682
  1091.7 107.3 %collective-permute-start.43 = (bf16[1024,2048]{1,0:T(8,128)(2,1)}, bf16[1024,2048]{1,0:T(8,128)(2,1)S(1)}, u32[]{:S(2)}, u32[]{:S(2)}) collective-permute-start(bf16[1024,2048]{1,0:T(8,128)(2,1)} %weight_gradient.7), channel_id=1, source_target_pairs={{0,16},{16,0},{1,17},{17,1},{2,18},{18,2},{3,19},{19,3},{4,20},{20... | collective-permute-start | bytes 12582920 | tf_op jit(solution)/shard_map/ppermute | solution.py:682
  1209.7 663.5 %reduce-scatter.10.cloned.1.call-start = ((), (), s32[]{:S(2)}) async-start(), calls=%async_computation.10 | async-start | bytes 5242880 | tf_op jit(solution)/shard_map/reduce_scatter | solution.py:961
  1209.7 147.9 %collective-permute-start.46 = (bf16[1024,2048]{1,0:T(8,128)(2,1)}, bf16[1024,2048]{1,0:T(8,128)(2,1)}, u32[]{:S(2)}, u32[]{:S(2)}) collective-permute-start(bf16[1024,2048]{1,0:T(8,128)(2,1)} %weight_gradient.8), channel_id=1, source_target_pairs={{0,16},{16,0},{1,17},{17,1},{2,18},{18,2},{3,19},{19,3},{4,20},{20... | collective-permute-start | bytes 12582920 | tf_op jit(solution)/shard_map/ppermute | solution.py:682
  1365.4 519.6 %reduce-scatter.12.cloned.1.call-start = ((), (), s32[]{:S(2)}) async-start(), calls=%async_computation.11 | async-start | bytes 5242880 | tf_op jit(solution)/shard_map/reduce_scatter | solution.py:961
  1368.4 76.9 %collective-permute-start.48 = (bf16[384,512]{1,0:T(8,128)(2,1)}, bf16[384,512]{1,0:T(8,128)(2,1)}, u32[]{:S(2)}, u32[]{:S(2)}) collective-permute-start(bf16[384,512]{1,0:T(8,128)(2,1)} %get-tuple-element.289), channel_id=1, source_target_pairs={{0,8},{4,12},{8,0},{12,4},{1,9},{5,13},{9,1},{13,5},{2,10},{6,14},... | collective-permute-start | bytes 1179656 | tf_op jit(solution)/shard_map/ppermute | solution.py:682
  1369.7 75.5 %collective-permute-start.47 = (bf16[384,512]{1,0:T(8,128)(2,1)}, bf16[384,512]{1,0:T(8,128)(2,1)}, u32[]{:S(2)}, u32[]{:S(2)}) collective-permute-start(bf16[384,512]{1,0:T(8,128)(2,1)} %get-tuple-element.290), channel_id=1, source_target_pairs={{0,4},{4,0},{8,12},{12,8},{1,5},{5,1},{9,13},{13,9},{2,6},{6,2},{1... | collective-permute-start | bytes 1179656 | tf_op jit(solution)/shard_map/ppermute | solution.py:682
  1372.3 124.8 %collective-permute-start.52 = (bf16[1024,2048]{1,0:T(8,128)(2,1)}, bf16[1024,2048]{1,0:T(8,128)(2,1)}, u32[]{:S(2)}, u32[]{:S(2)}) collective-permute-start(bf16[1024,2048]{1,0:T(8,128)(2,1)} %weight_gradient.10), channel_id=1, source_target_pairs={{0,16},{16,0},{1,17},{17,1},{2,18},{18,2},{3,19},{19,3},{4,20},{20... | collective-permute-start | bytes 12582920 | tf_op jit(solution)/shard_map/ppermute | solution.py:682
  1505.0 479.6 %reduce-scatter.8.cloned.1.call-start = ((), (), s32[]{:S(2)}) async-start(), calls=%async_computation.9 | async-start | bytes 7864320 | tf_op jit(solution)/shard_map/reduce_scatter | solution.py:998
  1511.2 86.6 %collective-permute-start.51 = (bf16[1,2,4,64,2048]{4,3,2,1,0:T(8,128)(2,1)S(1)}, bf16[1,2,4,64,2048]{4,3,2,1,0:T(8,128)(2,1)S(1)}, u32[]{:S(2)}, u32[]{:S(2)}) collective-permute-start(bf16[1,2,4,64,2048]{4,3,2,1,0:T(8,128)(2,1)S(1)} %constant_dynamic-slice_fusion.3), channel_id=1, source_target_pairs={{0,2},{1,3},{2,0},{3,1},{4,6},{5,7},{6,4},{7,5},{8,10},{9,11},{10,... | collective-permute-start | bytes 6291464 | tf_op jit(solution)/shard_map/ppermute | solution.py:682
  1513.7 81.6 %collective-permute-start.55 = (bf16[384,512]{1,0:T(8,128)(2,1)}, bf16[384,512]{1,0:T(8,128)(2,1)S(1)}, u32[]{:S(2)}, u32[]{:S(2)}) collective-permute-start(bf16[384,512]{1,0:T(8,128)(2,1)} %get-tuple-element.284), channel_id=1, source_target_pairs={{0,12},{4,8},{8,4},{12,0},{1,13},{5,9},{9,5},{13,1},{2,14},{6,10},... | collective-permute-start | bytes 1179656 | tf_op jit(solution)/shard_map/ppermute | solution.py:682
  1513.7 81.6 %collective-permute-start.54 = (bf16[384,512]{1,0:T(8,128)(2,1)S(1)}, bf16[384,512]{1,0:T(8,128)(2,1)}, u32[]{:S(2)}, u32[]{:S(2)}) collective-permute-start(bf16[384,512]{1,0:T(8,128)(2,1)S(1)} %get-tuple-element.285), channel_id=1, source_target_pairs={{0,8},{4,12},{8,0},{12,4},{1,9},{5,13},{9,1},{13,5},{2,10},{6,14},... | collective-permute-start | bytes 1179656 | tf_op jit(solution)/shard_map/ppermute | solution.py:682
  1513.7 81.6 %collective-permute-start.53 = (bf16[384,512]{1,0:T(8,128)(2,1)S(1)}, bf16[384,512]{1,0:T(8,128)(2,1)}, u32[]{:S(2)}, u32[]{:S(2)}) collective-permute-start(bf16[384,512]{1,0:T(8,128)(2,1)S(1)} %get-tuple-element.286), channel_id=1, source_target_pairs={{0,4},{4,0},{8,12},{12,8},{1,5},{5,1},{9,13},{13,9},{2,6},{6,2},{1... | collective-permute-start | bytes 1179656 | tf_op jit(solution)/shard_map/ppermute | solution.py:682
  1650.9 336.8 %reduce-scatter.6.cloned.1.call-start = ((), (), s32[]{:S(2)}) async-start(), calls=%async_computation.8 | async-start | bytes 7864320 | tf_op jit(solution)/shard_map/reduce_scatter | solution.py:1029
  1747.0 50.8 %collective-permute-start.78 = (f32[4,2048]{1,0:T(4,128)S(1)}, f32[4,2048]{1,0:T(4,128)S(1)}, u32[]{:S(2)}, u32[]{:S(2)}) collective-permute-start(f32[4,2048]{1,0:T(4,128)S(1)} %pad_maximum_fusion.22), channel_id=1, source_target_pairs={{0,16},{16,0},{1,17},{17,1},{2,18},{18,2},{3,19},{19,3},{4,20},{20... | collective-permute-start | bytes 98312 | tf_op jit(solution)/shard_map/ppermute | solution.py:682
  1797.9 79.7 %collective-permute-start.61 = (bf16[2,2,4,64,1536]{4,3,2,1,0:T(8,128)(2,1)}, bf16[2,2,4,64,1536]{4,3,2,1,0:T(8,128)(2,1)}, u32[]{:S(2)}, u32[]{:S(2)}) collective-permute-start(bf16[2,2,4,64,1536]{4,3,2,1,0:T(8,128)(2,1)} %dynamic-slice_bitcast_fusion.1), channel_id=1, source_target_pairs={{0,1},{1,0},{2,3},{3,2},{4,5},{5,4},{6,7},{7,6},{8,9},{9,8},{10,11... | collective-permute-start | bytes 9437192 | tf_op jit(solution)/shard_map/ppermute | solution.py:682
  1798.0 43.5 %collective-permute-start.67 = (bf16[2,64,2048]{2,1,0:T(8,128)(2,1)S(1)}, bf16[2,64,2048]{2,1,0:T(8,128)(2,1)S(1)}, u32[]{:S(2)}, u32[]{:S(2)}) collective-permute-start(bf16[2,64,2048]{2,1,0:T(8,128)(2,1)S(1)} %dynamic-slice_bitcast_fusion.3), channel_id=1, source_target_pairs={{0,4},{4,0},{8,12},{12,8},{1,5},{5,1},{9,13},{13,9},{2,6},{6,2},{1... | collective-permute-start | bytes 1572872 | tf_op jit(solution)/shard_map/ppermute | solution.py:682
  1826.9 113.6 %collective-permute-start.75 = (bf16[64,2048]{1,0:T(8,128)(2,1)}, bf16[64,2048]{1,0:T(8,128)(2,1)}, u32[]{:S(2)}, u32[]{:S(2)}) collective-permute-start(bf16[64,2048]{1,0:T(8,128)(2,1)} %get-tuple-element.311), channel_id=1, source_target_pairs={{0,1},{1,0},{2,3},{3,2},{4,5},{5,4},{6,7},{7,6},{8,9},{9,8},{10,11... | collective-permute-start | bytes 786440 | tf_op jit(solution)/shard_map/ppermute | solution.py:682
  1827.4 114.2 %collective-permute-start.76 = (bf16[64,2048]{1,0:T(8,128)(2,1)}, bf16[64,2048]{1,0:T(8,128)(2,1)}, u32[]{:S(2)}, u32[]{:S(2)}) collective-permute-start(bf16[64,2048]{1,0:T(8,128)(2,1)} %get-tuple-element.310), channel_id=1, source_target_pairs={{0,2},{1,3},{2,0},{3,1},{4,6},{5,7},{6,4},{7,5},{8,10},{9,11},{10,... | collective-permute-start | bytes 786440 | tf_op jit(solution)/shard_map/ppermute | solution.py:682
  1883.4 46.2 %collective-permute-start.62 = (bf16[1,2,4,64,1536]{4,3,2,1,0:T(8,128)(2,1)}, bf16[1,2,4,64,1536]{4,3,2,1,0:T(8,128)(2,1)}, u32[]{:S(2)}, u32[]{:S(2)}) collective-permute-start(bf16[1,2,4,64,1536]{4,3,2,1,0:T(8,128)(2,1)} %constant_dynamic-slice_fusion.1), channel_id=1, source_target_pairs={{0,2},{1,3},{2,0},{3,1},{4,6},{5,7},{6,4},{7,5},{8,10},{9,11},{10,... | collective-permute-start | bytes 4718600 | tf_op jit(solution)/shard_map/ppermute | solution.py:682
  1892.7 64.0 %collective-permute-start.77 = (bf16[64,2048]{1,0:T(8,128)(2,1)}, bf16[64,2048]{1,0:T(8,128)(2,1)S(1)}, u32[]{:S(2)}, u32[]{:S(2)}) collective-permute-start(bf16[64,2048]{1,0:T(8,128)(2,1)} %get-tuple-element.309), channel_id=1, source_target_pairs={{0,3},{1,2},{2,1},{3,0},{4,7},{5,6},{6,5},{7,4},{8,11},{9,10},{10,... | collective-permute-start | bytes 786440 | tf_op jit(solution)/shard_map/ppermute | solution.py:682
  (184 other events, 3288.9 us)
Sparse Core Ops, SparseCore 0:
  9.6 241.2 all-gather.11
  254.6 81.0 all-gather.5
  337.9 80.2 all-gather.7
  465.1 106.1 all-gather.9
  1209.8 73.6 reduce-scatter.13
  1365.5 99.8 reduce-scatter.9
  1505.1 102.1 reduce-scatter.11
  1651.0 109.7 reduce-scatter.7
  1763.2 129.5 reduce-scatter.5

commit v2 on v1

--- a/solution.py
+++ b/solution.py
@@ -75,6 +75,49 @@
 
 
 brief = pl.CostEstimate(flops=1024, bytes_accessed=1024, transcendentals=0)
+
+
+class Tied:
+    def __init__(self, value, others):
+        self.value, self.others = value, []
+        for other in others:
+            self.others += [other.value] + other.others if isinstance(other, Tied) else [other]
+
+
+def after(value, *others):
+    if isinstance(value, Tied):
+        return Tied(value.value, [value] + list(others))
+    return Tied(value, others)
+
+
+def plain(value):
+    return value.value if isinstance(value, Tied) else value
+
+
+def untie(*values):
+    others = [o for v in values if isinstance(v, Tied) for o in v.others]
+    return [plain(v) for v in values], others
+
+
+def launch(kernel, scalars, others, grid, in_specs, out_specs, out_shape, scratch_shapes=(), **options):
+    skip = len(others)
+
+    def run(*refs):
+        kernel(*refs[:scalars], *refs[scalars + skip :])
+
+    call = pl.pallas_call(
+        run,
+        out_shape=out_shape,
+        grid_spec=pltpu.PrefetchScalarGridSpec(
+            num_scalar_prefetch=scalars,
+            grid=grid,
+            in_specs=[pl.BlockSpec(memory_space=pl.ANY)] * skip + list(in_specs),
+            out_specs=out_specs,
+            scratch_shapes=list(scratch_shapes),
+        ),
+        **options,
+    )
+    return lambda *operands: call(*operands[:scalars], *others, *operands[scalars:])
 
 
 def params(steps, mib):
@@ -208,6 +251,42 @@
     )(order, *grads, projected, projected, scales, gains, cosine, sine)
 
 
+def finish_kernel(weighted_ref, q_ref, k_ref, scale_ref, mean_ref, value_ref, out_ref):
+    width = q_ref.shape[1]
+    for which, pre in enumerate((q_ref, k_ref)):
+        at = slice(which * width, (which + 1) * width)
+        scale = scale_ref[:, which : which + 1]
+        unit = pre[...] * scale
+        inward = scale * (weighted_ref[:, at] - unit * mean_ref[:, which : which + 1])
+        out_ref[:, at] = inward.astype(low_type)
+    out_ref[:, 2 * width :] = value_ref[...]
+
+
+def finish(weighted, projected, scales, means, values, count, stream):
+    length, width = values.shape
+    block = length // count
+    scale = pl.BlockSpec((block, 2), lambda b: (2 * b + stream, 0))
+    return launch(
+        finish_kernel,
+        0,
+        [],
+        grid=(count,),
+        out_shape=jax.ShapeDtypeStruct((length, 3 * width), low_type),
+        in_specs=[
+            pl.BlockSpec((block, 2 * width), lambda b: (b, 0)),
+            pl.BlockSpec((block, width), lambda b: (2 * b + stream, 0)),
+            pl.BlockSpec((block, width), lambda b: (2 * b + stream, 1)),
+            scale,
+            pl.BlockSpec((block, 2), lambda b: (b, 0)),
+            pl.BlockSpec((block, width), lambda b: (b, 0)),
+        ],
+        out_specs=pl.BlockSpec((block, 3 * width), lambda b: (b, 0)),
+        compiler_params=params(1, 40),
+        cost_estimate=brief,
+        name="finish",
+    )(weighted, projected, projected, scales, means, values)
+
+
 def causal(tile):
     key = lax.broadcasted_iota(jnp.int32, (tile, tile), 0)
     query = lax.broadcasted_iota(jnp.int32, (tile, tile), 1)
@@ -266,28 +345,28 @@
 
 
 def attend_forward(queries, keys, values, spots):
+    (queries,), others = untie(queries)
     length, width = queries.shape
     heads, parts = width // HEAD, len(keys)
     tile = tile_of(length)
     whole = pl.BlockSpec((length, HEAD), lambda h, i, o: (0, h))
     piece = pl.BlockSpec((tile, HEAD), lambda h, i, o: (i, h))
-    return pl.pallas_call(
+    return launch(
         functools.partial(forward_kernel, tile, parts),
+        1,
+        others,
         out_shape=(
             jax.ShapeDtypeStruct((length, width), low_type),
             jax.ShapeDtypeStruct((heads, 1, length), jnp.float32),
         ),
-        grid_spec=pltpu.PrefetchScalarGridSpec(
-            num_scalar_prefetch=1,
-            grid=(heads, length // tile),
-            in_specs=[piece] + [whole] * (2 * parts),
-            out_specs=(whole, pl.BlockSpec((1, 1, tile), lambda h, i, o: (h, 0, i))),
-            scratch_shapes=[
-                pltpu.VMEM((parts * length, HEAD), low_type),
-                pltpu.VMEM((HEAD, parts * length), low_type),
-                pltpu.VMEM((length, HEAD), low_type),
-            ],
-        ),
+        grid=(heads, length // tile),
+        in_specs=[piece] + [whole] * (2 * parts),
+        out_specs=(whole, pl.BlockSpec((1, 1, tile), lambda h, i, o: (h, 0, i))),
+        scratch_shapes=[
+            pltpu.VMEM((parts * length, HEAD), low_type),
+            pltpu.VMEM((HEAD, parts * length), low_type),
+            pltpu.VMEM((length, HEAD), low_type),
+        ],
         compiler_params=params(2, 40),
         cost_estimate=brief,
         name="attend_forward",
@@ -366,37 +445,37 @@
 
 
 def attend_backward(queries, outward, attended, logs, keys, values, added, spots):
+    (queries,), others = untie(queries)
     length, width = queries.shape
     heads, parts = width // HEAD, len(keys)
     tile = tile_of(length)
     whole = pl.BlockSpec((length, HEAD), lambda h, j, o: (0, h))
     piece = pl.BlockSpec((tile, HEAD), lambda h, j, o: (j, h))
     total = parts * length
-    return pl.pallas_call(
+    return launch(
         functools.partial(backward_kernel, tile, parts, len(added)),
+        1,
+        others,
         out_shape=(
             jax.ShapeDtypeStruct((length, width), jnp.float32),
             jax.ShapeDtypeStruct((total, width), jnp.float32),
             jax.ShapeDtypeStruct((total, width), jnp.float32),
         ),
-        grid_spec=pltpu.PrefetchScalarGridSpec(
-            num_scalar_prefetch=1,
-            grid=(heads, total // tile),
-            in_specs=[whole] * 3
-            + [pl.BlockSpec((1, 1, length), lambda h, j, o: (h, 0, 0))]
-            + [whole] * (2 * parts)
-            + [piece] * len(added),
-            out_specs=(whole, piece, piece),
-            scratch_shapes=[
-                pltpu.VMEM((total, HEAD), low_type),
-                pltpu.VMEM((total, HEAD), low_type),
-                pltpu.VMEM((HEAD, total), low_type),
-                pltpu.VMEM((length, HEAD), low_type),
-                pltpu.VMEM((length, HEAD), low_type),
-                pltpu.VMEM((1, length), jnp.float32),
-                pltpu.VMEM((HEAD, length), jnp.float32),
-            ],
-        ),
+        grid=(heads, total // tile),
+        in_specs=[whole] * 3
+        + [pl.BlockSpec((1, 1, length), lambda h, j, o: (h, 0, 0))]
+        + [whole] * (2 * parts)
+        + [piece] * len(added),
+        out_specs=(whole, piece, piece),
+        scratch_shapes=[
+            pltpu.VMEM((total, HEAD), low_type),
+            pltpu.VMEM((total, HEAD), low_type),
+            pltpu.VMEM((HEAD, total), low_type),
+            pltpu.VMEM((length, HEAD), low_type),
+            pltpu.VMEM((length, HEAD), low_type),
+            pltpu.VMEM((1, length), jnp.float32),
+            pltpu.VMEM((HEAD, length), jnp.float32),
+        ],
         compiler_params=params(2, 48),
         cost_estimate=brief,
         name="attend_backward",
@@ -411,52 +490,79 @@
     out_ref[...] += product(x_ref[0], w_ref[...])
 
 
-def out_project(pieces, weight, others):
+def out_project(pieces, weight, spots):
+    (pieces,), others = untie(pieces)
     count, rows, depth = pieces.shape
     width = weight.shape[1]
     across = min(1024, width)
+    return launch(
+        out_kernel,
+        1,
+        others,
+        out_shape=jax.ShapeDtypeStruct((rows, width), jnp.float32),
+        grid=(width // across, count),
+        in_specs=[
+            pl.BlockSpec((1, rows, depth), lambda n, k, o: (k, 0, 0)),
+            pl.BlockSpec((depth, across), lambda n, k, o: (o[k], n)),
+        ],
+        out_specs=pl.BlockSpec((rows, across), lambda n, k, o: (0, n)),
+        compiler_params=params(2, 32),
+        cost_estimate=brief,
+        name="out_project",
+    )(spots, pieces, weight)
+
+
+def weave_kernel(odd_ref, own_ref, other_ref, out_ref):
+    odd = odd_ref[0]
+    for high in range(own_ref.shape[0]):
+        out_ref[0, 0, 2 * high + odd] = own_ref[high, 0, 0]
+        out_ref[0, 0, 2 * high + 1 - odd] = other_ref[high, 0, 0]
+
+
+def weave(own, other, odd):
+    half, dps, ctxs, rows, width = own.shape
+    piece = pl.BlockSpec((half, 1, 1, rows, width), lambda i, j, o: (0, i, j, 0, 0))
     return pl.pallas_call(
-        out_kernel,
-        out_shape=jax.ShapeDtypeStruct((rows, width), jnp.float32),
+        weave_kernel,
+        out_shape=jax.ShapeDtypeStruct((dps, ctxs, 2 * half, rows, width), own.dtype),
         grid_spec=pltpu.PrefetchScalarGridSpec(
             num_scalar_prefetch=1,
-            grid=(width // across, count),
-            in_specs=[
-                pl.BlockSpec((1, rows, depth), lambda n, k, o: (k, 0, 0)),
-                pl.BlockSpec((depth, across), lambda n, k, o: (o[k], n)),
-            ],
-            out_specs=pl.BlockSpec((rows, across), lambda n, k, o: (0, n)),
+            grid=(dps, ctxs),
+            in_specs=[piece, piece],
+            out_specs=pl.BlockSpec(
+                (1, 1, 2 * half, rows, width), lambda i, j, o: (i, j, 0, 0, 0)
+            ),
         ),
         compiler_params=params(2, 32),
         cost_estimate=brief,
-        name="out_project",
-    )(others, pieces, weight)
+        name="weave",
+    )(odd, own, other)
 
 
 def out_back_kernel(others_ref, x_ref, w_ref, out_ref):
     out_ref[0] = against(x_ref[...], w_ref[...]).astype(low_type)
 
 
-def out_back(grad, weight, others):
+def out_back(grad, weight, spots):
+    (grad,), others = untie(grad)
     rows, width = grad.shape
-    count = others.shape[0]
+    count = spots.shape[0]
     depth = weight.shape[0] // count
-    return pl.pallas_call(
+    return launch(
         out_back_kernel,
+        1,
+        others,
         out_shape=jax.ShapeDtypeStruct((count, rows, depth), low_type),
-        grid_spec=pltpu.PrefetchScalarGridSpec(
-            num_scalar_prefetch=1,
-            grid=(count,),
-            in_specs=[
-                pl.BlockSpec((rows, width), lambda k, o: (0, 0)),
-                pl.BlockSpec((depth, width), lambda k, o: (o[k], 0)),
-            ],
-            out_specs=pl.BlockSpec((1, rows, depth), lambda k, o: (k, 0, 0)),
-        ),
+        grid=(count,),
+        in_specs=[
+            pl.BlockSpec((rows, width), lambda k, o: (0, 0)),
+            pl.BlockSpec((depth, width), lambda k, o: (o[k], 0)),
+        ],
+        out_specs=pl.BlockSpec((1, rows, depth), lambda k, o: (k, 0, 0)),
         compiler_params=params(1, 32),
         cost_estimate=brief,
         name="out_back",
-    )(others, grad, weight)
+    )(spots, grad, weight)
 
 
 def out_weight_kernel(streams, others_ref, *refs):
@@ -467,24 +573,24 @@
     out_ref[...] = total.astype(low_type)
 
 
-def out_weight(lefts, rights, others):
+def out_weight(lefts, rights, spots):
+    lefts, others = untie(*lefts)
     count, rows, depth = lefts[0].shape
     width = rights[0].shape[1]
     across = min(1024, width)
-    return pl.pallas_call(
+    return launch(
         functools.partial(out_weight_kernel, len(lefts)),
+        1,
+        others,
         out_shape=jax.ShapeDtypeStruct((count * depth, width), low_type),
-        grid_spec=pltpu.PrefetchScalarGridSpec(
-            num_scalar_prefetch=1,
-            grid=(width // across, count),
-            in_specs=[pl.BlockSpec((1, rows, depth), lambda n, k, o: (k, 0, 0))] * len(lefts)
-            + [pl.BlockSpec((rows, across), lambda n, k, o: (0, n))] * len(rights),
-            out_specs=pl.BlockSpec((depth, across), lambda n, k, o: (o[k], n)),
-        ),
+        grid=(width // across, count),
+        in_specs=[pl.BlockSpec((1, rows, depth), lambda n, k, o: (k, 0, 0))] * len(lefts)
+        + [pl.BlockSpec((rows, across), lambda n, k, o: (0, n))] * len(rights),
+        out_specs=pl.BlockSpec((depth, across), lambda n, k, o: (o[k], n)),
         compiler_params=params(2, 32),
         cost_estimate=brief,
         name="out_weight",
-    )(others, *lefts, *rights)
+    )(spots, *lefts, *rights)
 
 
 def chosen(refs, index, use):
@@ -512,13 +618,16 @@
 
 
 def gate_up(pieces, gates, ups):
+    pieces, others = untie(*pieces)
     count, (rows, width) = len(pieces), pieces[0].shape
     parts, columns = len(gates), gates[0].shape[1]
     across = min(512, columns)
     weight = pl.BlockSpec((width // parts, across), lambda n, m: (0, n))
     out = pl.BlockSpec((rows, across), lambda n, m: (m, n))
-    return pl.pallas_call(
+    return launch(
         functools.partial(gate_up_kernel, count, parts),
+        0,
+        others,
         grid=(columns // across, count),
         out_shape=(jax.ShapeDtypeStruct((count * rows, columns), low_type),) * 3,
         in_specs=[pl.BlockSpec((rows, width), lambda n, m: (0, 0))] * count
@@ -540,11 +649,14 @@
 
 
 def spread(lefts, weights, half):
+    lefts, others = untie(*lefts)
     rows, columns = lefts[0].shape[0] // 2, lefts[0].shape[1]
     terms, parts, features = len(lefts), len(weights[0]), weights[0][0].shape[0]
     across = min(256, features)
-    return pl.pallas_call(
+    return launch(
         functools.partial(spread_kernel, terms, parts),
+        0,
+        others,
         grid=(features // across,),
         out_shape=jax.ShapeDtypeStruct((parts, rows, features), low_type),
         in_specs=[pl.BlockSpec((rows, columns), lambda n: (half, 0))] * terms
@@ -574,12 +686,15 @@
 
 
 def inner_backward(pieces, gate, up, downs):
+    (gate,), others = untie(gate)
     count, (rows, width) = len(pieces), pieces[0].shape
     parts, columns = len(downs), downs[0].shape[1]
     across = min(1024, columns)
     out = pl.BlockSpec((rows, across), lambda n, m: (m, n))
-    return pl.pallas_call(
+    return launch(
         functools.partial(inner_kernel, count, parts),
+        0,
+        others,
         grid=(columns // across, count),
         out_shape=(jax.ShapeDtypeStruct((count * rows, columns), low_type),) * 2,
         in_specs=[pl.BlockSpec((rows, width), lambda n, m: (0, 0))] * count
@@ -609,13 +724,17 @@
 
 
 def weight_gradient(lefts, rights, start, size):
+    lefts, others = [list(left) for left in lefts], untie(*[v for left in lefts for v in left])[1]
+    lefts = [[plain(v) for v in left] for left in lefts]
     each, rows = len(lefts[0]), lefts[0][0].shape[0]
     columns, count = rights[0].shape[1], len(lefts) * each
     tile = min(512, size)
     across = next(a for a in (1024, 768, 512, 384, 128) if columns % a == 0)
     first = start // tile
-    return pl.pallas_call(
+    return launch(
         functools.partial(weight_kernel, count, each),
+        0,
+        others,
         grid=(size // tile, columns // across),
         out_shape=jax.ShapeDtypeStruct((size, columns), low_type),
         in_specs=[pl.BlockSpec((rows, tile), lambda m, n: (0, first + m))] * count
@@ -701,10 +820,6 @@
     return [pieces[0]] + [swap(pieces[k], axis, k) for k in range(1, lax.axis_size(axis))]
 
 
-def after(value, *others):
-    return lax.optimization_barrier((value,) + others)[0]
-
-
 def total_of(value, axes):
     for axis in axes:
         bits = 1
@@ -714,10 +829,10 @@
     return value
 
 
-def gather_pairs(value, axis):
+def gather_pairs(value, axis, stop=0):
     size, me = lax.axis_size(axis), lax.axis_index(axis)
     bits, value = size // 2, value[None]
-    while bits:
+    while bits > stop:
         other = swap(value, axis, bits)
         low = (me & bits) == 0
         value = jnp.stack([jnp.where(low, value, other), jnp.where(low, other, value)], axis=1)
@@ -766,7 +881,11 @@
         pieces = pieces[:, :, 0].astype(jnp.float32) + got[:, :, 0].astype(jnp.float32)
         got = swap(send.astype(low), axis, bits)
         bits *= 2
-    return pieces[:, 0].astype(jnp.float32) + got[:, 0].astype(jnp.float32)
+    return pieces[:, 0], got[:, 0]
+
+
+def joined(terms):
+    return list(terms[0].astype(jnp.float32) + terms[1].astype(jnp.float32))
 
 
 def own_first(parts, axis):
@@ -817,31 +936,31 @@
     orders = (pairing[0, 0], ctxs - 1 - pairing[0, 0])
     turns = [turn_tables(start + jnp.arange(length, dtype=jnp.int32)) for start in (0, length)]
 
-    def feed_columns(own, after):
-        own, after = lax.optimization_barrier((own, after))
-        own = lax.all_gather(own, "ctx", axis=0, tiled=True)
+    def own_rows(own):
+        return lax.all_gather(own, "ctx", axis=0, tiled=True)
+
+    def both_rows(own):
         return [own] + [swap(own, "dp", bits) for bits in range(1, dps)]
 
+    hold = lax.optimization_barrier
     inputs_all = lax.all_gather(inputs, "ctx", axis=0, tiled=True)
     qkv_low = attention_weights[:, : 3 * width].astype(low_type)
     qkv_low = qkv_low.reshape(owned, 3, ctxs, head_width).transpose(2, 0, 1, 3)
     qkv_low = qkv_low.reshape(ctxs, owned, 3 * head_width)
-    feed_low = after(feed_weights, qkv_low).astype(low_type)
-    qkv_mine = qkv_low = trade(qkv_low, "ctx")
+    feed_low = feed_weights.astype(low_type)
+    qkv_low = trade(qkv_low, "ctx")
     feed_low = feed_low.reshape(owned, 3, groups, part).transpose(2, 1, 0, 3)
     feed_low = trade(feed_low, "fsdp").transpose(1, 0, 2, 3).reshape(3, groups * owned, part)
     qkv_low = gather_pairs(gather_pairs(qkv_low, "dp"), "fsdp")
     qkv_low = qkv_low.transpose(1, 2, 0, 3, 4).reshape(width, 3 * head_width)
-    out_low = after(attention_weights[:, 3 * width :].astype(low_type), qkv_mine)
+    out_low = attention_weights[:, 3 * width :].astype(low_type)
     out_low = gather_pairs(gather_pairs(out_low, "ctx"), "dp")
     inputs_all, qkv_low, feed_low, out_low, turns = lax.optimization_barrier(
         (inputs_all, qkv_low, feed_low, out_low, turns)
     )
 
-    gates = feed_columns(feed_low[0], inputs_all)
-
-    others = jnp.arange(ctxs, dtype=jnp.int32) ^ ctx
-    spots = [jnp.sum(jnp.where(others[:, None] == jnp.arange(ctxs), o, 0), axis=1) for o in orders]
+    near = jnp.arange(ctxs, dtype=jnp.int32) ^ ctx
+    spots = [jnp.sum(jnp.where(near[:, None] == jnp.arange(ctxs), o, 0), axis=1) for o in orders]
     qk_gains = jnp.stack(
         [lax.dynamic_slice_in_dim(gains[i], ctx * head_width, head_width) for i in range(2)]
     )
@@ -849,9 +968,12 @@
     attended, logs, attended_near = [], [], []
     projs, proj_scales, states, chunks = [], [], [], []
     projected = product(inputs_all, qkv_low)
+    feed_own = [feed_low[0], feed_low[1], feed_low[2]]
+    feed_own[0] = own_rows(feed_own[0])
+    projected, feed_own[0], feed_own[1] = hold((projected, feed_own[0], feed_own[1]))
+    gates = both_rows(feed_own[0])
     pre = [projected[:, i * head_width : (i + 1) * head_width] for i in range(2)]
-    squares = after(jnp.stack([jnp.sum(p * p, axis=-1) for p in pre]), gates[0])
-    squares = total_of(squares, ("ctx",))
+    squares = total_of(jnp.stack([jnp.sum(p * p, axis=-1) for p in pre]), ("ctx",))
     scales = lax.rsqrt(squares / width + epsilon_norm).T
     for s in range(2):
         q, k, v = prepare(projected, scales, qk_gains, *turns[s], orders[s], s)
@@ -863,10 +985,11 @@
         out, log = attend_forward(after(queries[s], last), keys[: s + 1], values[: s + 1], spots[s])
         attended.append(out)
         logs.append(log)
-        attended_near.append(jnp.stack(trade_near(out.reshape(ctxs, block, head_width), "ctx")))
-
-    def leave(s, last):
-        proj = out_project(after(attended_near[s], last), out_low, others)
+        return trade_near(out.reshape(ctxs, block, head_width), "ctx")
+
+    def leave(s, pieces, *others):
+        attended_near.append(jnp.stack(pieces))
+        proj = out_project(after(attended_near[s], *others), out_low, near)
         projs.append(proj)
         proj_scales.append(
             lax.rsqrt(jnp.mean(proj * proj, axis=-1, keepdims=True) + epsilon_norm)
@@ -878,31 +1001,42 @@
         state_low = own_first(jnp.split(state_low, dps, axis=1), "dp")
         chunks.append(gather_group(state_low, "fsdp"))
 
-    out_low = gather_pairs(after(out_low, scales), "fsdp")
-    out_low = out_low.transpose(1, 2, 0, 3, 4).reshape(width, width)
-    attend(0, gates[0])
-    ups = feed_columns(feed_low[1], gates[0])
-    last = after(attended[0], ups[0])
-    downs = feed_columns(feed_low[2], last)
-    attend(1, last)
-    leave(0, attended[1])
-    attended_near[1] = after(attended_near[1], gates[-1])
-    leave(1, states[0])
+    out_low, scales = hold((out_low, scales))
+    out_low = gather_pairs(out_low, "fsdp", 1)
+    feed_own[1] = own_rows(feed_own[1])
+    lower = attend(0, gates[0])
+    out_low, feed_own[1], feed_own[2], attended[0] = hold(
+        (out_low, feed_own[1], feed_own[2], attended[0])
+    )
+    out_other = swap(out_low, "fsdp", 1)
+    ups = both_rows(feed_own[1])
+    feed_own[2] = own_rows(feed_own[2])
+    upper = attend(1, after(ups[0], gates[-1]))
+    out_other, lower, upper, attended[1] = hold((out_other, lower, upper, attended[1]))
+    odd = (lax.axis_index("fsdp") & 1)[None]
+    out_low = weave(out_low, out_other, odd).reshape(width, width)
+    leave(0, lower, gates[-1], ups[-1])
+    leave(1, upper, states[0])
+    feed_own[2], states[0] = hold((feed_own[2], states[0]))
+    downs = both_rows(feed_own[2])
 
     gate, up, inner = [None] * 2, [None] * 2, [None] * 2
-    chunks[0][-1] = after(chunks[0][-1], downs[0])
-    gate[0], up[0], inner[0] = gate_up(chunks[0], gates, ups)
-    chunks[1][-1] = after(chunks[1][-1], gate[0])
-    gate[1], up[1], inner[1] = gate_up(chunks[1], gates, ups)
     outs, grad_downs, gain_downs = [None] * 2, [None] * 2, [None] * 2
-    last, halves = inner[0], {}
-    for s in (1, 0):
+    last, sums = downs[0], [None] * 2
+    for s in range(2):
+        chunks[s][-1] = after(chunks[s][-1], last)
+        gate[s], up[s], inner[s] = gate_up(chunks[s], gates, ups)
+        last = inner[s]
+    for s in range(2):
         last = spread([after(inner[s], last)], [downs], 0)
-        halves[s, 0] = swap(last, "fsdp", 1)
-        halves[s, 1] = spread([after(inner[s], last)], [downs], 1)
-        last = after(halves[s, 1], halves[s, 0])
-    for s in (1, 0):
-        down = own_first(list(sum_group(halves[s, 0], halves[s, 1], "fsdp")), "dp")
+        got = swap(last, "fsdp", 1)
+        last = spread([after(inner[s], last)], [downs], 1)
+        sums[s] = sum_group(got, last, "fsdp")
+        last = after(last, got)
+    for s in range(2):
+        if s == 1:
+            sums[1], grad_downs[0] = hold((sums[1], grad_downs[0]))
+        down = own_first(joined(sums[s]), "dp")
         down_scale = lax.rsqrt(jnp.mean(down * down, axis=-1, keepdims=True) + epsilon_norm)
         outs[s] = (states[s] + down * down_scale * gains[3]).astype(low_type)
         grad_down, gain_downs[s] = norm_backward(
@@ -920,11 +1054,11 @@
         grad_gates[s], grad_ups[s] = inner_backward(
             grad_downs[s], after(gate[s], last), up[s], downs
         )
-        last = after(grad_ups[s], *grad_downs[0])
+        last = grad_ups[s]
         last = spread([after(grad_gates[s], last), grad_ups[s]], [gates, ups], 0)
         got = swap(last, "fsdp", 1)
         last = spread([after(grad_gates[s], last), grad_ups[s]], [gates, ups], 1)
-        return [got, last], after(last, got)
+        return sum_group(got, last, "fsdp"), after(last, got)
 
     def gradient_parts(lefts, rights, which, last):
         lefts = [[after(left[0], last)] + left[1:] for left in lefts]
@@ -932,25 +1066,16 @@
         return found, found[-1]
 
     def outward(s, sums):
-        back = sum_group(*sums, "fsdp")
-        grad_states[s] = upstream[rows_of[s]] + own_first(list(back), "dp")
+        grad_states[s] = upstream[rows_of[s]] + own_first(joined(sums), "dp")
         grad_proj, gain_branches[s] = norm_backward(
             projs[s], proj_scales[s], gains[2], grad_states[s]
         )
         grad_projs[s] = grad_proj.astype(low_type)
-        grad_attended = out_back(grad_projs[s], out_low, others)
-        grad_heads[s] = jnp.concatenate(trade_near(grad_attended, "ctx"), axis=0)
+        grad_attended = out_back(grad_projs[s], out_low, near)
+        grad_heads[s] = trade_near(grad_attended, "ctx")
         return grad_attended
 
-    away, near = range(1, dps), range(1)
-    sums, last = inward(1, downs[-1])
-    down_away, last = gradient_parts(grad_downs, inner, away, last)
-    down_away = [swap(piece, "dp", bits) for bits, piece in zip(away, down_away)]
-    lower_sums, last = inward(0, last)
-    gate_away, last = gradient_parts(chunks, grad_gates, away, last)
-    gate_away = [swap(piece, "dp", bits) for bits, piece in zip(away, gate_away)]
-    down_near, last = gradient_parts(grad_downs, inner, near, last)
-
+    away, own = range(1, dps), range(1)
     def kept_feed(own, others):
         kept = own[0].astype(jnp.float32)
         for other in others:
@@ -960,27 +1085,40 @@
     def reduce_feed(kept):
         return lax.psum_scatter(kept, "ctx", scatter_dimension=0, tiled=True)
 
+    def exchanged(pieces):
+        return [swap(piece, "dp", bits) for bits, piece in zip(away, pieces)]
+
+    away, own = range(1, dps), range(1)
+    lower_sums, last = inward(0, downs[-1])
+    down_away, last = gradient_parts(grad_downs, inner, away, last)
+    down_away = exchanged(down_away)
+    upper_sums, last = inward(1, last)
+    gate_away, last = gradient_parts(chunks, grad_gates, away, last)
+    upper_sums, down_away, gate_away = hold((upper_sums, down_away, gate_away))
+    gate_away = exchanged(gate_away)
+    last = outward(1, upper_sums)
+    down_near, last = gradient_parts(grad_downs, inner, own, last)
     down_kept = kept_feed(down_near, down_away)
+    lower_sums, down_kept, grad_heads[1] = hold((lower_sums, down_kept, grad_heads[1]))
     down_gradient = reduce_feed(down_kept)
-    sums[1] = after(sums[1], last, down_kept)
-    last = outward(1, sums)
+    last = outward(0, lower_sums)
     up_away, last = gradient_parts(chunks, grad_ups, away, last)
-    up_away = [swap(piece, "dp", bits) for bits, piece in zip(away, up_away)]
-    lower_sums[1] = after(lower_sums[1], last)
-    last = outward(0, lower_sums)
-    gate_near, last = gradient_parts(chunks, grad_gates, near, last)
+    up_away = exchanged(up_away)
+    gate_near, last = gradient_parts(chunks, grad_gates, own, last)
     gate_kept = kept_feed(gate_near, gate_away)
     gate_gradient = reduce_feed(gate_kept)
-    last = after(last, gate_kept, grad_heads[1])
-    up_near, last = gradient_parts(chunks, grad_ups, near, last)
-    attended_near[0] = after(attended_near[0], last)
-    out_gradient = out_weight(attended_near, grad_projs, others)
-    queries[1] = after(queries[1], out_gradient)
+    up_near, last = gradient_parts(
+        chunks, grad_ups, own, after(last, gate_kept, *grad_heads[1])
+    )
+    queries[1] = after(queries[1], last)
     up_kept = kept_feed(up_near, up_away)
     up_gradient = reduce_feed(up_kept)
 
-    out_gradient = out_gradient.reshape(dps, ctxs, groups, owned, width).transpose(2, 0, 1, 3, 4)
-    out_gradient = sum_pairs(out_gradient, "fsdp")
+    fsdp = lax.axis_index("fsdp")
+
+    def feed_trade(piece):
+        piece = piece.reshape(groups, owned, part)
+        return trade_near([pick(piece, fsdp ^ k) for k in range(groups)], "fsdp")
 
     def stream_rows(values, s):
         return values.reshape((ctxs, 2, block) + values.shape[1:])[:, s].reshape(
@@ -991,14 +1129,14 @@
     gain_qk = 0.0
     for s in (1, 0):
         if s == 0:
-            out_gradient = sum_pairs(out_gradient, "dp")
-            added, grad_part, out_gradient = lax.optimization_barrier(
-                (added, grad_part, out_gradient)
+            down_traded = feed_trade(down_gradient)
+            added, grad_part, out_gradient, down_traded = lax.optimization_barrier(
+                (added, grad_part, out_gradient, down_traded)
             )
             grad_inputs[1] = lax.psum_scatter(grad_part, "ctx", scatter_dimension=0, tiled=True)
         grads = attend_backward(
             queries[s],
-            grad_heads[s],
+            jnp.concatenate(grad_heads[s], axis=0),
             attended[s],
             logs[s],
             keys[: s + 1],
@@ -1007,24 +1145,34 @@
             spots[s],
         )
         if s == 1:
-            grads, out_gradient, up_kept, grad_heads[0] = lax.optimization_barrier(
-                (grads, out_gradient, up_kept, grad_heads[0])
-            )
+            grads, up_kept, grad_heads[0] = hold((grads, up_kept, grad_heads[0]))
+            attended_near[0] = after(attended_near[0], grads[0])
+            out_gradient = out_weight(attended_near, grad_projs, near)
+            out_gradient = out_gradient.reshape(dps, ctxs, groups, owned, width)
+            out_gradient = sum_pairs(out_gradient.transpose(2, 0, 1, 3, 4), "fsdp")
         added = grads[1:]
         weighted, value_low, dots, gain_sums = restore(
             grads, projected, scales, qk_gains, *turns[s], orders[s], s
         )
         gain_qk = gain_qk + gain_sums
         means = total_of(dots.T, ("ctx",)).T / width
-        grad_pre = []
-        for i in range(2):
-            at = slice(i * head_width, (i + 1) * head_width)
-            scale = stream_rows(scales, s)[:, i : i + 1]
-            unit = stream_rows(projected, s)[:, at] * scale
-            grad_pre.append(
-                (scale * (weighted[:, at] - unit * means[:, i : i + 1])).astype(low_type)
+        grad_projected[s] = finish(
+            weighted, projected, scales, means, value_low, ctxs, s
+        )
+        if s == 0:
+            out_gradient = sum_pairs(out_gradient, "dp")
+            gate_gradient, up_gradient, out_gradient, grad_projected[0] = hold(
+                (gate_gradient, up_gradient, out_gradient, grad_projected[0])
             )
-        grad_projected[s] = jnp.concatenate(grad_pre + [value_low], axis=1)
+            gate_traded = feed_trade(gate_gradient)
+            up_traded = feed_trade(up_gradient)
+            qkv_gradient = weight_gradient(
+                [[stream_rows(inputs_all, 0)], [stream_rows(inputs_all, 1)]],
+                grad_projected,
+                0,
+                width,
+            )
+            grad_projected[0], qkv_gradient = hold((grad_projected[0], qkv_gradient))
         grad_part = against(grad_projected[s], qkv_low).astype(low_type)
     grad_inputs[0] = lax.psum_scatter(grad_part, "ctx", scatter_dimension=0, tiled=True)
     out_gradient = sum_pairs(out_gradient, "ctx")
@@ -1032,23 +1180,13 @@
         [grad_states[s] + grad_inputs[s].astype(jnp.float32) for s in range(2)], axis=0
     ).astype(low_type)
 
-    qkv_gradient = weight_gradient(
-        [[stream_rows(inputs_all, 0)], [stream_rows(after(inputs_all, grad_part), 1)]],
-        grad_projected,
-        0,
-        width,
-    )
     qkv_gradient = qkv_gradient.reshape(dps, ctxs, groups, owned, 3 * head_width)
     qkv_gradient = sum_pairs(sum_pairs(qkv_gradient.transpose(2, 0, 1, 3, 4), "fsdp"), "dp")
     qkv_gradient = jnp.concatenate(
         trade_near([pick(qkv_gradient, ctx ^ k) for k in range(ctxs)], "ctx"), axis=0
     )
 
-    fsdp = lax.axis_index("fsdp")
-    feed_pieces = []
-    for piece in (gate_gradient, up_gradient, down_gradient):
-        piece = piece.reshape(groups, owned, part)
-        feed_pieces += trade_near([pick(piece, fsdp ^ k) for k in range(groups)], "fsdp")
+    feed_pieces = gate_traded + up_traded + list(down_traded)
     near_columns = jnp.arange(groups, dtype=jnp.int32) ^ fsdp
     feed_columns_of = jnp.concatenate([kind * groups + near_columns for kind in range(3)])
     feed_gradient, feed_moment_new, feed_square_new, feed_weights_new = update(
@@ -1061,7 +1199,7 @@
     )
     attention_columns = jnp.concatenate(
         [
-            (jnp.arange(3, dtype=jnp.int32)[None, :] * ctxs + others[:, None]).reshape(-1),
+            (jnp.arange(3, dtype=jnp.int32)[None, :] * ctxs + near[:, None]).reshape(-1),
             3 * ctxs + jnp.arange(ctxs, dtype=jnp.int32),
         ]
     )

time: 2010 us -> 1850 us (0.920)
  waiting for transfers between devices: 824 us -> 698 us
  local copies, waits for them, and re-layouts: 196 us -> 126 us
  starting transfers between devices: 81.7 us -> 112 us
  other arithmetic: 174 us -> 152 us
    ppermute x83, waiting for transfers between devices: 683 us -> 549 us  [swap(): return lax.ppermute(value, axis, [(i, i ^ bits) for i in range(size)])]
    ppermute x83, starting transfers between devices: 81.2 us -> 112 us  [swap(): return lax.ppermute(value, axis, [(i, i ^ bits) for i in range(size)])]
    unnamed x294 -> x326, local copies, waits for them, and re-layouts: 71.9 us -> 43.9 us
    pallas_call x28 -> x31, Pallas kernels: 594 us -> 615 us  [the longest x30 610 us: launch(): call(*operands[:scalars], *others, *operands[scalars:])]
    all_gather x1, waiting for transfers between devices: 58.1 us -> 78.6 us  [body(): inputs_all = lax.all_gather(inputs, 'ctx', axis=0, tiled=True)]
  transfers between devices with their start and end apart: 92 -> 92, of which waited for: 36 -> 41; matrix products, arithmetic and copies ran while one was open for 17% -> 15% of each run, Pallas kernels for 30% -> 33%
where the time goes in v2:
time: 1850 us; the launch traced here: 1830 us
  waiting for transfers between devices  698 us (38%)
  Pallas kernels  675 us (36%)
  other arithmetic  152 us (8%)
  local copies, waits for them, and re-layouts  126 us (7%)
  starting transfers between devices  112 us (6%)
  matrix products  54.1 us (3%)
    pallas_call x30, Pallas kernels, launch(): call(*operands[:scalars], *others, *operands[scalars:])  610 us
    ppermute x83, waiting for transfers between devices, swap(): return lax.ppermute(value, axis, [(i, i ^ bits) for i in range(size)])  549 us
    ppermute x83, starting transfers between devices, swap(): return lax.ppermute(value, axis, [(i, i ^ bits) for i in range(size)])  112 us
    all_gather x1, waiting for transfers between devices, body(): inputs_all = lax.all_gather(inputs, 'ctx', axis=0, tiled=True)  78.6 us
    all_gather x3, waiting for transfers between devices, own_rows(): return lax.all_gather(own, 'ctx', axis=0, tiled=True)  69.5 us
    unnamed x326, local copies, waits for them, and re-layouts  43.9 us
  transfers between devices with their start and end apart: 92, of which 41 were waited for; matrix products, arithmetic and copies ran while one was open for 15% of the time, Pallas kernels for 33%

profile of v2, /device:TPU:0, one launch (start us, length us, event | category | flops | bytes accessed | tf_op | source)
XLA Modules:
  0.0 1833.1 jit_solution(4026319958512484365)
XLA Ops:
  54.9 14.9 collective-permute-done.3
  90.0 24.7 %collective-permute-done.4 = bf16[1,2,4,64,1536]{4,3,2,1,0:T(8,128)(2,1)S(1)} collective-permute-done((bf16[1,2,4,64,1536]{4,3,2,1,0:T(8,128)(2,1)S(1)}, bf16[1,2,4,64,1536]{4,3,2,1,0:T(8,128)(2,1)S(1)}, u32[]{:S(2)}, u32[]{:S(2)}) %collective-permute-start.4) | collective-permute-done | bytes 1572896 | tf_op jit(solution)/shard_map/ppermute | solution.py:801
  118.5 21.1 %collective-permute-done.10 = bf16[2,64,2048]{2,1,0:T(8,128)(2,1)} collective-permute-done((bf16[2,64,2048]{2,1,0:T(8,128)(2,1)}, bf16[2,64,2048]{2,1,0:T(8,128)(2,1)}, u32[]{:S(2)}, u32[]{:S(2)}) %collective-permute-start.10) | collective-permute-done | bytes 524320 | tf_op jit(solution)/shard_map/ppermute | solution.py:801
  148.8 14.8 collective-permute-done.11
  171.4 78.6 %all-gather.11.cloned.1.call-done = bf16[1,1,3072,2048]{3,2,1,0:T(8,128)(2,1)} async-done(((bf16[1,1,768,2048]{3,2,1,0:T(8,128)(2,1)}), bf16[1,1,3072,2048]{3,2,1,0:T(8,128)(2,1)}) %all-gather.11.cloned.1.call-update) | async-done | bytes 12582928 | tf_op jit(solution)/shard_map/all_gather | solution.py:946
  253.7 26.1 %fusion.30.q_ref.k_ref.v_ref.refs_1_.refs_2_ = f32[3072,1536]{1,0:T(8,128)} fusion(bf16[3072,2048]{1,0:T(8,128)(2,1)} %bitcast.433, bf16[2048,1536]{1,0:T(8,128)(2,1)} %bitcast.439), kind=kOutput, calls=%fused_computation.257 | convolution fusion | flops 19327352832 | bytes 37748736 | tf_op jit(solution)/shard_map/dot_general | solution.py:52
  279.8 54.8 %all-gather.13.cloned.1.call-done = bf16[1,1024,2048]{2,1,0:T(8,128)(2,1)} async-done(((bf16[1,256,2048]{2,1,0:T(8,128)(2,1)}), bf16[1,1024,2048]{2,1,0:T(8,128)(2,1)}) %all-gather.13.cloned.1.call-update) | async-done | bytes 4194320 | tf_op jit(solution)/shard_map/all_gather | solution.py:940
  366.9 19.8 %attend_forward.2 = (bf16[1536,512]{1,0:T(8,128)(2,1)S(1)}, f32[4,1,1536]{2,1,0:T(1,128)S(1)}) custom-call(s32[4]{0:T(128)S(1)} %get-tuple-element.243.refs_0_, bf16[1024,2048]{1,0:T(8,128)(2,1)S(1)} %bitcast.404, bf16[1536,512]{1,0:T(8,128)(2,1)S(1)} %get-tuple-element.133.refs_2_.refs_1_, ...), custom_call_target="tpu_custom_call" | custom-call | flops 1024 | bytes 1024 | tf_op jit(solution)/shard_map/attend_forward/pallas_call | solution.py:120
  401.9 14.7 all-gather.7.cloned.1.call-done.refs_1_.refs_7_.refs_5_
  421.3 29.6 %collective-permute-done.15.refs_2_.refs_1_.refs_6_.refs_4_ = bf16[1024,2048]{1,0:T(8,128)(2,1)} collective-permute-done((bf16[1024,2048]{1,0:T(8,128)(2,1)}, bf16[1024,2048]{1,0:T(8,128)(2,1)}, u32[]{:S(2)}, u32[]{:S(2)}) %collective-permute-start.15) | collective-permute-done | bytes 4194336 | tf_op jit(solution)/shard_map/ppermute | solution.py:801
  458.2 46.0 %attend_forward.3 = (bf16[1536,512]{1,0:T(8,128)(2,1)S(1)}, f32[4,1,1536]{2,1,0:T(1,128)S(1)}) custom-call(s32[4]{0:T(128)S(1)} %get-tuple-element.242.refs_0_, bf16[1024,2048]{1,0:T(8,128)(2,1)S(1)} %copy-done.1, bf16[1024,2048]{1,0:T(8,128)(2,1)} %collective-permute-done.15.refs_2_.refs_1_.refs_6_.refs_4_, ...), custom_call_target="tpu_custom_call" | custom-call | flops 1024 | bytes 1024 | tf_op jit(solution)/shard_map/attend_forward/pallas_call | solution.py:120
  508.8 13.5 collective-permute-done.21
  522.3 25.9 %collective-permute-done.22 = bf16[384,512]{1,0:T(8,128)(2,1)S(1)} collective-permute-done((bf16[384,512]{1,0:T(8,128)(2,1)S(1)}, bf16[384,512]{1,0:T(8,128)(2,1)S(1)}, u32[]{:S(2)}, u32[]{:S(2)}) %collective-permute-start.22) | collective-permute-done | bytes 393248 | tf_op jit(solution)/shard_map/ppermute | solution.py:801
  578.5 24.5 %collective-permute-done.25.refs_4_.refs_9_.refs_7_.refs_17_ = bf16[384,2048]{1,0:T(8,128)(2,1)} collective-permute-done((bf16[384,2048]{1,0:T(8,128)(2,1)}, bf16[384,2048]{1,0:T(8,128)(2,1)}, u32[]{:S(2)}, u32[]{:S(2)}) %collective-permute-start.25) | collective-permute-done | bytes 1572896 | tf_op jit(solution)/shard_map/ppermute | solution.py:801
  603.6 22.2 %collective-permute-done.28.refs_4_.refs_13_.refs_11_.refs_21_ = bf16[384,2048]{1,0:T(8,128)(2,1)S(1)} collective-permute-done((bf16[384,2048]{1,0:T(8,128)(2,1)S(1)}, bf16[384,2048]{1,0:T(8,128)(2,1)S(1)}, u32[]{:S(2)}, u32[]{:S(2)}) %collective-permute-start.28) | collective-permute-done | bytes 1572896 | tf_op jit(solution)/shard_map/ppermute | solution.py:801
  625.8 37.7 %gate_up.2 = (bf16[1536,2048]{1,0:T(8,128)(2,1)}, bf16[1536,2048]{1,0:T(8,128)(2,1)}, bf16[1536,2048]{1,0:T(8,128)(2,1)}) custom-call(bf16[1024,2048]{1,0:T(8,128)(2,1)} %all-gather.9.cloned.1.call-done.refs_0_.refs_2_.refs_3_.refs_7_.refs_1_.refs_6_, bf16[384,2048]{1,0:T(8,128)(2,1)S(1)} %collective-permute-done.24.refs_1_.refs_6_.refs_4_.refs_14_, ...), custom_call_target="tpu_custom_call" | custom-call | flops 1024 | bytes 1024 | tf_op jit(solution)/shard_map/gate_up/pallas_call | solution.py:120
  665.2 36.8 %gate_up.3 = (bf16[1536,2048]{1,0:T(8,128)(2,1)}, bf16[1536,2048]{1,0:T(8,128)(2,1)}, bf16[1536,2048]{1,0:T(8,128)(2,1)}) custom-call(bf16[1536,2048]{1,0:T(8,128)(2,1)} %get-tuple-element.153.refs_0_.refs_1_.refs_12_.refs_5_.refs_10_.refs_3_.refs_13_, bf16[384,2048]{1,0:T(8,128)(2,1)S(1)} %collective-permute-done.27.refs_1_.refs_10_.refs_8_.refs_18_, ...), custom_call_target="tpu_custom_call" | custom-call | flops 1024 | bytes 1024 | tf_op jit(solution)/shard_map/gate_up/pallas_call | solution.py:120
  732.8 13.1 spread.10.refs_0_
  746.2 21.3 %collective-permute-done.32 = bf16[2,1,384,1024]{3,2,0,1:T(8,128)(2,1)} collective-permute-done((bf16[2,1,384,1024]{3,2,0,1:T(8,128)(2,1)}, bf16[2,1,384,1024]{3,2,0,1:T(8,128)(2,1)}, u32[]{:S(2)}, u32[]{:S(2)}) %collective-permute-start.32) | collective-permute-done | bytes 1572896 | tf_op jit(solution)/shard_map/ppermute | solution.py:801
  778.3 11.2 spread.11
  793.8 18.9 %collective-permute-done.36.refs_4_.refs_7_.refs_5_ = bf16[384,2048]{1,0:T(8,128)(2,1)} collective-permute-done((bf16[384,2048]{1,0:T(8,128)(2,1)S(1)}, bf16[384,2048]{1,0:T(8,128)(2,1)}, u32[]{:S(2)}, u32[]{:S(2)}) %collective-permute-start.36) | collective-permute-done | bytes 1572896 | tf_op jit(solution)/shard_map/ppermute | solution.py:801
  816.5 33.1 %collective-permute-done.34 = bf16[2,1,384,1024]{3,2,0,1:T(8,128)(2,1)S(1)} collective-permute-done((bf16[2,1,384,1024]{3,2,0,1:T(8,128)(2,1)S(1)}, bf16[2,1,384,1024]{3,2,0,1:T(8,128)(2,1)S(1)}, u32[]{:S(2)}, u32[]{:S(2)}) %collective-permute-start.34) | collective-permute-done | bytes 1572896 | tf_op jit(solution)/shard_map/ppermute | solution.py:801
  855.0 24.6 %inner_backward.2 = (bf16[1536,2048]{1,0:T(8,128)(2,1)}, bf16[1536,2048]{1,0:T(8,128)(2,1)}) custom-call(bf16[1024,2048]{1,0:T(8,128)(2,1)} %copy-done.82, bf16[384,2048]{1,0:T(8,128)(2,1)S(1)} %collective-permute-done.35.refs_1_.refs_4_.refs_2_, bf16[384,2048]{1,0:T(8,128)(2,1)} %collective-permute-done.37.refs_2_.refs_5_.refs_3_, ...), custom_call_target="tpu_custom_call" | custom-call | flops 1024 | bytes 1024 | tf_op jit(solution)/shard_map/inner_backward/pallas_call | solution.py:120
  879.6 19.3 %spread.12.refs_0_ = bf16[2,768,1024]{2,1,0:T(8,128)(2,1)} custom-call(bf16[1536,2048]{1,0:T(8,128)(2,1)} %get-tuple-element.167.refs_0_.refs_2_.refs_12_.refs_22_, bf16[1536,2048]{1,0:T(8,128)(2,1)} %get-tuple-element.168.refs_1_.refs_14_.refs_12_, bf16[1536,2048]{1,0:T(8,128)(2,1)} %get-tuple-element.167.refs_0_.refs_2_.refs_12_.refs_22_, ...), custom_call_target="tpu_custom_call" | custom-call | flops 1024 | bytes 1024 | tf_op jit(solution)/shard_map/spread/pallas_call | solution.py:120
  899.6 19.6 %spread.13.refs_0_.refs_2_ = bf16[2,768,1024]{2,1,0:T(8,128)(2,1)} custom-call(bf16[2,768,1024]{2,1,0:T(8,128)(2,1)} %spread.12.refs_0_, bf16[1536,2048]{1,0:T(8,128)(2,1)} %get-tuple-element.168.refs_1_.refs_14_.refs_12_, bf16[1536,2048]{1,0:T(8,128)(2,1)} %get-tuple-element.167.refs_0_.refs_2_.refs_12_.refs_22_, bf16[1024,2048]{1,0:T(8,128)(2,1)} %bitcast.401, ...), custom_call_target="tpu_custom_call" | custom-call | flops 1024 | bytes 1024 | tf_op jit(solution)/shard_map/spread/pallas_call | solution.py:120
  922.0 20.8 %weight_gradient.7.refs_0_ = bf16[1024,2048]{1,0:T(8,128)(2,1)} custom-call(bf16[2,768,1024]{2,1,0:T(8,128)(2,1)} %spread.13.refs_0_.refs_2_, bf16[2,768,1024]{2,1,0:T(8,128)(2,1)} %copy-done.92, bf16[2,768,1024]{2,1,0:T(8,128)(2,1)} %spread.13.refs_0_.refs_2_, bf16[2,768,1024]{2,1,0:T(8,128)(2,1)} %copy-done.92, ...), custom_call_target="tpu_custom_call" | custom-call | flops 1024 | bytes 1024 | tf_op jit(solution)/shard_map/weight_gradient/pallas_call | solution.py:120
  944.2 24.8 %inner_backward.3 = (bf16[1536,2048]{1,0:T(8,128)(2,1)}, bf16[1536,2048]{1,0:T(8,128)(2,1)}) custom-call(bf16[1024,2048]{1,0:T(8,128)(2,1)} %weight_gradient.7.refs_0_, bf16[384,2048]{1,0:T(8,128)(2,1)S(1)} %copy-done.23, bf16[384,2048]{1,0:T(8,128)(2,1)} %collective-permute-done.42.refs_9_.refs_2_.refs_7_, bf16[384,2048]{1,0:T(8,128)(2,1)} %copy-done.100, ...), custom_call_target="tpu_custom_call" | custom-call | flops 1024 | bytes 1024 | tf_op jit(solution)/shard_map/inner_backward/pallas_call | solution.py:120
  969.0 19.2 %spread.14.refs_0_ = bf16[2,768,1024]{2,1,0:T(8,128)(2,1)} custom-call(bf16[1536,2048]{1,0:T(8,128)(2,1)} %get-tuple-element.171.refs_0_.refs_2_.refs_13_.refs_23_, bf16[1536,2048]{1,0:T(8,128)(2,1)} %get-tuple-element.172.refs_1_.refs_15_.refs_13_, bf16[1536,2048]{1,0:T(8,128)(2,1)} %get-tuple-element.171.refs_0_.refs_2_.refs_13_.refs_23_, ...), custom_call_target="tpu_custom_call" | custom-call | flops 1024 | bytes 1024 | tf_op jit(solution)/shard_map/spread/pallas_call | solution.py:120
  988.8 19.6 %spread.15.refs_0_.refs_3_ = bf16[2,768,1024]{2,1,0:T(8,128)(2,1)} custom-call(bf16[2,768,1024]{2,1,0:T(8,128)(2,1)} %spread.14.refs_0_, bf16[1536,2048]{1,0:T(8,128)(2,1)} %get-tuple-element.172.refs_1_.refs_15_.refs_13_, bf16[1536,2048]{1,0:T(8,128)(2,1)} %get-tuple-element.171.refs_0_.refs_2_.refs_13_.refs_23_, bf16[1024,2048]{1,0:T(8,128)(2,1)} %bitcast.403, ...), custom_call_target="tpu_custom_call" | custom-call | flops 1024 | bytes 1024 | tf_op jit(solution)/shard_map/spread/pallas_call | solution.py:120
  1020.9 20.8 %weight_gradient.8 = bf16[1024,2048]{1,0:T(8,128)(2,1)} custom-call(bf16[2,768,1024]{2,1,0:T(8,128)(2,1)} %spread.15.refs_0_.refs_3_, bf16[2,768,1024]{2,1,0:T(8,128)(2,1)} %copy-done.94, bf16[1024,2048]{1,0:T(8,128)(2,1)} %all-gather.9.cloned.1.call-done.refs_0_.refs_2_.refs_3_.refs_7_.refs_1_.refs_6_, bf16[2,768,1024]{2,1,0:T(8,128)(2,1)} %spread.15.refs_0_.refs_3_, ...), custom_call_target="tpu_custom_call" | custom-call | flops 1024 | bytes 1024 | tf_op jit(solution)/shard_map/weight_gradient/pallas_call | solution.py:120
  1041.6 39.8 %collective-permute-done.45 = bf16[1024,2048]{1,0:T(8,128)(2,1)} collective-permute-done((bf16[1024,2048]{1,0:T(8,128)(2,1)}, bf16[1024,2048]{1,0:T(8,128)(2,1)}, u32[]{:S(2)}, u32[]{:S(2)}) %collective-permute-start.45) | collective-permute-done | bytes 4194336 | tf_op jit(solution)/shard_map/ppermute | solution.py:801
  1098.3 16.0 collective-permute-start.46
  1117.6 21.3 %weight_gradient.9 = bf16[1024,2048]{1,0:T(8,128)(2,1)} custom-call(bf16[4,384,512]{2,1,0:T(8,128)(2,1)S(1)} %out_back.2.refs_0_.refs_1_, bf16[4,384,512]{2,1,0:T(8,128)(2,1)S(1)} %out_back.2.refs_0_.refs_1_, bf16[384,2048]{1,0:T(8,128)(2,1)} %copy-done.21, bf16[384,2048]{1,0:T(8,128)(2,1)} %collective-permute-done.37.refs_2_.refs_5_.refs_3_, ...), custom_call_target="tpu_custom_call" | custom-call | flops 1024 | bytes 1024 | tf_op jit(solution)/shard_map/weight_gradient/pallas_call | solution.py:120
  1162.1 21.4 %weight_gradient.10.refs_0_.refs_2_ = bf16[1024,2048]{1,0:T(8,128)(2,1)} custom-call(bf16[4,384,512]{2,1,0:T(8,128)(2,1)S(1)} %out_back.3.refs_0_.refs_2_, bf16[1024,2048]{1,0:T(8,128)(2,1)} %all-gather.9.cloned.1.call-done.refs_0_.refs_2_.refs_3_.refs_7_.refs_1_.refs_6_, bf16[4,384,512]{2,1,0:T(8,128)(2,1)S(1)} %out_back.3.refs_0_.refs_2_, ...), custom_call_target="tpu_custom_call" | custom-call | flops 1024 | bytes 1024 | tf_op jit(solution)/shard_map/weight_gradient/pallas_call | solution.py:120
  1183.5 21.1 %weight_gradient.11.refs_0_.refs_7_ = bf16[1024,2048]{1,0:T(8,128)(2,1)} custom-call(bf16[1024,2048]{1,0:T(8,128)(2,1)} %weight_gradient.10.refs_0_.refs_2_, bf16[1024,2048]{1,0:T(8,128)(2,1)} %all-gather.9.cloned.1.call-done.refs_0_.refs_2_.refs_3_.refs_7_.refs_1_.refs_6_, bf16[1024,2048]{1,0:T(8,128)(2,1)} %weight_gradient.10.refs_0_.refs_2_, ...), custom_call_target="tpu_custom_call" | custom-call | flops 1024 | bytes 1024 | tf_op jit(solution)/shard_map/weight_gradient/pallas_call | solution.py:120
  1204.7 34.2 %collective-permute-done.49 = bf16[1024,2048]{1,0:T(8,128)(2,1)S(1)} collective-permute-done((bf16[1024,2048]{1,0:T(8,128)(2,1)}, bf16[1024,2048]{1,0:T(8,128)(2,1)S(1)}, u32[]{:S(2)}, u32[]{:S(2)}) %collective-permute-start.49) | collective-permute-done | bytes 4194336 | tf_op jit(solution)/shard_map/ppermute | solution.py:801
  1254.8 21.2 %weight_gradient.12.refs_1_ = bf16[1024,2048]{1,0:T(8,128)(2,1)} custom-call(bf16[1024,2048]{1,0:T(8,128)(2,1)} %weight_gradient.11.refs_0_.refs_7_, bf16[1024,2048]{1,0:T(8,128)(2,1)} %add_convert_fusion.1.refs_1_.refs_8_, bf16[384,512]{1,0:T(8,128)(2,1)S(1)} %get-tuple-element.179.refs_2_.refs_9_, bf16[384,512]{1,0:T(8,128)(2,1)S(1)} %copy-done.53, ...), custom_call_target="tpu_custom_call" | custom-call | flops 1024 | bytes 1024 | tf_op jit(solution)/shard_map/weight_gradient/pallas_call | solution.py:120
  1276.0 60.4 %collective-permute-done.50 = bf16[1024,2048]{1,0:T(8,128)(2,1)} collective-permute-done((bf16[1024,2048]{1,0:T(8,128)(2,1)}, bf16[1024,2048]{1,0:T(8,128)(2,1)}, u32[]{:S(2)}, u32[]{:S(2)}) %collective-permute-start.50) | collective-permute-done | bytes 4194336 | tf_op jit(solution)/shard_map/ppermute | solution.py:801
  1346.5 62.5 %attend_backward.2 = (f32[1536,512]{1,0:T(8,128)}, f32[3072,512]{1,0:T(8,128)}, f32[3072,512]{1,0:T(8,128)}) custom-call(s32[4]{0:T(128)S(1)} %copy-done.75, bf16[1024,2048]{1,0:T(8,128)(2,1)} %weight_gradient.12.refs_1_, bf16[1536,512]{1,0:T(8,128)(2,1)S(1)} %copy-done.45, bf16[1536,512]{1,0:T(8,128)(2,1)S(1)} %pad_maximum_fusion.11.refs_3_, ...), custom_call_target="tpu_custom_call" | custom-call | flops 1024 | bytes 1024 | tf_op jit(solution)/shard_map/attend_backward/pallas_call | solution.py:120
  1410.9 11.8 out_weight.1
  1484.1 14.0 convolution_convert_fusion.1
  1501.3 30.7 %collective-permute-done.57 = bf16[1,2,4,64,2048]{4,3,2,1,0:T(8,128)(2,1)} collective-permute-done((bf16[1,2,4,64,2048]{4,3,2,1,0:T(8,128)(2,1)}, bf16[1,2,4,64,2048]{4,3,2,1,0:T(8,128)(2,1)}, u32[]{:S(2)}, u32[]{:S(2)}) %collective-permute-start.57) | collective-permute-done | bytes 2097184 | tf_op jit(solution)/shard_map/ppermute | solution.py:801
  1542.2 28.8 %attend_backward.3 = (f32[1536,512]{1,0:T(8,128)}, f32[1536,512]{1,0:T(8,128)}, f32[1536,512]{1,0:T(8,128)}) custom-call(s32[4]{0:T(128)S(1)} %copy-done.77, bf16[1536,512]{1,0:T(8,128)(2,1)S(1)} %copy-done.43, bf16[1536,512]{1,0:T(8,128)(2,1)S(1)} %pad_maximum_fusion.12.refs_2_, bf16[1536,512]{1,0:T(8,128)(2,1)S(1)} %copy-done.49, ...), custom_call_target="tpu_custom_call" | custom-call | flops 1024 | bytes 1024 | tf_op jit(solution)/shard_map/attend_backward/pallas_call | solution.py:120
  1619.4 32.5 %weight_gradient.13 = bf16[2048,1536]{1,0:T(8,128)(2,1)} custom-call(bf16[1536,2048]{1,0:T(8,128)(2,1)} %bitcast.431, bf16[1536,2048]{1,0:T(8,128)(2,1)} %bitcast.430, bf16[1536,1536]{1,0:T(8,128)(2,1)} %copy-done.19, bf16[1536,1536]{1,0:T(8,128)(2,1)} %copy-done.18), custom_call_target="tpu_custom_call" | custom-call | flops 1024 | bytes 1024 | tf_op jit(solution)/shard_map/weight_gradient/pallas_call | solution.py:120
  1651.9 14.0 convolution_convert_fusion
  1722.0 34.0 %collective-permute-done.65 = bf16[1,2,4,64,1536]{4,3,2,1,0:T(8,128)(2,1)S(1)} collective-permute-done((bf16[1,2,4,64,1536]{4,3,2,1,0:T(8,128)(2,1)S(1)}, bf16[1,2,4,64,1536]{4,3,2,1,0:T(8,128)(2,1)S(1)}, u32[]{:S(2)}, u32[]{:S(2)}) %collective-permute-start.65) | collective-permute-done | bytes 1572896 | tf_op jit(solution)/shard_map/ppermute | solution.py:801
  1758.1 18.4 %update.3 = (f32[64,24576]{1,0:T(8,128)}, f32[64,24576]{1,0:T(8,128)}, f32[64,24576]{1,0:T(8,128)}, f32[64,24576]{1,0:T(8,128)}) custom-call(s32[12]{0:T(128)S(1)} %pad_add_fusion.1.columns_ref, bf16[768,2048]{1,0:T(8,128)(2,1)S(1)} %constant_dynamic-update-slice_fusion.refs_0_, f32[64,24576]{1,0:T(8,128)S(1)} %bitcast.407, f32[64,24576]{1,0:T(8,128)} %refs_2_.3, ...), custom_call_target="tpu_custom_call" | custom-call | flops 1024 | bytes 1024 | tf_op jit(solution)/shard_map/update/pallas_call | solution.py:784
  1784.6 11.7 collective-permute-done.71
  (685 shorter events, 550.6 us)
Async XLA Ops:
  7.2 242.8 %all-gather.11.cloned.1.call-start = ((), (), s32[]{:S(2)}) async-start(), calls=%async_computation.12 | async-start | bytes 15728640 | tf_op jit(solution)/shard_map/all_gather | solution.py:946
  7.9 326.7 %all-gather.13.cloned.1.call-start = ((), (), s32[]{:S(2)}) async-start(), calls=%async_computation.13 | async-start | bytes 5242880 | tf_op jit(solution)/shard_map/all_gather | solution.py:940
  17.7 65.5 %collective-permute-start.9 = (bf16[1,64,2048]{2,1,0:T(8,128)(2,1)S(1)}, bf16[1,64,2048]{2,1,0:T(8,128)(2,1)}, u32[]{:S(2)}, u32[]{:S(2)}) collective-permute-start(bf16[1,64,2048]{2,1,0:T(8,128)(2,1)S(1)} %slice_bitcast_fusion.28), channel_id=1, source_target_pairs={{0,8},{4,12},{8,0},{12,4},{1,9},{5,13},{9,1},{13,5},{2,10},{6,14},... | collective-permute-start | bytes 786440 | tf_op jit(solution)/shard_map/ppermute | solution.py:801
  38.7 103.9 %collective-permute-start.6 = (bf16[3,64,2048]{2,1,0:T(8,128)(2,1)}, bf16[3,64,2048]{2,1,0:T(8,128)(2,1)}, u32[]{:S(2)}, u32[]{:S(2)}) collective-permute-start(bf16[3,64,2048]{2,1,0:T(8,128)(2,1)} %bitcast.387), channel_id=1, source_target_pairs={{0,1},{1,0},{2,3},{3,2},{4,5},{5,4},{6,7},{7,6},{8,9},{9,8},{10,11... | collective-permute-start | bytes 2359304 | tf_op jit(solution)/shard_map/ppermute | solution.py:801
  43.9 100.7 %collective-permute-start.7 = (bf16[3,64,2048]{2,1,0:T(8,128)(2,1)}, bf16[3,64,2048]{2,1,0:T(8,128)(2,1)}, u32[]{:S(2)}, u32[]{:S(2)}) collective-permute-start(bf16[3,64,2048]{2,1,0:T(8,128)(2,1)} %bitcast.386), channel_id=1, source_target_pairs={{0,2},{1,3},{2,0},{3,1},{4,6},{5,7},{6,4},{7,5},{8,10},{9,11},{10,... | collective-permute-start | bytes 2359304 | tf_op jit(solution)/shard_map/ppermute | solution.py:801
  48.0 98.7 %collective-permute-start.8 = (bf16[3,64,2048]{2,1,0:T(8,128)(2,1)}, bf16[3,64,2048]{2,1,0:T(8,128)(2,1)}, u32[]{:S(2)}, u32[]{:S(2)}) collective-permute-start(bf16[3,64,2048]{2,1,0:T(8,128)(2,1)} %bitcast.385), channel_id=1, source_target_pairs={{0,3},{1,2},{2,1},{3,0},{4,7},{5,6},{6,5},{7,4},{8,11},{9,10},{10,... | collective-permute-start | bytes 2359304 | tf_op jit(solution)/shard_map/ppermute | solution.py:801
  70.0 44.6 %collective-permute-start.4 = (bf16[1,2,4,64,1536]{4,3,2,1,0:T(8,128)(2,1)S(1)}, bf16[1,2,4,64,1536]{4,3,2,1,0:T(8,128)(2,1)S(1)}, u32[]{:S(2)}, u32[]{:S(2)}) collective-permute-start(bf16[1,2,4,64,1536]{4,3,2,1,0:T(8,128)(2,1)S(1)} %pad_maximum_fusion.4), channel_id=1, source_target_pairs={{0,2},{1,3},{2,0},{3,1},{4,6},{5,7},{6,4},{7,5},{8,10},{9,11},{10,... | collective-permute-start | bytes 4718600 | tf_op jit(solution)/shard_map/ppermute | solution.py:801
  85.1 54.5 %collective-permute-start.10 = (bf16[2,64,2048]{2,1,0:T(8,128)(2,1)}, bf16[2,64,2048]{2,1,0:T(8,128)(2,1)}, u32[]{:S(2)}, u32[]{:S(2)}) collective-permute-start(bf16[2,64,2048]{2,1,0:T(8,128)(2,1)} %maximum_bitcast_fusion.4), channel_id=1, source_target_pairs={{0,4},{4,0},{8,12},{12,8},{1,5},{5,1},{9,13},{13,9},{2,6},{6,2},{1... | collective-permute-start | bytes 1572872 | tf_op jit(solution)/shard_map/ppermute | solution.py:801
  116.8 48.5 %collective-permute-start.5 = (bf16[2,2,4,64,1536]{4,3,2,1,0:T(8,128)(2,1)}, bf16[2,2,4,64,1536]{4,3,2,1,0:T(8,128)(2,1)}, u32[]{:S(2)}, u32[]{:S(2)}) collective-permute-start(bf16[2,2,4,64,1536]{4,3,2,1,0:T(8,128)(2,1)} %maximum_bitcast_fusion.1), channel_id=1, source_target_pairs={{0,1},{1,0},{2,3},{3,2},{4,5},{5,4},{6,7},{7,6},{8,9},{9,8},{10,11... | collective-permute-start | bytes 9437192 | tf_op jit(solution)/shard_map/ppermute | solution.py:801
  253.7 163.0 %all-gather.7.cloned.1.call-start = ((), (), s32[]{:S(2)}) async-start(), calls=%async_computation.5 | async-start | bytes 5242880 | tf_op jit(solution)/shard_map/all_gather | solution.py:940
  334.6 239.2 %all-gather.9.cloned.1.call-start = ((), (), s32[]{:S(2)}) async-start(), calls=%async_computation.6 | async-start | bytes 5242880 | tf_op jit(solution)/shard_map/all_gather | solution.py:940
  355.1 42.3 %collective-permute-start.14 = (bf16[1,2,4,64,2048]{4,3,2,1,0:T(8,128)(2,1)}, bf16[1,2,4,64,2048]{4,3,2,1,0:T(8,128)(2,1)}, u32[]{:S(2)}, u32[]{:S(2)}) collective-permute-start(bf16[1,2,4,64,2048]{4,3,2,1,0:T(8,128)(2,1)} %bitcast.438), channel_id=1, source_target_pairs={{0,2},{1,3},{2,0},{3,1},{4,6},{5,7},{6,4},{7,5},{8,10},{9,11},{10,... | collective-permute-start | bytes 6291464 | tf_op jit(solution)/shard_map/ppermute | solution.py:801
  357.0 93.9 %collective-permute-start.15 = (bf16[1024,2048]{1,0:T(8,128)(2,1)}, bf16[1024,2048]{1,0:T(8,128)(2,1)}, u32[]{:S(2)}, u32[]{:S(2)}) collective-permute-start(bf16[1024,2048]{1,0:T(8,128)(2,1)} %bitcast.397), channel_id=1, source_target_pairs={{0,16},{16,0},{1,17},{17,1},{2,18},{18,2},{3,19},{19,3},{4,20},{20... | collective-permute-start | bytes 12582920 | tf_op jit(solution)/shard_map/ppermute | solution.py:801
  416.6 131.6 %collective-permute-start.17 = (bf16[2,2,4,64,2048]{4,3,2,1,0:T(8,128)(2,1)}, bf16[2,2,4,64,2048]{4,3,2,1,0:T(8,128)(2,1)}, u32[]{:S(2)}, u32[]{:S(2)}) collective-permute-start(bf16[2,2,4,64,2048]{4,3,2,1,0:T(8,128)(2,1)} %maximum_bitcast_fusion.own_ref), channel_id=1, source_target_pairs={{0,1},{1,0},{2,3},{3,2},{4,5},{5,4},{6,7},{7,6},{8,9},{9,8},{10,11... | collective-permute-start | bytes 12582920 | tf_op jit(solution)/shard_map/ppermute | solution.py:801
  416.6 136.8 %collective-permute-start.16 = (bf16[1024,2048]{1,0:T(8,128)(2,1)}, bf16[1024,2048]{1,0:T(8,128)(2,1)}, u32[]{:S(2)}, u32[]{:S(2)}) collective-permute-start(bf16[1024,2048]{1,0:T(8,128)(2,1)} %all-gather.7.cloned.1.call-done.refs_1_.refs_7_.refs_5_), channel_id=1, source_target_pairs={{0,16},{16,0},{1,17},{17,1},{2,18},{18,2},{3,19},{19,3},{4,20},{20... | collective-permute-start | bytes 12582920 | tf_op jit(solution)/shard_map/ppermute | solution.py:801
  418.2 1079.9 %reduce-scatter.10.cloned.1.call-start = ((), (), s32[]{:S(2)}) async-start(), calls=%async_computation.9 | async-start | bytes 5242880 | tf_op jit(solution)/shard_map/reduce_scatter | solution.py:1086
  419.8 84.6 %collective-permute-start.18 = (bf16[384,512]{1,0:T(8,128)(2,1)S(1)}, bf16[384,512]{1,0:T(8,128)(2,1)S(1)}, u32[]{:S(2)}, u32[]{:S(2)}) collective-permute-start(bf16[384,512]{1,0:T(8,128)(2,1)S(1)} %get-tuple-element.308), channel_id=1, source_target_pairs={{0,4},{4,0},{8,12},{12,8},{1,5},{5,1},{9,13},{13,9},{2,6},{6,2},{1... | collective-permute-start | bytes 1179656 | tf_op jit(solution)/shard_map/ppermute | solution.py:801
  419.9 84.6 %collective-permute-start.19 = (bf16[384,512]{1,0:T(8,128)(2,1)S(1)}, bf16[384,512]{1,0:T(8,128)(2,1)S(1)}, u32[]{:S(2)}, u32[]{:S(2)}) collective-permute-start(bf16[384,512]{1,0:T(8,128)(2,1)S(1)} %get-tuple-element.307), channel_id=1, source_target_pairs={{0,8},{4,12},{8,0},{12,4},{1,9},{5,13},{9,1},{13,5},{2,10},{6,14},... | collective-permute-start | bytes 1179656 | tf_op jit(solution)/shard_map/ppermute | solution.py:801
  450.9 57.2 %collective-permute-start.20 = (bf16[384,512]{1,0:T(8,128)(2,1)S(1)}, bf16[384,512]{1,0:T(8,128)(2,1)S(1)}, u32[]{:S(2)}, u32[]{:S(2)}) collective-permute-start(bf16[384,512]{1,0:T(8,128)(2,1)S(1)} %get-tuple-element.306), channel_id=1, source_target_pairs={{0,12},{4,8},{8,4},{12,0},{1,13},{5,9},{9,5},{13,1},{2,14},{6,10},... | collective-permute-start | bytes 1179656 | tf_op jit(solution)/shard_map/ppermute | solution.py:801
  504.5 43.7 %collective-permute-start.22 = (bf16[384,512]{1,0:T(8,128)(2,1)S(1)}, bf16[384,512]{1,0:T(8,128)(2,1)S(1)}, u32[]{:S(2)}, u32[]{:S(2)}) collective-permute-start(bf16[384,512]{1,0:T(8,128)(2,1)S(1)} %get-tuple-element.303), channel_id=1, source_target_pairs={{0,8},{4,12},{8,0},{12,4},{1,9},{5,13},{9,1},{13,5},{2,10},{6,14},... | collective-permute-start | bytes 1179656 | tf_op jit(solution)/shard_map/ppermute | solution.py:801
  508.1 40.1 %collective-permute-start.23 = (bf16[384,512]{1,0:T(8,128)(2,1)S(1)}, bf16[384,512]{1,0:T(8,128)(2,1)S(1)}, u32[]{:S(2)}, u32[]{:S(2)}) collective-permute-start(bf16[384,512]{1,0:T(8,128)(2,1)S(1)} %get-tuple-element.302), channel_id=1, source_target_pairs={{0,12},{4,8},{8,4},{12,0},{1,13},{5,9},{9,5},{13,1},{2,14},{6,10},... | collective-permute-start | bytes 1179656 | tf_op jit(solution)/shard_map/ppermute | solution.py:801
  565.4 37.6 %collective-permute-start.25 = (bf16[384,2048]{1,0:T(8,128)(2,1)}, bf16[384,2048]{1,0:T(8,128)(2,1)}, u32[]{:S(2)}, u32[]{:S(2)}) collective-permute-start(bf16[384,2048]{1,0:T(8,128)(2,1)} %pad_maximum_fusion.6.refs_3_.refs_8_.refs_6_.refs_16_), channel_id=1, source_target_pairs={{0,2},{1,3},{2,0},{3,1},{4,6},{5,7},{6,4},{7,5},{8,10},{9,11},{10,... | collective-permute-start | bytes 4718600 | tf_op jit(solution)/shard_map/ppermute | solution.py:801
  573.8 128.3 %collective-permute-start.30 = (bf16[1024,2048]{1,0:T(8,128)(2,1)}, bf16[1024,2048]{1,0:T(8,128)(2,1)S(1)}, u32[]{:S(2)}, u32[]{:S(2)}) collective-permute-start(bf16[1024,2048]{1,0:T(8,128)(2,1)} %all-gather.9.cloned.1.call-done.refs_0_.refs_2_.refs_3_.refs_7_.refs_1_.refs_6_), channel_id=1, source_target_pairs={{0,16},{16,0},{1,17},{17,1},{2,18},{18,2},{3,19},{19,3},{4,20},{20... | collective-permute-start | bytes 12582920 | tf_op jit(solution)/shard_map/ppermute | solution.py:801
  577.3 48.4 %collective-permute-start.28 = (bf16[384,2048]{1,0:T(8,128)(2,1)S(1)}, bf16[384,2048]{1,0:T(8,128)(2,1)S(1)}, u32[]{:S(2)}, u32[]{:S(2)}) collective-permute-start(bf16[384,2048]{1,0:T(8,128)(2,1)S(1)} %pad_maximum_fusion.8.refs_3_.refs_12_.refs_10_.refs_20_), channel_id=1, source_target_pairs={{0,2},{1,3},{2,0},{3,1},{4,6},{5,7},{6,4},{7,5},{8,10},{9,11},{10,... | collective-permute-start | bytes 4718600 | tf_op jit(solution)/shard_map/ppermute | solution.py:801
  578.5 47.3 %collective-permute-start.24 = (bf16[384,2048]{1,0:T(8,128)(2,1)}, bf16[384,2048]{1,0:T(8,128)(2,1)S(1)}, u32[]{:S(2)}, u32[]{:S(2)}) collective-permute-start(bf16[384,2048]{1,0:T(8,128)(2,1)} %pad_maximum_fusion.6.refs_3_.refs_8_.refs_6_.refs_16_), channel_id=1, source_target_pairs={{0,1},{1,0},{2,3},{3,2},{4,5},{5,4},{6,7},{7,6},{8,9},{9,8},{10,11... | collective-permute-start | bytes 4718600 | tf_op jit(solution)/shard_map/ppermute | solution.py:801
  603.1 60.5 %collective-permute-start.27 = (bf16[384,2048]{1,0:T(8,128)(2,1)S(1)}, bf16[384,2048]{1,0:T(8,128)(2,1)S(1)}, u32[]{:S(2)}, u32[]{:S(2)}) collective-permute-start(bf16[384,2048]{1,0:T(8,128)(2,1)S(1)} %pad_maximum_fusion.8.refs_3_.refs_12_.refs_10_.refs_20_), channel_id=1, source_target_pairs={{0,1},{1,0},{2,3},{3,2},{4,5},{5,4},{6,7},{7,6},{8,9},{9,8},{10,11... | collective-permute-start | bytes 4718600 | tf_op jit(solution)/shard_map/ppermute | solution.py:801
  625.8 37.8 %collective-permute-start.29 = (bf16[384,2048]{1,0:T(8,128)(2,1)S(1)}, bf16[384,2048]{1,0:T(8,128)(2,1)S(1)}, u32[]{:S(2)}, u32[]{:S(2)}) collective-permute-start(bf16[384,2048]{1,0:T(8,128)(2,1)S(1)} %collective-permute-done.28.refs_4_.refs_13_.refs_11_.refs_21_), channel_id=1, source_target_pairs={{0,1},{1,0},{2,3},{3,2},{4,5},{5,4},{6,7},{7,6},{8,9},{9,8},{10,11... | collective-permute-start | bytes 4718600 | tf_op jit(solution)/shard_map/ppermute | solution.py:801
  746.0 43.6 %collective-permute-start.33 = (bf16[2,768,1024]{2,1,0:T(8,128)(2,1)}, bf16[2,768,1024]{2,1,0:T(8,128)(2,1)}, u32[]{:S(2)}, u32[]{:S(2)}) collective-permute-start(bf16[2,768,1024]{2,1,0:T(8,128)(2,1)} %spread.10.refs_0_), channel_id=1, source_target_pairs={{0,1},{1,0},{2,3},{3,2},{4,5},{5,4},{6,7},{7,6},{8,9},{9,8},{10,11... | collective-permute-start | bytes 9437192 | tf_op jit(solution)/shard_map/ppermute | solution.py:801
  853.3 46.1 %collective-permute-start.41 = (bf16[384,2048]{1,0:T(8,128)(2,1)S(1)}, bf16[384,2048]{1,0:T(8,128)(2,1)S(1)}, u32[]{:S(2)}, u32[]{:S(2)}) collective-permute-start(bf16[384,2048]{1,0:T(8,128)(2,1)S(1)} %pad_maximum_fusion.10.refs_10_.refs_3_.refs_8_), channel_id=1, source_target_pairs={{0,2},{1,3},{2,0},{3,1},{4,6},{5,7},{6,4},{7,5},{8,10},{9,11},{10,... | collective-permute-start | bytes 4718600 | tf_op jit(solution)/shard_map/ppermute | solution.py:801
  988.2 93.3 %collective-permute-start.45 = (bf16[1024,2048]{1,0:T(8,128)(2,1)}, bf16[1024,2048]{1,0:T(8,128)(2,1)}, u32[]{:S(2)}, u32[]{:S(2)}) collective-permute-start(bf16[1024,2048]{1,0:T(8,128)(2,1)} %weight_gradient.7.refs_0_), channel_id=1, source_target_pairs={{0,16},{16,0},{1,17},{17,1},{2,18},{18,2},{3,19},{19,3},{4,20},{20... | collective-permute-start | bytes 12582920 | tf_op jit(solution)/shard_map/ppermute | solution.py:801
  1015.1 66.4 %collective-permute-start.44 = (bf16[2,1,384,1024]{3,2,0,1:T(8,128)(2,1)}, bf16[2,1,384,1024]{3,2,0,1:T(8,128)(2,1)}, u32[]{:S(2)}, u32[]{:S(2)}) collective-permute-start(bf16[2,1,384,1024]{3,2,0,1:T(8,128)(2,1)} %get-tuple-element.256), channel_id=1, source_target_pairs={{0,2},{1,3},{2,0},{3,1},{4,6},{5,7},{6,4},{7,5},{8,10},{9,11},{10,... | collective-permute-start | bytes 4718600 | tf_op jit(solution)/shard_map/ppermute | solution.py:801
  1019.3 127.5 %collective-permute-start.39 = (bf16[2,1,384,1024]{3,2,0,1:T(8,128)(2,1)}, bf16[2,1,384,1024]{3,2,0,1:T(8,128)(2,1)}, u32[]{:S(2)}, u32[]{:S(2)}) collective-permute-start(bf16[2,1,384,1024]{3,2,0,1:T(8,128)(2,1)} %get-tuple-element.254), channel_id=1, source_target_pairs={{0,2},{1,3},{2,0},{3,1},{4,6},{5,7},{6,4},{7,5},{8,10},{9,11},{10,... | collective-permute-start | bytes 4718600 | tf_op jit(solution)/shard_map/ppermute | solution.py:801
  1098.3 48.6 %collective-permute-start.46 = (bf16[384,512]{1,0:T(8,128)(2,1)S(1)}, bf16[384,512]{1,0:T(8,128)(2,1)S(1)}, u32[]{:S(2)}, u32[]{:S(2)}) collective-permute-start(bf16[384,512]{1,0:T(8,128)(2,1)S(1)} %get-tuple-element.292), channel_id=1, source_target_pairs={{0,4},{4,0},{8,12},{12,8},{1,5},{5,1},{9,13},{13,9},{2,6},{6,2},{1... | collective-permute-start | bytes 1179656 | tf_op jit(solution)/shard_map/ppermute | solution.py:801
  1146.9 472.5 %reduce-scatter.6.cloned.1.call-start = ((), (), s32[]{:S(2)}) async-start(), calls=%async_computation.7 | async-start | bytes 5242880 | tf_op jit(solution)/shard_map/reduce_scatter | solution.py:1086
  1147.0 91.9 %collective-permute-start.49 = (bf16[1024,2048]{1,0:T(8,128)(2,1)}, bf16[1024,2048]{1,0:T(8,128)(2,1)S(1)}, u32[]{:S(2)}, u32[]{:S(2)}) collective-permute-start(bf16[1024,2048]{1,0:T(8,128)(2,1)} %weight_gradient.8), channel_id=1, source_target_pairs={{0,16},{16,0},{1,17},{17,1},{2,18},{18,2},{3,19},{19,3},{4,20},{20... | collective-permute-start | bytes 12582920 | tf_op jit(solution)/shard_map/ppermute | solution.py:801
  1245.3 374.1 %reduce-scatter.8.cloned.1.call-start = ((), (), s32[]{:S(2)}) async-start(), calls=%async_computation.8 | async-start | bytes 5242880 | tf_op jit(solution)/shard_map/reduce_scatter | solution.py:1086
  1245.4 91.0 %collective-permute-start.50 = (bf16[1024,2048]{1,0:T(8,128)(2,1)}, bf16[1024,2048]{1,0:T(8,128)(2,1)}, u32[]{:S(2)}, u32[]{:S(2)}) collective-permute-start(bf16[1024,2048]{1,0:T(8,128)(2,1)} %weight_gradient.10.refs_0_.refs_2_), channel_id=1, source_target_pairs={{0,16},{16,0},{1,17},{17,1},{2,18},{18,2},{3,19},{19,3},{4,20},{20... | collective-permute-start | bytes 12582920 | tf_op jit(solution)/shard_map/ppermute | solution.py:801
  1247.5 161.5 %collective-permute-start.51 = (bf16[384,512]{1,0:T(8,128)(2,1)}, bf16[384,512]{1,0:T(8,128)(2,1)}, u32[]{:S(2)}, u32[]{:S(2)}) collective-permute-start(bf16[384,512]{1,0:T(8,128)(2,1)} %get-tuple-element.288), channel_id=1, source_target_pairs={{0,4},{4,0},{8,12},{12,8},{1,5},{5,1},{9,13},{13,9},{2,6},{6,2},{1... | collective-permute-start | bytes 1179656 | tf_op jit(solution)/shard_map/ppermute | solution.py:801
  1251.5 157.6 %collective-permute-start.52 = (bf16[384,512]{1,0:T(8,128)(2,1)}, bf16[384,512]{1,0:T(8,128)(2,1)}, u32[]{:S(2)}, u32[]{:S(2)}) collective-permute-start(bf16[384,512]{1,0:T(8,128)(2,1)} %get-tuple-element.287), channel_id=1, source_target_pairs={{0,8},{4,12},{8,0},{12,4},{1,9},{5,13},{9,1},{13,5},{2,10},{6,14},... | collective-permute-start | bytes 1179656 | tf_op jit(solution)/shard_map/ppermute | solution.py:801
  1253.4 155.6 %collective-permute-start.53 = (bf16[384,512]{1,0:T(8,128)(2,1)}, bf16[384,512]{1,0:T(8,128)(2,1)}, u32[]{:S(2)}, u32[]{:S(2)}) collective-permute-start(bf16[384,512]{1,0:T(8,128)(2,1)} %get-tuple-element.286), channel_id=1, source_target_pairs={{0,12},{4,8},{8,4},{12,0},{1,13},{5,9},{9,5},{13,1},{2,14},{6,10},... | collective-permute-start | bytes 1179656 | tf_op jit(solution)/shard_map/ppermute | solution.py:801
  1344.2 473.7 %reduce-scatter.14.cloned.1.call-start = ((), (), s32[]{:S(2)}) async-start(), calls=%async_computation.11 | async-start | bytes 7864320 | tf_op jit(solution)/shard_map/reduce_scatter | solution.py:1136
  1483.1 48.9 %collective-permute-start.57 = (bf16[1,2,4,64,2048]{4,3,2,1,0:T(8,128)(2,1)}, bf16[1,2,4,64,2048]{4,3,2,1,0:T(8,128)(2,1)}, u32[]{:S(2)}, u32[]{:S(2)}) collective-permute-start(bf16[1,2,4,64,2048]{4,3,2,1,0:T(8,128)(2,1)} %constant_dynamic-slice_fusion.3), channel_id=1, source_target_pairs={{0,2},{1,3},{2,0},{3,1},{4,6},{5,7},{6,4},{7,5},{8,10},{9,11},{10,... | collective-permute-start | bytes 6291464 | tf_op jit(solution)/shard_map/ppermute | solution.py:801
  1499.3 37.1 %collective-permute-start.58 = (bf16[64,2048]{1,0:T(8,128)(2,1)S(1)}, bf16[64,2048]{1,0:T(8,128)(2,1)S(1)}, u32[]{:S(2)}, u32[]{:S(2)}) collective-permute-start(bf16[64,2048]{1,0:T(8,128)(2,1)S(1)} %get-tuple-element.322), channel_id=1, source_target_pairs={{0,1},{1,0},{2,3},{3,2},{4,5},{5,4},{6,7},{7,6},{8,9},{9,8},{10,11... | collective-permute-start | bytes 786440 | tf_op jit(solution)/shard_map/ppermute | solution.py:801
  1499.4 38.1 %collective-permute-start.59 = (bf16[64,2048]{1,0:T(8,128)(2,1)S(1)}, bf16[64,2048]{1,0:T(8,128)(2,1)S(1)}, u32[]{:S(2)}, u32[]{:S(2)}) collective-permute-start(bf16[64,2048]{1,0:T(8,128)(2,1)S(1)} %get-tuple-element.321), channel_id=1, source_target_pairs={{0,2},{1,3},{2,0},{3,1},{4,6},{5,7},{6,4},{7,5},{8,10},{9,11},{10,... | collective-permute-start | bytes 786440 | tf_op jit(solution)/shard_map/ppermute | solution.py:801
  1500.5 38.5 %collective-permute-start.60 = (bf16[64,2048]{1,0:T(8,128)(2,1)S(1)}, bf16[64,2048]{1,0:T(8,128)(2,1)S(1)}, u32[]{:S(2)}, u32[]{:S(2)}) collective-permute-start(bf16[64,2048]{1,0:T(8,128)(2,1)S(1)} %get-tuple-element.320), channel_id=1, source_target_pairs={{0,3},{1,2},{2,1},{3,0},{4,7},{5,6},{6,5},{7,4},{8,11},{9,10},{10,... | collective-permute-start | bytes 786440 | tf_op jit(solution)/shard_map/ppermute | solution.py:801
  1539.8 282.3 %reduce-scatter.12.cloned.1.call-start = ((), (), s32[]{:S(2)}) async-start(), calls=%async_computation.10 | async-start | bytes 7864320 | tf_op jit(solution)/shard_map/reduce_scatter | solution.py:1177
  1710.6 65.8 %collective-permute-start.70 = (bf16[2,64,2048]{2,1,0:T(8,128)(2,1)S(1)}, bf16[2,64,2048]{2,1,0:T(8,128)(2,1)S(1)}, u32[]{:S(2)}, u32[]{:S(2)}) collective-permute-start(bf16[2,64,2048]{2,1,0:T(8,128)(2,1)S(1)} %dynamic-slice_bitcast_fusion.3), channel_id=1, source_target_pairs={{0,4},{4,0},{8,12},{12,8},{1,5},{5,1},{9,13},{13,9},{2,6},{6,2},{1... | collective-permute-start | bytes 1572872 | tf_op jit(solution)/shard_map/ppermute | solution.py:801
  1715.4 40.6 %collective-permute-start.65 = (bf16[1,2,4,64,1536]{4,3,2,1,0:T(8,128)(2,1)S(1)}, bf16[1,2,4,64,1536]{4,3,2,1,0:T(8,128)(2,1)S(1)}, u32[]{:S(2)}, u32[]{:S(2)}) collective-permute-start(bf16[1,2,4,64,1536]{4,3,2,1,0:T(8,128)(2,1)S(1)} %constant_dynamic-slice_fusion.1), channel_id=1, source_target_pairs={{0,2},{1,3},{2,0},{3,1},{4,6},{5,7},{6,4},{7,5},{8,10},{9,11},{10,... | collective-permute-start | bytes 4718600 | tf_op jit(solution)/shard_map/ppermute | solution.py:801
  (200 other events, 4904.4 us)
Sparse Core Ops, SparseCore 0:
  9.6 240.3 all-gather.10
  253.8 80.7 all-gather.12
  336.8 79.8 all-gather.6
  418.6 138.6 all-gather.8
  1147.1 79.3 reduce-scatter.9
  1245.5 101.8 reduce-scatter.5
  1349.6 83.3 reduce-scatter.7
  1539.9 111.0 reduce-scatter.13
  1666.1 134.1 reduce-scatter.11

commit v3 on v2

--- a/solution.py
+++ b/solution.py
@@ -1033,9 +1033,11 @@
         last = spread([after(inner[s], last)], [downs], 1)
         sums[s] = sum_group(got, last, "fsdp")
         last = after(last, got)
+    grad_gates, grad_ups, grad_states = [None] * 2, [None] * 2, [None] * 2
     for s in range(2):
         if s == 1:
-            sums[1], grad_downs[0] = hold((sums[1], grad_downs[0]))
+            grad_gates[0], grad_ups[0] = inner_backward(grad_downs[0], gate[0], up[0], downs)
+            sums[1], grad_ups[0] = hold((sums[1], grad_ups[0]))
         down = own_first(joined(sums[s]), "dp")
         down_scale = lax.rsqrt(jnp.mean(down * down, axis=-1, keepdims=True) + epsilon_norm)
         outs[s] = (states[s] + down * down_scale * gains[3]).astype(low_type)
@@ -1046,14 +1048,14 @@
         grad_downs[s] = gather_group(grad_down, "fsdp")
     output_states = jnp.concatenate(outs, axis=0)
 
-    grad_gates, grad_ups, grad_states = [None] * 2, [None] * 2, [None] * 2
     grad_projs, grad_heads, gain_branches = [None] * 2, [None] * 2, [None] * 2
     size = width // dps
 
     def inward(s, last):
-        grad_gates[s], grad_ups[s] = inner_backward(
-            grad_downs[s], after(gate[s], last), up[s], downs
-        )
+        if grad_gates[s] is None:
+            grad_gates[s], grad_ups[s] = inner_backward(
+                grad_downs[s], after(gate[s], last), up[s], downs
+            )
         last = grad_ups[s]
         last = spread([after(grad_gates[s], last), grad_ups[s]], [gates, ups], 0)
         got = swap(last, "fsdp", 1)
@@ -1094,7 +1096,7 @@
     down_away = exchanged(down_away)
     upper_sums, last = inward(1, last)
     gate_away, last = gradient_parts(chunks, grad_gates, away, last)
-    upper_sums, down_away, gate_away = hold((upper_sums, down_away, gate_away))
+    upper_sums, gate_away = hold((upper_sums, gate_away))
     gate_away = exchanged(gate_away)
     last = outward(1, upper_sums)
     down_near, last = gradient_parts(grad_downs, inner, own, last)
@@ -1105,14 +1107,11 @@
     up_away, last = gradient_parts(chunks, grad_ups, away, last)
     up_away = exchanged(up_away)
     gate_near, last = gradient_parts(chunks, grad_gates, own, last)
+    up_near, last = gradient_parts(chunks, grad_ups, own, after(last, *grad_heads[1]))
+    up_near, gate_away = hold((up_near, gate_away))
     gate_kept = kept_feed(gate_near, gate_away)
     gate_gradient = reduce_feed(gate_kept)
-    up_near, last = gradient_parts(
-        chunks, grad_ups, own, after(last, gate_kept, *grad_heads[1])
-    )
-    queries[1] = after(queries[1], last)
-    up_kept = kept_feed(up_near, up_away)
-    up_gradient = reduce_feed(up_kept)
+    queries[1] = after(queries[1], last, gate_kept)
 
     fsdp = lax.axis_index("fsdp")
 
@@ -1130,9 +1129,7 @@
     for s in (1, 0):
         if s == 0:
             down_traded = feed_trade(down_gradient)
-            added, grad_part, out_gradient, down_traded = lax.optimization_barrier(
-                (added, grad_part, out_gradient, down_traded)
-            )
+            added, grad_part, down_traded = hold((added, grad_part, down_traded))
             grad_inputs[1] = lax.psum_scatter(grad_part, "ctx", scatter_dimension=0, tiled=True)
         grads = attend_backward(
             queries[s],
@@ -1145,11 +1142,15 @@
             spots[s],
         )
         if s == 1:
-            grads, up_kept, grad_heads[0] = hold((grads, up_kept, grad_heads[0]))
+            grads, up_away, grad_heads[0] = hold((grads, up_away, grad_heads[0]))
+            up_gradient = reduce_feed(kept_feed(up_near, up_away))
             attended_near[0] = after(attended_near[0], grads[0])
             out_gradient = out_weight(attended_near, grad_projs, near)
             out_gradient = out_gradient.reshape(dps, ctxs, groups, owned, width)
             out_gradient = sum_pairs(out_gradient.transpose(2, 0, 1, 3, 4), "fsdp")
+        else:
+            grads, out_gradient = hold((grads, out_gradient))
+            out_gradient = sum_pairs(out_gradient, "dp")
         added = grads[1:]
         weighted, value_low, dots, gain_sums = restore(
             grads, projected, scales, qk_gains, *turns[s], orders[s], s
@@ -1160,9 +1161,8 @@
             weighted, projected, scales, means, value_low, ctxs, s
         )
         if s == 0:
-            out_gradient = sum_pairs(out_gradient, "dp")
-            gate_gradient, up_gradient, out_gradient, grad_projected[0] = hold(
-                (gate_gradient, up_gradient, out_gradient, grad_projected[0])
+            gate_gradient, up_gradient, grad_projected[0] = hold(
+                (gate_gradient, up_gradient, grad_projected[0])
             )
             gate_traded = feed_trade(gate_gradient)
             up_traded = feed_trade(up_gradient)

time: 1850 us -> 1810 us (0.978)
  waiting for transfers between devices: 698 us -> 653 us
    ppermute x83, waiting for transfers between devices: 549 us -> 504 us  [swap(): return lax.ppermute(value, axis, [(i, i ^ bits) for i in range(size)])]
    unnamed x326 -> x328, local copies, waits for them, and re-layouts: 43.9 us -> 55.2 us
  transfers between devices with their start and end apart: 92 -> 92, of which waited for: 41 -> 38; matrix products, arithmetic and copies ran while one was open for 15% -> 15% of each run, Pallas kernels for 33% -> 33%
where the time goes in v3:
time: 1810 us; the launch traced here: 1800 us
  Pallas kernels  675 us (37%)
  waiting for transfers between devices  653 us (36%)
  other arithmetic  152 us (8%)
  local copies, waits for them, and re-layouts  138 us (8%)
  starting transfers between devices  110 us (6%)
  matrix products  55.5 us (3%)
    pallas_call x30, Pallas kernels, launch(): call(*operands[:scalars], *others, *operands[scalars:])  610 us
    ppermute x83, waiting for transfers between devices, swap(): return lax.ppermute(value, axis, [(i, i ^ bits) for i in range(size)])  504 us
    ppermute x83, starting transfers between devices, swap(): return lax.ppermute(value, axis, [(i, i ^ bits) for i in range(size)])  109 us
    all_gather x1, waiting for transfers between devices, body(): inputs_all = lax.all_gather(inputs, 'ctx', axis=0, tiled=True)  78.6 us
    all_gather x3, waiting for transfers between devices, own_rows(): return lax.all_gather(own, 'ctx', axis=0, tiled=True)  69.5 us
    unnamed x328, local copies, waits for them, and re-layouts  55.2 us
  transfers between devices with their start and end apart: 92, of which 38 were waited for; matrix products, arithmetic and copies ran while one was open for 15% of the time, Pallas kernels for 33%

profile of v3, /device:TPU:0, one launch (start us, length us, event | category | flops | bytes accessed | tf_op | source)
XLA Modules:
  0.0 1799.0 jit_solution(6169246927526905466)
XLA Ops:
  54.9 14.9 collective-permute-done.3
  90.0 24.7 %collective-permute-done.4 = bf16[1,2,4,64,1536]{4,3,2,1,0:T(8,128)(2,1)S(1)} collective-permute-done((bf16[1,2,4,64,1536]{4,3,2,1,0:T(8,128)(2,1)S(1)}, bf16[1,2,4,64,1536]{4,3,2,1,0:T(8,128)(2,1)S(1)}, u32[]{:S(2)}, u32[]{:S(2)}) %collective-permute-start.4) | collective-permute-done | bytes 1572896 | tf_op jit(solution)/shard_map/ppermute | solution.py:801
  118.5 21.1 %collective-permute-done.10 = bf16[2,64,2048]{2,1,0:T(8,128)(2,1)} collective-permute-done((bf16[2,64,2048]{2,1,0:T(8,128)(2,1)}, bf16[2,64,2048]{2,1,0:T(8,128)(2,1)}, u32[]{:S(2)}, u32[]{:S(2)}) %collective-permute-start.10) | collective-permute-done | bytes 524320 | tf_op jit(solution)/shard_map/ppermute | solution.py:801
  148.8 14.8 collective-permute-done.11
  171.4 78.6 %all-gather.11.cloned.1.call-done = bf16[1,1,3072,2048]{3,2,1,0:T(8,128)(2,1)} async-done(((bf16[1,1,768,2048]{3,2,1,0:T(8,128)(2,1)}), bf16[1,1,3072,2048]{3,2,1,0:T(8,128)(2,1)}) %all-gather.11.cloned.1.call-update) | async-done | bytes 12582928 | tf_op jit(solution)/shard_map/all_gather | solution.py:946
  253.7 26.1 %fusion.29.q_ref.k_ref.v_ref.refs_1_.refs_2_ = f32[3072,1536]{1,0:T(8,128)} fusion(bf16[3072,2048]{1,0:T(8,128)(2,1)} %bitcast.429, bf16[2048,1536]{1,0:T(8,128)(2,1)} %bitcast.435), kind=kOutput, calls=%fused_computation.256 | convolution fusion | flops 19327352832 | bytes 37748736 | tf_op jit(solution)/shard_map/dot_general | solution.py:52
  279.8 54.8 %all-gather.13.cloned.1.call-done = bf16[1,1024,2048]{2,1,0:T(8,128)(2,1)} async-done(((bf16[1,256,2048]{2,1,0:T(8,128)(2,1)}), bf16[1,1024,2048]{2,1,0:T(8,128)(2,1)}) %all-gather.13.cloned.1.call-update) | async-done | bytes 4194320 | tf_op jit(solution)/shard_map/all_gather | solution.py:940
  366.9 19.7 %attend_forward.2 = (bf16[1536,512]{1,0:T(8,128)(2,1)S(1)}, f32[4,1,1536]{2,1,0:T(1,128)S(1)}) custom-call(s32[4]{0:T(128)S(1)} %get-tuple-element.245.refs_0_, bf16[1024,2048]{1,0:T(8,128)(2,1)S(1)} %bitcast.402, bf16[1536,512]{1,0:T(8,128)(2,1)S(1)} %get-tuple-element.134.refs_2_.refs_1_, ...), custom_call_target="tpu_custom_call" | custom-call | flops 1024 | bytes 1024 | tf_op jit(solution)/shard_map/attend_forward/pallas_call | solution.py:120
  401.9 14.7 all-gather.7.cloned.1.call-done.refs_1_.refs_7_.refs_5_
  421.3 29.6 %collective-permute-done.15.refs_2_.refs_1_.refs_6_.refs_4_ = bf16[1024,2048]{1,0:T(8,128)(2,1)} collective-permute-done((bf16[1024,2048]{1,0:T(8,128)(2,1)}, bf16[1024,2048]{1,0:T(8,128)(2,1)}, u32[]{:S(2)}, u32[]{:S(2)}) %collective-permute-start.15) | collective-permute-done | bytes 4194336 | tf_op jit(solution)/shard_map/ppermute | solution.py:801
  458.2 46.0 %attend_forward.3 = (bf16[1536,512]{1,0:T(8,128)(2,1)S(1)}, f32[4,1,1536]{2,1,0:T(1,128)S(1)}) custom-call(s32[4]{0:T(128)S(1)} %get-tuple-element.244.refs_0_, bf16[1024,2048]{1,0:T(8,128)(2,1)S(1)} %copy-done.1, bf16[1024,2048]{1,0:T(8,128)(2,1)} %collective-permute-done.15.refs_2_.refs_1_.refs_6_.refs_4_, ...), custom_call_target="tpu_custom_call" | custom-call | flops 1024 | bytes 1024 | tf_op jit(solution)/shard_map/attend_forward/pallas_call | solution.py:120
  508.8 13.5 collective-permute-done.21
  522.3 25.9 %collective-permute-done.22 = bf16[384,512]{1,0:T(8,128)(2,1)S(1)} collective-permute-done((bf16[384,512]{1,0:T(8,128)(2,1)S(1)}, bf16[384,512]{1,0:T(8,128)(2,1)S(1)}, u32[]{:S(2)}, u32[]{:S(2)}) %collective-permute-start.22) | collective-permute-done | bytes 393248 | tf_op jit(solution)/shard_map/ppermute | solution.py:801
  578.4 24.5 %collective-permute-done.25.refs_4_.refs_9_.refs_7_.refs_15_ = bf16[384,2048]{1,0:T(8,128)(2,1)} collective-permute-done((bf16[384,2048]{1,0:T(8,128)(2,1)}, bf16[384,2048]{1,0:T(8,128)(2,1)}, u32[]{:S(2)}, u32[]{:S(2)}) %collective-permute-start.25) | collective-permute-done | bytes 1572896 | tf_op jit(solution)/shard_map/ppermute | solution.py:801
  603.5 22.3 %collective-permute-done.28.refs_4_.refs_13_.refs_11_.refs_19_ = bf16[384,2048]{1,0:T(8,128)(2,1)S(1)} collective-permute-done((bf16[384,2048]{1,0:T(8,128)(2,1)S(1)}, bf16[384,2048]{1,0:T(8,128)(2,1)S(1)}, u32[]{:S(2)}, u32[]{:S(2)}) %collective-permute-start.28) | collective-permute-done | bytes 1572896 | tf_op jit(solution)/shard_map/ppermute | solution.py:801
  625.8 37.7 %gate_up.2 = (bf16[1536,2048]{1,0:T(8,128)(2,1)}, bf16[1536,2048]{1,0:T(8,128)(2,1)}, bf16[1536,2048]{1,0:T(8,128)(2,1)}) custom-call(bf16[1024,2048]{1,0:T(8,128)(2,1)} %all-gather.9.cloned.1.call-done.refs_0_.refs_2_.refs_3_.refs_6_.refs_7_.refs_1_.refs_5_, bf16[384,2048]{1,0:T(8,128)(2,1)S(1)} %collective-permute-done.24.refs_1_.refs_6_.refs_4_.refs_12_, ...), custom_call_target="tpu_custom_call" | custom-call | flops 1024 | bytes 1024 | tf_op jit(solution)/shard_map/gate_up/pallas_call | solution.py:120
  665.2 36.8 %gate_up.3 = (bf16[1536,2048]{1,0:T(8,128)(2,1)}, bf16[1536,2048]{1,0:T(8,128)(2,1)}, bf16[1536,2048]{1,0:T(8,128)(2,1)}) custom-call(bf16[1536,2048]{1,0:T(8,128)(2,1)} %get-tuple-element.154.refs_0_.refs_1_.refs_12_.refs_5_.refs_10_.refs_3_.refs_11_, bf16[384,2048]{1,0:T(8,128)(2,1)S(1)} %collective-permute-done.27.refs_1_.refs_10_.refs_8_.refs_16_, ...), custom_call_target="tpu_custom_call" | custom-call | flops 1024 | bytes 1024 | tf_op jit(solution)/shard_map/gate_up/pallas_call | solution.py:120
  732.7 13.2 spread.10.refs_0_
  746.1 21.3 %collective-permute-done.32 = bf16[2,1,384,1024]{3,2,0,1:T(8,128)(2,1)} collective-permute-done((bf16[2,1,384,1024]{3,2,0,1:T(8,128)(2,1)}, bf16[2,1,384,1024]{3,2,0,1:T(8,128)(2,1)}, u32[]{:S(2)}, u32[]{:S(2)}) %collective-permute-start.32) | collective-permute-done | bytes 1572896 | tf_op jit(solution)/shard_map/ppermute | solution.py:801
  788.9 23.7 %collective-permute-done.36.refs_3_.refs_7_.refs_5_ = bf16[384,2048]{1,0:T(8,128)(2,1)} collective-permute-done((bf16[384,2048]{1,0:T(8,128)(2,1)S(1)}, bf16[384,2048]{1,0:T(8,128)(2,1)}, u32[]{:S(2)}, u32[]{:S(2)}) %collective-permute-start.36) | collective-permute-done | bytes 1572896 | tf_op jit(solution)/shard_map/ppermute | solution.py:801
  820.8 25.1 %inner_backward.2 = (bf16[1536,2048]{1,0:T(8,128)(2,1)}, bf16[1536,2048]{1,0:T(8,128)(2,1)}) custom-call(bf16[384,2048]{1,0:T(8,128)(2,1)S(1)} %collective-permute-done.35.refs_0_.refs_4_.refs_2_, bf16[384,2048]{1,0:T(8,128)(2,1)} %collective-permute-done.37.refs_1_.refs_5_.refs_3_, bf16[384,2048]{1,0:T(8,128)(2,1)} %copy-done.102, ...), custom_call_target="tpu_custom_call" | custom-call | flops 1024 | bytes 1024 | tf_op jit(solution)/shard_map/inner_backward/pallas_call | solution.py:120
  864.1 19.3 %spread.12.refs_0_ = bf16[2,768,1024]{2,1,0:T(8,128)(2,1)} custom-call(bf16[1536,2048]{1,0:T(8,128)(2,1)} %get-tuple-element.165.refs_0_.refs_2_.refs_12_.refs_20_, bf16[1536,2048]{1,0:T(8,128)(2,1)} %get-tuple-element.166.refs_1_.refs_14_.refs_12_, bf16[1536,2048]{1,0:T(8,128)(2,1)} %get-tuple-element.165.refs_0_.refs_2_.refs_12_.refs_20_, ...), custom_call_target="tpu_custom_call" | custom-call | flops 1024 | bytes 1024 | tf_op jit(solution)/shard_map/spread/pallas_call | solution.py:120
  883.9 14.6 collective-permute-done.41.refs_11_.refs_4_.refs_9_
  898.5 19.7 %spread.13.refs_0_.refs_2_ = bf16[2,768,1024]{2,1,0:T(8,128)(2,1)} custom-call(bf16[2,768,1024]{2,1,0:T(8,128)(2,1)} %spread.12.refs_0_, bf16[1536,2048]{1,0:T(8,128)(2,1)} %get-tuple-element.166.refs_1_.refs_14_.refs_12_, bf16[1536,2048]{1,0:T(8,128)(2,1)} %get-tuple-element.165.refs_0_.refs_2_.refs_12_.refs_20_, bf16[1024,2048]{1,0:T(8,128)(2,1)} %bitcast.399, ...), custom_call_target="tpu_custom_call" | custom-call | flops 1024 | bytes 1024 | tf_op jit(solution)/shard_map/spread/pallas_call | solution.py:120
  921.1 20.8 %weight_gradient.7.refs_0_ = bf16[1024,2048]{1,0:T(8,128)(2,1)} custom-call(bf16[2,768,1024]{2,1,0:T(8,128)(2,1)} %spread.13.refs_0_.refs_2_, bf16[2,768,1024]{2,1,0:T(8,128)(2,1)} %copy-done.95, bf16[2,768,1024]{2,1,0:T(8,128)(2,1)} %spread.13.refs_0_.refs_2_, bf16[2,768,1024]{2,1,0:T(8,128)(2,1)} %copy-done.95, ...), custom_call_target="tpu_custom_call" | custom-call | flops 1024 | bytes 1024 | tf_op jit(solution)/shard_map/weight_gradient/pallas_call | solution.py:120
  943.2 24.8 %inner_backward.3 = (bf16[1536,2048]{1,0:T(8,128)(2,1)}, bf16[1536,2048]{1,0:T(8,128)(2,1)}) custom-call(bf16[1024,2048]{1,0:T(8,128)(2,1)} %weight_gradient.7.refs_0_, bf16[384,2048]{1,0:T(8,128)(2,1)S(1)} %copy-done.24, bf16[384,2048]{1,0:T(8,128)(2,1)} %collective-permute-done.42.refs_9_.refs_2_.refs_7_, bf16[384,2048]{1,0:T(8,128)(2,1)} %copy-done.103, ...), custom_call_target="tpu_custom_call" | custom-call | flops 1024 | bytes 1024 | tf_op jit(solution)/shard_map/inner_backward/pallas_call | solution.py:120
  968.0 19.2 %spread.14.refs_0_ = bf16[2,768,1024]{2,1,0:T(8,128)(2,1)} custom-call(bf16[1536,2048]{1,0:T(8,128)(2,1)} %get-tuple-element.169.refs_0_.refs_2_.refs_13_.refs_21_, bf16[1536,2048]{1,0:T(8,128)(2,1)} %get-tuple-element.170.refs_1_.refs_15_.refs_13_, bf16[1536,2048]{1,0:T(8,128)(2,1)} %get-tuple-element.169.refs_0_.refs_2_.refs_13_.refs_21_, ...), custom_call_target="tpu_custom_call" | custom-call | flops 1024 | bytes 1024 | tf_op jit(solution)/shard_map/spread/pallas_call | solution.py:120
  987.8 19.6 %spread.15.refs_0_.refs_3_ = bf16[2,768,1024]{2,1,0:T(8,128)(2,1)} custom-call(bf16[2,768,1024]{2,1,0:T(8,128)(2,1)} %spread.14.refs_0_, bf16[1536,2048]{1,0:T(8,128)(2,1)} %get-tuple-element.170.refs_1_.refs_15_.refs_13_, bf16[1536,2048]{1,0:T(8,128)(2,1)} %get-tuple-element.169.refs_0_.refs_2_.refs_13_.refs_21_, bf16[1024,2048]{1,0:T(8,128)(2,1)} %bitcast.401, ...), custom_call_target="tpu_custom_call" | custom-call | flops 1024 | bytes 1024 | tf_op jit(solution)/shard_map/spread/pallas_call | solution.py:120
  1019.9 20.9 %weight_gradient.8 = bf16[1024,2048]{1,0:T(8,128)(2,1)} custom-call(bf16[2,768,1024]{2,1,0:T(8,128)(2,1)} %spread.15.refs_0_.refs_3_, bf16[2,768,1024]{2,1,0:T(8,128)(2,1)} %copy-done.97, bf16[1024,2048]{1,0:T(8,128)(2,1)} %all-gather.9.cloned.1.call-done.refs_0_.refs_2_.refs_3_.refs_6_.refs_7_.refs_1_.refs_5_, ...), custom_call_target="tpu_custom_call" | custom-call | flops 1024 | bytes 1024 | tf_op jit(solution)/shard_map/weight_gradient/pallas_call | solution.py:120
  1068.4 16.4 collective-permute-start.46
  1088.2 21.3 %weight_gradient.9 = bf16[1024,2048]{1,0:T(8,128)(2,1)} custom-call(bf16[4,384,512]{2,1,0:T(8,128)(2,1)S(1)} %out_back.2.refs_0_.refs_1_, bf16[4,384,512]{2,1,0:T(8,128)(2,1)S(1)} %out_back.2.refs_0_.refs_1_, bf16[384,2048]{1,0:T(8,128)(2,1)} %copy-done.22, bf16[384,2048]{1,0:T(8,128)(2,1)} %collective-permute-done.37.refs_1_.refs_5_.refs_3_, ...), custom_call_target="tpu_custom_call" | custom-call | flops 1024 | bytes 1024 | tf_op jit(solution)/shard_map/weight_gradient/pallas_call | solution.py:120
  1134.5 21.4 %weight_gradient.10.refs_0_.refs_2_ = bf16[1024,2048]{1,0:T(8,128)(2,1)} custom-call(bf16[4,384,512]{2,1,0:T(8,128)(2,1)S(1)} %out_back.3.refs_0_.refs_2_, bf16[1024,2048]{1,0:T(8,128)(2,1)} %all-gather.9.cloned.1.call-done.refs_0_.refs_2_.refs_3_.refs_6_.refs_7_.refs_1_.refs_5_, bf16[4,384,512]{2,1,0:T(8,128)(2,1)S(1)} %out_back.3.refs_0_.refs_2_, ...), custom_call_target="tpu_custom_call" | custom-call | flops 1024 | bytes 1024 | tf_op jit(solution)/shard_map/weight_gradient/pallas_call | solution.py:120
  1155.9 21.1 %weight_gradient.11.refs_0_.refs_6_ = bf16[1024,2048]{1,0:T(8,128)(2,1)} custom-call(bf16[1024,2048]{1,0:T(8,128)(2,1)} %weight_gradient.10.refs_0_.refs_2_, bf16[1024,2048]{1,0:T(8,128)(2,1)} %all-gather.9.cloned.1.call-done.refs_0_.refs_2_.refs_3_.refs_6_.refs_7_.refs_1_.refs_5_, bf16[1024,2048]{1,0:T(8,128)(2,1)} %weight_gradient.10.refs_0_.refs_2_, ...), custom_call_target="tpu_custom_call" | custom-call | flops 1024 | bytes 1024 | tf_op jit(solution)/shard_map/weight_gradient/pallas_call | solution.py:120
  1177.0 21.5 %weight_gradient.12.refs_1_ = bf16[1024,2048]{1,0:T(8,128)(2,1)} custom-call(bf16[1024,2048]{1,0:T(8,128)(2,1)} %weight_gradient.11.refs_0_.refs_6_, bf16[384,512]{1,0:T(8,128)(2,1)S(1)} %get-tuple-element.175.refs_1_.refs_7_, bf16[384,512]{1,0:T(8,128)(2,1)S(1)} %collective-permute-done.46.refs_2_.refs_8_, ...), custom_call_target="tpu_custom_call" | custom-call | flops 1024 | bytes 1024 | tf_op jit(solution)/shard_map/weight_gradient/pallas_call | solution.py:120
  1223.0 62.3 %attend_backward.2 = (f32[1536,512]{1,0:T(8,128)}, f32[3072,512]{1,0:T(8,128)}, f32[3072,512]{1,0:T(8,128)}) custom-call(s32[4]{0:T(128)S(1)} %copy-done.78, bf16[1024,2048]{1,0:T(8,128)(2,1)} %weight_gradient.12.refs_1_, bf16[1024,2048]{1,0:T(8,128)(2,1)} %add_convert_fusion.1.refs_2_, bf16[1536,512]{1,0:T(8,128)(2,1)S(1)} %copy-done.48, ...), custom_call_target="tpu_custom_call" | custom-call | flops 1024 | bytes 1024 | tf_op jit(solution)/shard_map/attend_backward/pallas_call | solution.py:120
  1285.3 17.1 collective-permute-done.50
  1354.5 15.3 convolution_convert_fusion.1
  1378.9 11.8 out_weight.1
  1427.0 29.3 %attend_backward.3 = (f32[1536,512]{1,0:T(8,128)}, f32[1536,512]{1,0:T(8,128)}, f32[1536,512]{1,0:T(8,128)}) custom-call(s32[4]{0:T(128)S(1)} %copy-done.76, bf16[1536,512]{1,0:T(8,128)(2,1)S(1)} %copy-done.46, bf16[1536,512]{1,0:T(8,128)(2,1)S(1)} %pad_maximum_fusion.12.refs_2_, bf16[1536,512]{1,0:T(8,128)(2,1)S(1)} %copy-done.52, ...), custom_call_target="tpu_custom_call" | custom-call | flops 1024 | bytes 1024 | tf_op jit(solution)/shard_map/attend_backward/pallas_call | solution.py:120
  1456.4 15.4 collective-permute-done.60
  1519.4 32.2 %weight_gradient.13 = bf16[2048,1536]{1,0:T(8,128)(2,1)} custom-call(bf16[1536,2048]{1,0:T(8,128)(2,1)} %bitcast.427, bf16[1536,2048]{1,0:T(8,128)(2,1)} %bitcast.426, bf16[1536,1536]{1,0:T(8,128)(2,1)} %copy-done.19, bf16[1536,1536]{1,0:T(8,128)(2,1)} %copy-done.18), custom_call_target="tpu_custom_call" | custom-call | flops 1024 | bytes 1024 | tf_op jit(solution)/shard_map/weight_gradient/pallas_call | solution.py:120
  1551.6 14.1 convolution_convert_fusion
  1569.8 21.8 %collective-permute-done.78 = f32[4,2048]{1,0:T(4,128)S(1)} collective-permute-done((f32[4,2048]{1,0:T(4,128)S(1)}, f32[4,2048]{1,0:T(4,128)S(1)}, u32[]{:S(2)}, u32[]{:S(2)}) %collective-permute-start.78) | collective-permute-done | bytes 32800 | tf_op jit(solution)/shard_map/ppermute | solution.py:801
  1606.7 23.8 %collective-permute-done.80 = f32[4,2048]{1,0:T(4,128)S(1)} collective-permute-done((f32[4,2048]{1,0:T(4,128)S(1)}, f32[4,2048]{1,0:T(4,128)S(1)}, u32[]{:S(2)}, u32[]{:S(2)}) %collective-permute-start.80) | collective-permute-done | bytes 32800 | tf_op jit(solution)/shard_map/ppermute | solution.py:801
  1645.8 31.1 %collective-permute-done.71 = bf16[1,64,2048]{2,1,0:T(8,128)(2,1)S(1)} collective-permute-done((bf16[1,64,2048]{2,1,0:T(8,128)(2,1)S(1)}, bf16[1,64,2048]{2,1,0:T(8,128)(2,1)S(1)}, u32[]{:S(2)}, u32[]{:S(2)}) %collective-permute-start.71) | collective-permute-done | bytes 262176 | tf_op jit(solution)/shard_map/ppermute | solution.py:801
  1691.9 39.8 %collective-permute-done.76 = bf16[64,2048]{1,0:T(8,128)(2,1)S(1)} collective-permute-done((bf16[64,2048]{1,0:T(8,128)(2,1)S(1)}, bf16[64,2048]{1,0:T(8,128)(2,1)S(1)}, u32[]{:S(2)}, u32[]{:S(2)}) %collective-permute-start.76) | collective-permute-done | bytes 262176 | tf_op jit(solution)/shard_map/ppermute | solution.py:801
  1736.8 14.4 collective-permute-done.65
  1756.0 18.6 %update.3 = (f32[64,24576]{1,0:T(8,128)}, f32[64,24576]{1,0:T(8,128)}, f32[64,24576]{1,0:T(8,128)}, f32[64,24576]{1,0:T(8,128)}) custom-call(s32[12]{0:T(128)S(1)} %pad_add_fusion.1.columns_ref, bf16[768,2048]{1,0:T(8,128)(2,1)S(1)} %constant_dynamic-update-slice_fusion.refs_0_, f32[64,24576]{1,0:T(8,128)S(1)} %bitcast.405, f32[64,24576]{1,0:T(8,128)} %refs_2_.3, ...), custom_call_target="tpu_custom_call" | custom-call | flops 1024 | bytes 1024 | tf_op jit(solution)/shard_map/update/pallas_call | solution.py:784
  (686 shorter events, 585.5 us)
Async XLA Ops:
  7.2 242.8 %all-gather.11.cloned.1.call-start = ((), (), s32[]{:S(2)}) async-start(), calls=%async_computation.12 | async-start | bytes 15728640 | tf_op jit(solution)/shard_map/all_gather | solution.py:946
  7.9 326.7 %all-gather.13.cloned.1.call-start = ((), (), s32[]{:S(2)}) async-start(), calls=%async_computation.13 | async-start | bytes 5242880 | tf_op jit(solution)/shard_map/all_gather | solution.py:940
  17.7 65.5 %collective-permute-start.9 = (bf16[1,64,2048]{2,1,0:T(8,128)(2,1)S(1)}, bf16[1,64,2048]{2,1,0:T(8,128)(2,1)}, u32[]{:S(2)}, u32[]{:S(2)}) collective-permute-start(bf16[1,64,2048]{2,1,0:T(8,128)(2,1)S(1)} %slice_bitcast_fusion.28), channel_id=1, source_target_pairs={{0,8},{4,12},{8,0},{12,4},{1,9},{5,13},{9,1},{13,5},{2,10},{6,14},... | collective-permute-start | bytes 786440 | tf_op jit(solution)/shard_map/ppermute | solution.py:801
  38.7 103.9 %collective-permute-start.6 = (bf16[3,64,2048]{2,1,0:T(8,128)(2,1)}, bf16[3,64,2048]{2,1,0:T(8,128)(2,1)}, u32[]{:S(2)}, u32[]{:S(2)}) collective-permute-start(bf16[3,64,2048]{2,1,0:T(8,128)(2,1)} %bitcast.385), channel_id=1, source_target_pairs={{0,1},{1,0},{2,3},{3,2},{4,5},{5,4},{6,7},{7,6},{8,9},{9,8},{10,11... | collective-permute-start | bytes 2359304 | tf_op jit(solution)/shard_map/ppermute | solution.py:801
  43.9 100.7 %collective-permute-start.7 = (bf16[3,64,2048]{2,1,0:T(8,128)(2,1)}, bf16[3,64,2048]{2,1,0:T(8,128)(2,1)}, u32[]{:S(2)}, u32[]{:S(2)}) collective-permute-start(bf16[3,64,2048]{2,1,0:T(8,128)(2,1)} %bitcast.384), channel_id=1, source_target_pairs={{0,2},{1,3},{2,0},{3,1},{4,6},{5,7},{6,4},{7,5},{8,10},{9,11},{10,... | collective-permute-start | bytes 2359304 | tf_op jit(solution)/shard_map/ppermute | solution.py:801
  48.0 98.7 %collective-permute-start.8 = (bf16[3,64,2048]{2,1,0:T(8,128)(2,1)}, bf16[3,64,2048]{2,1,0:T(8,128)(2,1)}, u32[]{:S(2)}, u32[]{:S(2)}) collective-permute-start(bf16[3,64,2048]{2,1,0:T(8,128)(2,1)} %bitcast.383), channel_id=1, source_target_pairs={{0,3},{1,2},{2,1},{3,0},{4,7},{5,6},{6,5},{7,4},{8,11},{9,10},{10,... | collective-permute-start | bytes 2359304 | tf_op jit(solution)/shard_map/ppermute | solution.py:801
  70.0 44.6 %collective-permute-start.4 = (bf16[1,2,4,64,1536]{4,3,2,1,0:T(8,128)(2,1)S(1)}, bf16[1,2,4,64,1536]{4,3,2,1,0:T(8,128)(2,1)S(1)}, u32[]{:S(2)}, u32[]{:S(2)}) collective-permute-start(bf16[1,2,4,64,1536]{4,3,2,1,0:T(8,128)(2,1)S(1)} %pad_maximum_fusion.4), channel_id=1, source_target_pairs={{0,2},{1,3},{2,0},{3,1},{4,6},{5,7},{6,4},{7,5},{8,10},{9,11},{10,... | collective-permute-start | bytes 4718600 | tf_op jit(solution)/shard_map/ppermute | solution.py:801
  85.1 54.5 %collective-permute-start.10 = (bf16[2,64,2048]{2,1,0:T(8,128)(2,1)}, bf16[2,64,2048]{2,1,0:T(8,128)(2,1)}, u32[]{:S(2)}, u32[]{:S(2)}) collective-permute-start(bf16[2,64,2048]{2,1,0:T(8,128)(2,1)} %maximum_bitcast_fusion.4), channel_id=1, source_target_pairs={{0,4},{4,0},{8,12},{12,8},{1,5},{5,1},{9,13},{13,9},{2,6},{6,2},{1... | collective-permute-start | bytes 1572872 | tf_op jit(solution)/shard_map/ppermute | solution.py:801
  116.8 48.4 %collective-permute-start.5 = (bf16[2,2,4,64,1536]{4,3,2,1,0:T(8,128)(2,1)}, bf16[2,2,4,64,1536]{4,3,2,1,0:T(8,128)(2,1)}, u32[]{:S(2)}, u32[]{:S(2)}) collective-permute-start(bf16[2,2,4,64,1536]{4,3,2,1,0:T(8,128)(2,1)} %maximum_bitcast_fusion.1), channel_id=1, source_target_pairs={{0,1},{1,0},{2,3},{3,2},{4,5},{5,4},{6,7},{7,6},{8,9},{9,8},{10,11... | collective-permute-start | bytes 9437192 | tf_op jit(solution)/shard_map/ppermute | solution.py:801
  253.7 163.0 %all-gather.7.cloned.1.call-start = ((), (), s32[]{:S(2)}) async-start(), calls=%async_computation.5 | async-start | bytes 5242880 | tf_op jit(solution)/shard_map/all_gather | solution.py:940
  334.6 239.0 %all-gather.9.cloned.1.call-start = ((), (), s32[]{:S(2)}) async-start(), calls=%async_computation.6 | async-start | bytes 5242880 | tf_op jit(solution)/shard_map/all_gather | solution.py:940
  355.1 42.3 %collective-permute-start.14 = (bf16[1,2,4,64,2048]{4,3,2,1,0:T(8,128)(2,1)}, bf16[1,2,4,64,2048]{4,3,2,1,0:T(8,128)(2,1)}, u32[]{:S(2)}, u32[]{:S(2)}) collective-permute-start(bf16[1,2,4,64,2048]{4,3,2,1,0:T(8,128)(2,1)} %bitcast.434), channel_id=1, source_target_pairs={{0,2},{1,3},{2,0},{3,1},{4,6},{5,7},{6,4},{7,5},{8,10},{9,11},{10,... | collective-permute-start | bytes 6291464 | tf_op jit(solution)/shard_map/ppermute | solution.py:801
  357.0 93.9 %collective-permute-start.15 = (bf16[1024,2048]{1,0:T(8,128)(2,1)}, bf16[1024,2048]{1,0:T(8,128)(2,1)}, u32[]{:S(2)}, u32[]{:S(2)}) collective-permute-start(bf16[1024,2048]{1,0:T(8,128)(2,1)} %bitcast.395), channel_id=1, source_target_pairs={{0,16},{16,0},{1,17},{17,1},{2,18},{18,2},{3,19},{19,3},{4,20},{20... | collective-permute-start | bytes 12582920 | tf_op jit(solution)/shard_map/ppermute | solution.py:801
  416.6 131.5 %collective-permute-start.17 = (bf16[2,2,4,64,2048]{4,3,2,1,0:T(8,128)(2,1)}, bf16[2,2,4,64,2048]{4,3,2,1,0:T(8,128)(2,1)}, u32[]{:S(2)}, u32[]{:S(2)}) collective-permute-start(bf16[2,2,4,64,2048]{4,3,2,1,0:T(8,128)(2,1)} %maximum_bitcast_fusion.own_ref), channel_id=1, source_target_pairs={{0,1},{1,0},{2,3},{3,2},{4,5},{5,4},{6,7},{7,6},{8,9},{9,8},{10,11... | collective-permute-start | bytes 12582920 | tf_op jit(solution)/shard_map/ppermute | solution.py:801
  416.6 136.8 %collective-permute-start.16 = (bf16[1024,2048]{1,0:T(8,128)(2,1)}, bf16[1024,2048]{1,0:T(8,128)(2,1)}, u32[]{:S(2)}, u32[]{:S(2)}) collective-permute-start(bf16[1024,2048]{1,0:T(8,128)(2,1)} %all-gather.7.cloned.1.call-done.refs_1_.refs_7_.refs_5_), channel_id=1, source_target_pairs={{0,16},{16,0},{1,17},{17,1},{2,18},{18,2},{3,19},{19,3},{4,20},{20... | collective-permute-start | bytes 12582920 | tf_op jit(solution)/shard_map/ppermute | solution.py:801
  418.2 933.1 %reduce-scatter.10.cloned.1.call-start = ((), (), s32[]{:S(2)}) async-start(), calls=%async_computation.9 | async-start | bytes 5242880 | tf_op jit(solution)/shard_map/reduce_scatter | solution.py:1088
  419.8 84.5 %collective-permute-start.18 = (bf16[384,512]{1,0:T(8,128)(2,1)S(1)}, bf16[384,512]{1,0:T(8,128)(2,1)S(1)}, u32[]{:S(2)}, u32[]{:S(2)}) collective-permute-start(bf16[384,512]{1,0:T(8,128)(2,1)S(1)} %get-tuple-element.310), channel_id=1, source_target_pairs={{0,4},{4,0},{8,12},{12,8},{1,5},{5,1},{9,13},{13,9},{2,6},{6,2},{1... | collective-permute-start | bytes 1179656 | tf_op jit(solution)/shard_map/ppermute | solution.py:801
  419.9 84.5 %collective-permute-start.19 = (bf16[384,512]{1,0:T(8,128)(2,1)S(1)}, bf16[384,512]{1,0:T(8,128)(2,1)S(1)}, u32[]{:S(2)}, u32[]{:S(2)}) collective-permute-start(bf16[384,512]{1,0:T(8,128)(2,1)S(1)} %get-tuple-element.309), channel_id=1, source_target_pairs={{0,8},{4,12},{8,0},{12,4},{1,9},{5,13},{9,1},{13,5},{2,10},{6,14},... | collective-permute-start | bytes 1179656 | tf_op jit(solution)/shard_map/ppermute | solution.py:801
  450.9 57.2 %collective-permute-start.20 = (bf16[384,512]{1,0:T(8,128)(2,1)S(1)}, bf16[384,512]{1,0:T(8,128)(2,1)S(1)}, u32[]{:S(2)}, u32[]{:S(2)}) collective-permute-start(bf16[384,512]{1,0:T(8,128)(2,1)S(1)} %get-tuple-element.308), channel_id=1, source_target_pairs={{0,12},{4,8},{8,4},{12,0},{1,13},{5,9},{9,5},{13,1},{2,14},{6,10},... | collective-permute-start | bytes 1179656 | tf_op jit(solution)/shard_map/ppermute | solution.py:801
  504.4 43.7 %collective-permute-start.22 = (bf16[384,512]{1,0:T(8,128)(2,1)S(1)}, bf16[384,512]{1,0:T(8,128)(2,1)S(1)}, u32[]{:S(2)}, u32[]{:S(2)}) collective-permute-start(bf16[384,512]{1,0:T(8,128)(2,1)S(1)} %get-tuple-element.305), channel_id=1, source_target_pairs={{0,8},{4,12},{8,0},{12,4},{1,9},{5,13},{9,1},{13,5},{2,10},{6,14},... | collective-permute-start | bytes 1179656 | tf_op jit(solution)/shard_map/ppermute | solution.py:801
  508.1 40.1 %collective-permute-start.23 = (bf16[384,512]{1,0:T(8,128)(2,1)S(1)}, bf16[384,512]{1,0:T(8,128)(2,1)S(1)}, u32[]{:S(2)}, u32[]{:S(2)}) collective-permute-start(bf16[384,512]{1,0:T(8,128)(2,1)S(1)} %get-tuple-element.304), channel_id=1, source_target_pairs={{0,12},{4,8},{8,4},{12,0},{1,13},{5,9},{9,5},{13,1},{2,14},{6,10},... | collective-permute-start | bytes 1179656 | tf_op jit(solution)/shard_map/ppermute | solution.py:801
  565.3 37.7 %collective-permute-start.25 = (bf16[384,2048]{1,0:T(8,128)(2,1)}, bf16[384,2048]{1,0:T(8,128)(2,1)}, u32[]{:S(2)}, u32[]{:S(2)}) collective-permute-start(bf16[384,2048]{1,0:T(8,128)(2,1)} %pad_maximum_fusion.6.refs_3_.refs_8_.refs_6_.refs_14_), channel_id=1, source_target_pairs={{0,2},{1,3},{2,0},{3,1},{4,6},{5,7},{6,4},{7,5},{8,10},{9,11},{10,... | collective-permute-start | bytes 4718600 | tf_op jit(solution)/shard_map/ppermute | solution.py:801
  573.7 128.3 %collective-permute-start.30 = (bf16[1024,2048]{1,0:T(8,128)(2,1)}, bf16[1024,2048]{1,0:T(8,128)(2,1)S(1)}, u32[]{:S(2)}, u32[]{:S(2)}) collective-permute-start(bf16[1024,2048]{1,0:T(8,128)(2,1)} %all-gather.9.cloned.1.call-done.refs_0_.refs_2_.refs_3_.refs_6_.refs_7_.refs_1_.refs_5_), channel_id=1, source_target_pairs={{0,16},{16,0},{1,17},{17,1},{2,18},{18,2},{3,19},{19,3},{4,20},{20... | collective-permute-start | bytes 12582920 | tf_op jit(solution)/shard_map/ppermute | solution.py:801
  577.3 48.4 %collective-permute-start.28 = (bf16[384,2048]{1,0:T(8,128)(2,1)S(1)}, bf16[384,2048]{1,0:T(8,128)(2,1)S(1)}, u32[]{:S(2)}, u32[]{:S(2)}) collective-permute-start(bf16[384,2048]{1,0:T(8,128)(2,1)S(1)} %pad_maximum_fusion.8.refs_3_.refs_12_.refs_10_.refs_18_), channel_id=1, source_target_pairs={{0,2},{1,3},{2,0},{3,1},{4,6},{5,7},{6,4},{7,5},{8,10},{9,11},{10,... | collective-permute-start | bytes 4718600 | tf_op jit(solution)/shard_map/ppermute | solution.py:801
  578.4 47.3 %collective-permute-start.24 = (bf16[384,2048]{1,0:T(8,128)(2,1)}, bf16[384,2048]{1,0:T(8,128)(2,1)S(1)}, u32[]{:S(2)}, u32[]{:S(2)}) collective-permute-start(bf16[384,2048]{1,0:T(8,128)(2,1)} %pad_maximum_fusion.6.refs_3_.refs_8_.refs_6_.refs_14_), channel_id=1, source_target_pairs={{0,1},{1,0},{2,3},{3,2},{4,5},{5,4},{6,7},{7,6},{8,9},{9,8},{10,11... | collective-permute-start | bytes 4718600 | tf_op jit(solution)/shard_map/ppermute | solution.py:801
  603.0 60.6 %collective-permute-start.27 = (bf16[384,2048]{1,0:T(8,128)(2,1)S(1)}, bf16[384,2048]{1,0:T(8,128)(2,1)S(1)}, u32[]{:S(2)}, u32[]{:S(2)}) collective-permute-start(bf16[384,2048]{1,0:T(8,128)(2,1)S(1)} %pad_maximum_fusion.8.refs_3_.refs_12_.refs_10_.refs_18_), channel_id=1, source_target_pairs={{0,1},{1,0},{2,3},{3,2},{4,5},{5,4},{6,7},{7,6},{8,9},{9,8},{10,11... | collective-permute-start | bytes 4718600 | tf_op jit(solution)/shard_map/ppermute | solution.py:801
  625.7 37.8 %collective-permute-start.29 = (bf16[384,2048]{1,0:T(8,128)(2,1)S(1)}, bf16[384,2048]{1,0:T(8,128)(2,1)S(1)}, u32[]{:S(2)}, u32[]{:S(2)}) collective-permute-start(bf16[384,2048]{1,0:T(8,128)(2,1)S(1)} %collective-permute-done.28.refs_4_.refs_13_.refs_11_.refs_19_), channel_id=1, source_target_pairs={{0,1},{1,0},{2,3},{3,2},{4,5},{5,4},{6,7},{7,6},{8,9},{9,8},{10,11... | collective-permute-start | bytes 4718600 | tf_op jit(solution)/shard_map/ppermute | solution.py:801
  730.2 37.1 %collective-permute-start.32 = (bf16[2,1,384,1024]{3,2,0,1:T(8,128)(2,1)}, bf16[2,1,384,1024]{3,2,0,1:T(8,128)(2,1)}, u32[]{:S(2)}, u32[]{:S(2)}) collective-permute-start(bf16[2,1,384,1024]{3,2,0,1:T(8,128)(2,1)} %fusion.4), channel_id=1, source_target_pairs={{0,2},{1,3},{2,0},{3,1},{4,6},{5,7},{6,4},{7,5},{8,10},{9,11},{10,... | collective-permute-start | bytes 4718600 | tf_op jit(solution)/shard_map/ppermute | solution.py:801
  745.8 66.8 %collective-permute-start.33 = (bf16[2,768,1024]{2,1,0:T(8,128)(2,1)}, bf16[2,768,1024]{2,1,0:T(8,128)(2,1)}, u32[]{:S(2)}, u32[]{:S(2)}) collective-permute-start(bf16[2,768,1024]{2,1,0:T(8,128)(2,1)} %spread.10.refs_0_), channel_id=1, source_target_pairs={{0,1},{1,0},{2,3},{3,2},{4,5},{5,4},{6,7},{7,6},{8,9},{9,8},{10,11... | collective-permute-start | bytes 9437192 | tf_op jit(solution)/shard_map/ppermute | solution.py:801
  987.2 122.3 %collective-permute-start.45 = (bf16[1024,2048]{1,0:T(8,128)(2,1)}, bf16[1024,2048]{1,0:T(8,128)(2,1)}, u32[]{:S(2)}, u32[]{:S(2)}) collective-permute-start(bf16[1024,2048]{1,0:T(8,128)(2,1)} %weight_gradient.7.refs_0_), channel_id=1, source_target_pairs={{0,16},{16,0},{1,17},{17,1},{2,18},{18,2},{3,19},{19,3},{4,20},{20... | collective-permute-start | bytes 12582920 | tf_op jit(solution)/shard_map/ppermute | solution.py:801
  1014.1 37.6 %collective-permute-start.44 = (bf16[2,1,384,1024]{3,2,0,1:T(8,128)(2,1)}, bf16[2,1,384,1024]{3,2,0,1:T(8,128)(2,1)}, u32[]{:S(2)}, u32[]{:S(2)}) collective-permute-start(bf16[2,1,384,1024]{3,2,0,1:T(8,128)(2,1)} %get-tuple-element.258), channel_id=1, source_target_pairs={{0,2},{1,3},{2,0},{3,1},{4,6},{5,7},{6,4},{7,5},{8,10},{9,11},{10,... | collective-permute-start | bytes 4718600 | tf_op jit(solution)/shard_map/ppermute | solution.py:801
  1019.6 97.8 %collective-permute-start.39 = (bf16[2,1,384,1024]{3,2,0,1:T(8,128)(2,1)}, bf16[2,1,384,1024]{3,2,0,1:T(8,128)(2,1)}, u32[]{:S(2)}, u32[]{:S(2)}) collective-permute-start(bf16[2,1,384,1024]{3,2,0,1:T(8,128)(2,1)} %get-tuple-element.256), channel_id=1, source_target_pairs={{0,2},{1,3},{2,0},{3,1},{4,6},{5,7},{6,4},{7,5},{8,10},{9,11},{10,... | collective-permute-start | bytes 4718600 | tf_op jit(solution)/shard_map/ppermute | solution.py:801
  1068.4 48.9 %collective-permute-start.46 = (bf16[384,512]{1,0:T(8,128)(2,1)S(1)}, bf16[384,512]{1,0:T(8,128)(2,1)S(1)}, u32[]{:S(2)}, u32[]{:S(2)}) collective-permute-start(bf16[384,512]{1,0:T(8,128)(2,1)S(1)} %get-tuple-element.294), channel_id=1, source_target_pairs={{0,4},{4,0},{8,12},{12,8},{1,5},{5,1},{9,13},{13,9},{2,6},{6,2},{1... | collective-permute-start | bytes 1179656 | tf_op jit(solution)/shard_map/ppermute | solution.py:801
  1117.4 401.9 %reduce-scatter.6.cloned.1.call-start = ((), (), s32[]{:S(2)}) async-start(), calls=%async_computation.7 | async-start | bytes 5242880 | tf_op jit(solution)/shard_map/reduce_scatter | solution.py:1088
  1117.5 90.7 %collective-permute-start.49 = (bf16[1024,2048]{1,0:T(8,128)(2,1)}, bf16[1024,2048]{1,0:T(8,128)(2,1)S(1)}, u32[]{:S(2)}, u32[]{:S(2)}) collective-permute-start(bf16[1024,2048]{1,0:T(8,128)(2,1)} %weight_gradient.8), channel_id=1, source_target_pairs={{0,16},{16,0},{1,17},{17,1},{2,18},{18,2},{3,19},{19,3},{4,20},{20... | collective-permute-start | bytes 12582920 | tf_op jit(solution)/shard_map/ppermute | solution.py:801
  1212.5 306.8 %reduce-scatter.8.cloned.1.call-start = ((), (), s32[]{:S(2)}) async-start(), calls=%async_computation.8 | async-start | bytes 5242880 | tf_op jit(solution)/shard_map/reduce_scatter | solution.py:1088
  1212.6 89.8 %collective-permute-start.50 = (bf16[1024,2048]{1,0:T(8,128)(2,1)}, bf16[1024,2048]{1,0:T(8,128)(2,1)S(1)}, u32[]{:S(2)}, u32[]{:S(2)}) collective-permute-start(bf16[1024,2048]{1,0:T(8,128)(2,1)} %weight_gradient.10.refs_0_.refs_2_), channel_id=1, source_target_pairs={{0,16},{16,0},{1,17},{17,1},{2,18},{18,2},{3,19},{19,3},{4,20},{20... | collective-permute-start | bytes 12582920 | tf_op jit(solution)/shard_map/ppermute | solution.py:801
  1215.3 70.0 %collective-permute-start.51 = (bf16[384,512]{1,0:T(8,128)(2,1)}, bf16[384,512]{1,0:T(8,128)(2,1)S(1)}, u32[]{:S(2)}, u32[]{:S(2)}) collective-permute-start(bf16[384,512]{1,0:T(8,128)(2,1)} %get-tuple-element.290), channel_id=1, source_target_pairs={{0,4},{4,0},{8,12},{12,8},{1,5},{5,1},{9,13},{13,9},{2,6},{6,2},{1... | collective-permute-start | bytes 1179656 | tf_op jit(solution)/shard_map/ppermute | solution.py:801
  1218.2 67.1 %collective-permute-start.52 = (bf16[384,512]{1,0:T(8,128)(2,1)}, bf16[384,512]{1,0:T(8,128)(2,1)S(1)}, u32[]{:S(2)}, u32[]{:S(2)}) collective-permute-start(bf16[384,512]{1,0:T(8,128)(2,1)} %get-tuple-element.289), channel_id=1, source_target_pairs={{0,8},{4,12},{8,0},{12,4},{1,9},{5,13},{9,1},{13,5},{2,10},{6,14},... | collective-permute-start | bytes 1179656 | tf_op jit(solution)/shard_map/ppermute | solution.py:801
  1220.1 65.2 %collective-permute-start.53 = (bf16[384,512]{1,0:T(8,128)(2,1)S(1)}, bf16[384,512]{1,0:T(8,128)(2,1)S(1)}, u32[]{:S(2)}, u32[]{:S(2)}) collective-permute-start(bf16[384,512]{1,0:T(8,128)(2,1)S(1)} %get-tuple-element.288), channel_id=1, source_target_pairs={{0,12},{4,8},{8,4},{12,0},{1,13},{5,9},{9,5},{13,1},{2,14},{6,10},... | collective-permute-start | bytes 1179656 | tf_op jit(solution)/shard_map/ppermute | solution.py:801
  1306.5 477.3 %reduce-scatter.14.cloned.1.call-start = ((), (), s32[]{:S(2)}) async-start(), calls=%async_computation.11 | async-start | bytes 7864320 | tf_op jit(solution)/shard_map/reduce_scatter | solution.py:1133
  1371.4 416.6 %reduce-scatter.12.cloned.1.call-start = ((), (), s32[]{:S(2)}) async-start(), calls=%async_computation.10 | async-start | bytes 7864320 | tf_op jit(solution)/shard_map/reduce_scatter | solution.py:1177
  1423.6 48.2 %collective-permute-start.60 = (bf16[1,2,4,64,2048]{4,3,2,1,0:T(8,128)(2,1)}, bf16[1,2,4,64,2048]{4,3,2,1,0:T(8,128)(2,1)}, u32[]{:S(2)}, u32[]{:S(2)}) collective-permute-start(bf16[1,2,4,64,2048]{4,3,2,1,0:T(8,128)(2,1)} %constant_dynamic-slice_fusion.3), channel_id=1, source_target_pairs={{0,2},{1,3},{2,0},{3,1},{4,6},{5,7},{6,4},{7,5},{8,10},{9,11},{10,... | collective-permute-start | bytes 6291464 | tf_op jit(solution)/shard_map/ppermute | solution.py:801
  1603.0 76.6 %collective-permute-start.63 = (bf16[2,2,4,64,1536]{4,3,2,1,0:T(8,128)(2,1)}, bf16[2,2,4,64,1536]{4,3,2,1,0:T(8,128)(2,1)}, u32[]{:S(2)}, u32[]{:S(2)}) collective-permute-start(bf16[2,2,4,64,1536]{4,3,2,1,0:T(8,128)(2,1)} %dynamic-slice_bitcast_fusion.1), channel_id=1, source_target_pairs={{0,1},{1,0},{2,3},{3,2},{4,5},{5,4},{6,7},{7,6},{8,9},{9,8},{10,11... | collective-permute-start | bytes 9437192 | tf_op jit(solution)/shard_map/ppermute | solution.py:801
  1605.4 39.4 %collective-permute-start.70 = (bf16[2,64,2048]{2,1,0:T(8,128)(2,1)}, bf16[2,64,2048]{2,1,0:T(8,128)(2,1)S(1)}, u32[]{:S(2)}, u32[]{:S(2)}) collective-permute-start(bf16[2,64,2048]{2,1,0:T(8,128)(2,1)} %dynamic-slice_bitcast_fusion.3), channel_id=1, source_target_pairs={{0,4},{4,0},{8,12},{12,8},{1,5},{5,1},{9,13},{13,9},{2,6},{6,2},{1... | collective-permute-start | bytes 1572872 | tf_op jit(solution)/shard_map/ppermute | solution.py:801
  1682.6 49.0 %collective-permute-start.64 = (bf16[1,2,4,64,1536]{4,3,2,1,0:T(8,128)(2,1)S(1)}, bf16[1,2,4,64,1536]{4,3,2,1,0:T(8,128)(2,1)S(1)}, u32[]{:S(2)}, u32[]{:S(2)}) collective-permute-start(bf16[1,2,4,64,1536]{4,3,2,1,0:T(8,128)(2,1)S(1)} %constant_dynamic-slice_fusion.2), channel_id=1, source_target_pairs={{0,2},{1,3},{2,0},{3,1},{4,6},{5,7},{6,4},{7,5},{8,10},{9,11},{10,... | collective-permute-start | bytes 4718600 | tf_op jit(solution)/shard_map/ppermute | solution.py:801
  1684.6 47.0 %collective-permute-start.76 = (bf16[64,2048]{1,0:T(8,128)(2,1)S(1)}, bf16[64,2048]{1,0:T(8,128)(2,1)S(1)}, u32[]{:S(2)}, u32[]{:S(2)}) collective-permute-start(bf16[64,2048]{1,0:T(8,128)(2,1)S(1)} %get-tuple-element.317), channel_id=1, source_target_pairs={{0,2},{1,3},{2,0},{3,1},{4,6},{5,7},{6,4},{7,5},{8,10},{9,11},{10,... | collective-permute-start | bytes 786440 | tf_op jit(solution)/shard_map/ppermute | solution.py:801
  1686.7 50.0 %collective-permute-start.77 = (bf16[64,2048]{1,0:T(8,128)(2,1)S(1)}, bf16[64,2048]{1,0:T(8,128)(2,1)S(1)}, u32[]{:S(2)}, u32[]{:S(2)}) collective-permute-start(bf16[64,2048]{1,0:T(8,128)(2,1)S(1)} %get-tuple-element.316), channel_id=1, source_target_pairs={{0,3},{1,2},{2,1},{3,0},{4,7},{5,6},{6,5},{7,4},{8,11},{9,10},{10,... | collective-permute-start | bytes 786440 | tf_op jit(solution)/shard_map/ppermute | solution.py:801
  (201 other events, 5024.5 us)
Sparse Core Ops, SparseCore 0:
  9.6 240.3 all-gather.10
  253.8 80.7 all-gather.12
  336.8 79.8 all-gather.6
  418.6 138.6 all-gather.8
  1117.5 79.5 reduce-scatter.9
  1212.6 100.2 reduce-scatter.5
  1315.3 83.5 reduce-scatter.7
  1401.2 111.7 reduce-scatter.13
  1565.9 129.4 reduce-scatter.11
